TPU v7x, 32 devices: a whole 2x2x4 slice. The times are simulated.
32 devices in a mesh: ctx: 16 (over z, y, core), fsdp: 2 (over x).
Axes of the slice: x: 2, y: 2, z: 4, core: 2. Of those that a mesh axis runs over, the one named last changes fastest.
Arguments:
- tokens: bfloat16 [4, 2048, 1536], P('fsdp', 'ctx'), may hold values from -6 to 6
- attn_gain: float32 [1536], replicated, may hold values from 0.25 to 1.75
- w_query: bfloat16 [1536, 1536], P('fsdp'), may hold values from -0.21875 to 0.21875
- w_key: bfloat16 [1536, 768], P('fsdp'), may hold values from -0.15625 to 0.15625
- w_value: bfloat16 [1536, 768], P('fsdp'), may hold values from -0.15625 to 0.15625
- w_out: bfloat16 [1536, 1536], P('fsdp'), may hold values from -0.4375 to 0.4375
- mlp_gain: float32 [1536], replicated, may hold values from 0.25 to 1.75
- w_gate: bfloat16 [1536, 4096], P('fsdp'), may hold values from -0.15625 to 0.15625
- w_up: bfloat16 [1536, 4096], P('fsdp'), may hold values from -0.15625 to 0.15625
- w_down: bfloat16 [4096, 1536], P('fsdp'), may hold values from -0.125 to 0.125
- cotangent: bfloat16 [4, 2048, 1536], P('fsdp', 'ctx'), may hold values from -6 to 6
Outputs:
- mixed: bfloat16 [4, 2048, 1536], P('fsdp', 'ctx')
- tokens_grad: bfloat16 [4, 2048, 1536], P('fsdp', 'ctx')
- attn_gain_grad: float32 [1536], replicated
- w_query_grad: float32 [1536, 1536], P('fsdp', 'ctx')
- w_key_grad: float32 [1536, 768], P('fsdp', 'ctx')
- w_value_grad: float32 [1536, 768], P('fsdp', 'ctx')
- w_out_grad: float32 [1536, 1536], P('fsdp', 'ctx')
- mlp_gain_grad: float32 [1536], replicated
- w_gate_grad: float32 [1536, 4096], P('fsdp', 'ctx')
- w_up_grad: float32 [1536, 4096], P('fsdp', 'ctx')
- w_down_grad: float32 [4096, 1536], P('fsdp', 'ctx')
All inputs are finite; a program needn't handle non-finite values.
Results may differ from a plain program's by a relative error of at most 0.024.
Values may be sent and summed in bfloat16 or wider, within the bound.
A program may use at most 384 MiB of HBM per device.

v0:
```python
import jax
import jax.numpy as jnp
from jax import lax
from jax.sharding import PartitionSpec as P

HQ = 16
HK = 8
HD = 96
MICRO = 2


EPSILON = 1e-05
ROPE_BASE = 100000.0
MASK_FILL = -1e30


def matmul(left, right):
    return jnp.dot(left, right, preferred_element_type=jnp.float32)


def times_transposed(left, right):
    return lax.dot_general(
        left, right, (((1,), (1,)), ((), ())), preferred_element_type=jnp.float32
    )


def transposed_times(left, right):
    return lax.dot_general(
        left, right, (((0,), (0,)), ((), ())), preferred_element_type=jnp.float32
    )


def normalize(values):
    inv_rms = lax.rsqrt(jnp.mean(values * values, axis=-1, keepdims=True) + EPSILON)
    return (values * inv_rms, inv_rms)


def norm_back(grad_normed, gain_row, unit_rows, inv_rms):
    scaled = grad_normed * gain_row
    return inv_rms * (scaled - unit_rows * jnp.mean(scaled * unit_rows, axis=-1, keepdims=True))


def rotate(values, cosine, sine_rows):
    half_dim = values.shape[-1] // 2
    front = values[..., :half_dim]
    back_half = values[..., half_dim:]
    return jnp.concatenate(
        [front * cosine - back_half * sine_rows, back_half * cosine + front * sine_rows], axis=-1
    )


def attend_forward(query_rows, key_rows, value_rows, allowed):
    width_ct = query_rows.shape[0]
    grouped = query_rows.reshape(width_ct, HK, HQ // HK, HD)
    key_heads = key_rows.reshape(-1, HK, HD)
    value_heads = value_rows.reshape(-1, HK, HD)
    scores = jnp.einsum("cgrd,lgd->grcl", grouped, key_heads, preferred_element_type=jnp.float32)
    scores = jnp.where(allowed, scores, MASK_FILL)
    row_top = jnp.max(scores, axis=-1, keepdims=True)
    shifted_exp = jnp.exp(scores - row_top)
    row_total = jnp.sum(shifted_exp, axis=-1, keepdims=True)
    prob_low = (shifted_exp / row_total).astype(jnp.bfloat16)
    attended = jnp.einsum(
        "grcl,lgd->cgrd", prob_low, value_heads, preferred_element_type=jnp.float32
    )
    return (attended.reshape(width_ct, HQ * HD), row_top + jnp.log(row_total))


def attend_backward(query_rows, key_rows, value_rows, allowed, log_total, grad_rows):
    width_ct = query_rows.shape[0]
    grouped = query_rows.reshape(width_ct, HK, HQ // HK, HD)
    key_heads = key_rows.reshape(-1, HK, HD)
    value_heads = value_rows.reshape(-1, HK, HD)
    scores = jnp.einsum("cgrd,lgd->grcl", grouped, key_heads, preferred_element_type=jnp.float32)
    prob_full = jnp.exp(jnp.where(allowed, scores, MASK_FILL) - log_total)
    prob_low = prob_full.astype(jnp.bfloat16)
    grad_heads = grad_rows.reshape(width_ct, HK, HQ // HK, HD)
    grad_prob = jnp.einsum(
        "cgrd,lgd->grcl", grad_heads, value_heads, preferred_element_type=jnp.float32
    )
    row_inner = jnp.sum(prob_full * grad_prob, axis=-1, keepdims=True)
    grad_scores = (prob_full * (grad_prob - row_inner)).astype(jnp.bfloat16)
    grad_query = jnp.einsum(
        "grcl,lgd->cgrd", grad_scores, key_heads, preferred_element_type=jnp.float32
    )
    grad_key = jnp.einsum(
        "grcl,cgrd->lgd", grad_scores, grouped, preferred_element_type=jnp.float32
    )
    grad_value = jnp.einsum(
        "grcl,cgrd->lgd", prob_low, grad_heads, preferred_element_type=jnp.float32
    )
    return (
        grad_query.reshape(width_ct, HQ * HD),
        grad_key.reshape(-1, HK * HD),
        grad_value.reshape(-1, HK * HD),
        row_inner,
    )


def reduce_grad(full_grad):
    partial_grad = lax.psum_scatter(
        full_grad.astype(jnp.bfloat16), "fsdp", scatter_dimension=0, tiled=True
    )
    return lax.psum_scatter(partial_grad, "ctx", scatter_dimension=1, tiled=True).astype(
        jnp.float32
    )


def shards(
    tokens, attn_gain, w_query, w_key, w_value, w_out, mlp_gain, w_gate, w_up, w_down, cotangent
):
    seq_local, width_ct, model_width = tokens.shape
    seq_block = seq_local // MICRO
    row_count = seq_block * width_ct
    length = width_ct * lax.axis_size("ctx")
    half_dim = HD // 2
    offset = lax.axis_index("ctx") * width_ct
    query_pos = offset + jnp.arange(width_ct, dtype=jnp.int32)
    key_pos = jnp.arange(length, dtype=jnp.int32)
    allowed = key_pos[None, :] <= query_pos[:, None]
    inv_freq = 1.0 / ROPE_BASE ** (jnp.arange(half_dim, dtype=jnp.float32) * 2.0 / HD)
    angles = query_pos.astype(jnp.float32)[:, None] * inv_freq[None, :]
    cos_one = jnp.cos(angles)[:, None, :]
    sin_one = jnp.sin(angles)[:, None, :]
    cos_rows = jnp.tile(cos_one, (seq_block, 1, 1))
    sin_rows = jnp.tile(sin_one, (seq_block, 1, 1))
    head_scale = HD ** (-0.5)
    mixed_list, token_grad_list = ([], [])
    kept_normed_one, kept_grad_query, kept_grad_key, kept_grad_value = ([], [], [], [])
    kept_attended, kept_grad_branch, kept_normed_two = ([], [], [])
    kept_grad_gate, kept_grad_upper, kept_inner, kept_grad_down = ([], [], [], [])
    attn_gain_acc = jnp.zeros((model_width,), jnp.float32)
    mlp_gain_acc = jnp.zeros((model_width,), jnp.float32)
    for micro_at in range(MICRO):
        first_seq = micro_at * seq_block
        inputs = (
            tokens[first_seq : first_seq + seq_block]
            .reshape(row_count, model_width)
            .astype(jnp.float32)
        )
        outer_grad = (
            cotangent[first_seq : first_seq + seq_block]
            .reshape(row_count, model_width)
            .astype(jnp.float32)
        )
        attn_all = (
            lax.all_gather(w_query, "fsdp", axis=0, tiled=True),
            lax.all_gather(w_key, "fsdp", axis=0, tiled=True),
            lax.all_gather(w_value, "fsdp", axis=0, tiled=True),
            lax.all_gather(w_out, "fsdp", axis=0, tiled=True),
        )
        unit_one, inv_one = normalize(inputs)
        normed_one = (unit_one * attn_gain).astype(jnp.bfloat16)
        query_raw = matmul(normed_one, attn_all[0]).reshape(row_count, HQ, HD)
        key_raw = matmul(normed_one, attn_all[1]).reshape(row_count, HK, HD)
        value_raw = matmul(normed_one, attn_all[2])
        queries = (
            (rotate(query_raw, cos_rows, sin_rows) * head_scale)
            .astype(jnp.bfloat16)
            .reshape(seq_block, width_ct, HQ * HD)
        )
        keys = (
            rotate(key_raw, cos_rows, sin_rows)
            .astype(jnp.bfloat16)
            .reshape(seq_block, width_ct, HK * HD)
        )
        values = value_raw.astype(jnp.bfloat16).reshape(seq_block, width_ct, HK * HD)
        key_all, value_all = (
            lax.all_gather(keys, "ctx", axis=1, tiled=True),
            lax.all_gather(values, "ctx", axis=1, tiled=True),
        )
        attended_parts, lse_parts = ([], [])
        seq_at = 0
        attended_one, lse_one = attend_forward(
            queries[seq_at], key_all[seq_at], value_all[seq_at], allowed
        )
        attended_parts.append(attended_one)
        lse_parts.append(lse_one)
        attended = attended_parts[0].astype(jnp.bfloat16)
        resid = inputs + matmul(attended, attn_all[3])
        unit_two, inv_two = normalize(resid)
        normed_two = (unit_two * mlp_gain).astype(jnp.bfloat16)
        gate_proj = matmul(normed_two, lax.all_gather(w_gate, "fsdp", axis=0, tiled=True))
        up_proj = matmul(normed_two, lax.all_gather(w_up, "fsdp", axis=0, tiled=True))
        sigma = jax.nn.sigmoid(gate_proj)
        active = gate_proj * sigma
        hidden_act = (active * up_proj).astype(jnp.bfloat16)
        down_out = matmul(hidden_act, lax.all_gather(w_down, "fsdp", axis=0, tiled=True))
        mixed_list.append((resid + down_out).astype(jnp.bfloat16))
        grad_down = outer_grad.astype(jnp.bfloat16)
        grad_hidden = times_transposed(
            grad_down, lax.all_gather(w_down, "fsdp", axis=0, tiled=True)
        )
        grad_gate = (grad_hidden * up_proj * sigma * (1.0 + gate_proj * (1.0 - sigma))).astype(
            jnp.bfloat16
        )
        grad_upper = (grad_hidden * active).astype(jnp.bfloat16)
        pair_pieces = lax.all_gather((w_gate, w_up), "fsdp", axis=0, tiled=True)
        grad_normed_two = times_transposed(grad_gate, pair_pieces[0]) + times_transposed(
            grad_upper, pair_pieces[1]
        )
        mlp_gain_acc = mlp_gain_acc + jnp.sum(grad_normed_two * unit_two, axis=0)
        grad_resid = outer_grad + norm_back(grad_normed_two, mlp_gain, unit_two, inv_two)
        grad_branch = grad_resid.astype(jnp.bfloat16)
        attn_back = (
            lax.all_gather(w_query, "fsdp", axis=0, tiled=True),
            lax.all_gather(w_key, "fsdp", axis=0, tiled=True),
            lax.all_gather(w_value, "fsdp", axis=0, tiled=True),
            lax.all_gather(w_out, "fsdp", axis=0, tiled=True),
        )
        grad_attended = times_transposed(grad_branch, attn_back[3]).astype(jnp.bfloat16)
        key_back, value_back = (
            lax.all_gather(keys, "ctx", axis=1, tiled=True),
            lax.all_gather(values, "ctx", axis=1, tiled=True),
        )
        query_parts, key_parts, value_parts = ([], [], [])
        seq_at = 0
        query_one = queries[seq_at]
        key_one = key_back[seq_at]
        value_one = value_back[seq_at]
        lse_one = lse_parts[seq_at]
        grad_query, grad_key, grad_value, row_inner = attend_backward(
            query_one, key_one, value_one, allowed, lse_one, grad_attended
        )
        own_key = lax.psum_scatter(
            grad_key.astype(jnp.bfloat16), "ctx", scatter_dimension=0, tiled=True
        ).astype(jnp.float32)
        own_value = lax.psum_scatter(
            grad_value.astype(jnp.bfloat16), "ctx", scatter_dimension=0, tiled=True
        ).astype(jnp.float32)
        query_parts.append(
            rotate((grad_query * head_scale).reshape(width_ct, HQ, HD), cos_one, -sin_one).reshape(
                width_ct, HQ * HD
            )
        )
        key_parts.append(
            rotate(own_key.reshape(width_ct, HK, HD), cos_one, -sin_one).reshape(width_ct, HK * HD)
        )
        value_parts.append(own_value)
        grad_query_raw = query_parts[0].astype(jnp.bfloat16)
        grad_key_raw = key_parts[0].astype(jnp.bfloat16)
        grad_value_raw = value_parts[0].astype(jnp.bfloat16)
        grad_normed_one = (
            times_transposed(grad_query_raw, attn_back[0])
            + times_transposed(grad_key_raw, attn_back[1])
            + times_transposed(grad_value_raw, attn_back[2])
        )
        attn_gain_acc = attn_gain_acc + jnp.sum(grad_normed_one * unit_one, axis=0)
        token_grad_list.append(
            (grad_resid + norm_back(grad_normed_one, attn_gain, unit_one, inv_one)).astype(
                jnp.bfloat16
            )
        )
        kept_normed_one.append(normed_one)
        kept_grad_query.append(grad_query_raw)
        kept_grad_key.append(grad_key_raw)
        kept_grad_value.append(grad_value_raw)
        kept_attended.append(attended)
        kept_grad_branch.append(grad_branch)
        kept_normed_two.append(normed_two)
        kept_grad_gate.append(grad_gate)
        kept_grad_upper.append(grad_upper)
        kept_inner.append(hidden_act)
        kept_grad_down.append(grad_down)
    normed_one_all = jnp.concatenate(kept_normed_one, axis=0)
    normed_two_all = jnp.concatenate(kept_normed_two, axis=0)
    w_query_grad = reduce_grad(
        transposed_times(normed_one_all, jnp.concatenate(kept_grad_query, axis=0))
    )
    w_key_grad = reduce_grad(
        transposed_times(normed_one_all, jnp.concatenate(kept_grad_key, axis=0))
    )
    w_value_grad = reduce_grad(
        transposed_times(normed_one_all, jnp.concatenate(kept_grad_value, axis=0))
    )
    w_out_grad = reduce_grad(
        transposed_times(
            jnp.concatenate(kept_attended, axis=0), jnp.concatenate(kept_grad_branch, axis=0)
        )
    )
    w_gate_grad = reduce_grad(
        transposed_times(normed_two_all, jnp.concatenate(kept_grad_gate, axis=0))
    )
    w_up_grad = reduce_grad(
        transposed_times(normed_two_all, jnp.concatenate(kept_grad_upper, axis=0))
    )
    w_down_grad = reduce_grad(
        transposed_times(
            jnp.concatenate(kept_inner, axis=0), jnp.concatenate(kept_grad_down, axis=0)
        )
    )
    attn_gain_grad, mlp_gain_grad = lax.psum((attn_gain_acc, mlp_gain_acc), ("ctx", "fsdp"))
    mixed = jnp.concatenate(mixed_list, axis=0).reshape(seq_local, width_ct, model_width)
    tokens_grad = jnp.concatenate(token_grad_list, axis=0).reshape(seq_local, width_ct, model_width)
    return (
        mixed,
        tokens_grad,
        attn_gain_grad,
        w_query_grad,
        w_key_grad,
        w_value_grad,
        w_out_grad,
        mlp_gain_grad,
        w_gate_grad,
        w_up_grad,
        w_down_grad,
    )


def solution(mesh):
    placed = (
        P("fsdp", "ctx", None),
        P(),
        P("fsdp", None),
        P("fsdp", None),
        P("fsdp", None),
        P("fsdp", None),
        P(),
        P("fsdp", None),
        P("fsdp", None),
        P("fsdp", None),
        P("fsdp", "ctx", None),
    )
    return jax.shard_map(
        shards,
        mesh=mesh,
        in_specs=placed,
        out_specs=(
            P("fsdp", "ctx", None),
            P("fsdp", "ctx", None),
            P(),
            P("fsdp", "ctx"),
            P("fsdp", "ctx"),
            P("fsdp", "ctx"),
            P("fsdp", "ctx"),
            P(),
            P("fsdp", "ctx"),
            P("fsdp", "ctx"),
            P("fsdp", "ctx"),
        ),
        check_vma=False,
    )
```

profile of v0, /device:TPU:12, one launch (start us, length us, event | category | flops | bytes accessed | tf_op | source)
XLA Modules:
  0.0 2457.3 jit_solution(7192068586239904424)
XLA Ops:
  10.0 36.8 %all-gather.14.cloned.1.call-done = bf16[1536,768]{1,0:T(8,128)(2,1)} async-done(((bf16[768,768]{1,0:T(8,128)(2,1)}), bf16[1536,768]{1,0:T(8,128)(2,1)}) %all-gather.14.cloned.1.call-update) | async-done | bytes 2359312 | tf_op jit(solution)/shard_map/all_gather | solution.py:149
  53.4 31.0 %all-gather.16.cloned.1.call-done = bf16[1536,768]{1,0:T(8,128)(2,1)} async-done(((bf16[768,768]{1,0:T(8,128)(2,1)}), bf16[1536,768]{1,0:T(8,128)(2,1)}) %all-gather.16.cloned.1.call-update) | async-done | bytes 2359312 | tf_op jit(solution)/shard_map/all_gather | solution.py:148
  93.6 55.1 %all-gather.20.cloned.1.call-done = bf16[1536,1536]{1,0:T(8,128)(2,1)} async-done(((bf16[768,1536]{1,0:T(8,128)(2,1)}), bf16[1536,1536]{1,0:T(8,128)(2,1)}) %all-gather.20.cloned.1.call-update) | async-done | bytes 4718608 | tf_op jit(solution)/shard_map/all_gather | solution.py:147
  148.7 6.6 copy.66
  161.9 34.3 %all-gather.34.cloned.1.call-done = bf16[2048,768]{1,0:T(8,128)(2,1)} async-done(((bf16[128,768]{1,0:T(8,128)(2,1)}), bf16[2048,768]{1,0:T(8,128)(2,1)}) %all-gather.34.cloned.1.call-update) | async-done | bytes 3145744 | tf_op jit(solution)/shard_map/all_gather | solution.py:170
  196.1 4.7 copy.68
  200.8 42.0 %all-gather.32.cloned.1.call-done = bf16[2048,768]{1,0:T(8,128)(2,1)} async-done(((bf16[128,768]{1,0:T(8,128)(2,1)}), bf16[2048,768]{1,0:T(8,128)(2,1)}) %all-gather.32.cloned.1.call-update) | async-done | bytes 3145744 | tf_op jit(solution)/shard_map/all_gather | solution.py:170
  242.8 4.9 copy.64
  247.7 42.1 %all-gather.18.cloned.1.call-done = bf16[1,2048,768]{1,2,0:T(8,128)(2,1)} async-done(((bf16[1,128,768]{1,2,0:T(8,128)(2,1)}), bf16[1,2048,768]{1,2,0:T(8,128)(2,1)}) %all-gather.18.cloned.1.call-update) | async-done | bytes 3145744 | tf_op jit(solution)/shard_map/all_gather | solution.py:169
  289.8 11.2 fusion.8
  301.0 9.6 fusion.6
  310.6 10.3 fusion.42
  320.9 33.5 %all-gather.22.cloned.1.call-done = bf16[1536,1536]{1,0:T(8,128)(2,1)} async-done(((bf16[768,1536]{1,0:T(8,128)(2,1)}), bf16[1536,1536]{1,0:T(8,128)(2,1)}) %all-gather.22.cloned.1.call-update) | async-done | bytes 4718608 | tf_op jit(solution)/shard_map/all_gather | solution.py:150
  357.8 44.3 %all-gather.30.cloned.1.call-done = bf16[1,2048,768]{1,2,0:T(8,128)(2,1)} async-done(((bf16[1,128,768]{1,2,0:T(8,128)(2,1)}), bf16[1,2048,768]{1,2,0:T(8,128)(2,1)}) %all-gather.30.cloned.1.call-update) | async-done | bytes 3145744 | tf_op jit(solution)/shard_map/all_gather | solution.py:169
  402.2 12.9 fusion.106
  415.1 141.6 %all-gather.24.cloned.1.call-done = bf16[1536,4096]{1,0:T(8,128)(2,1)} async-done(((bf16[768,4096]{1,0:T(8,128)(2,1)}), bf16[1536,4096]{1,0:T(8,128)(2,1)}) %all-gather.24.cloned.1.call-update) | async-done | bytes 12582928 | tf_op jit(solution)/shard_map/all_gather | solution.py:183
  556.7 7.7 fusion.136
  564.4 146.3 %all-gather.28.cloned.1.call-done = bf16[4096,1536]{1,0:T(8,128)(2,1)} async-done(((bf16[2048,1536]{1,0:T(8,128)(2,1)}), bf16[4096,1536]{1,0:T(8,128)(2,1)}) %all-gather.28.cloned.1.call-update) | async-done | bytes 12582928 | tf_op jit(solution)/shard_map/all_gather | solution.py:188
  710.7 10.1 fusion.132
  720.7 144.0 %all-gather.26.cloned.1.call-done = bf16[1536,4096]{1,0:T(8,128)(2,1)} async-done(((bf16[768,4096]{1,0:T(8,128)(2,1)}), bf16[1536,4096]{1,0:T(8,128)(2,1)}) %all-gather.26.cloned.1.call-update) | async-done | bytes 12582928 | tf_op jit(solution)/shard_map/all_gather | solution.py:184
  864.8 10.2 multiply_convert_fusion.5
  875.0 10.2 fusion.139
  885.2 7.4 multiply_reduce_fusion.1
  899.1 20.8 fusion.3
  919.9 8.8 fusion.7
  928.7 10.4 fusion.41
  950.3 11.0 multiply_convert_fusion
  961.3 9.6 fusion.141
  971.0 9.1 multiply_reduce_fusion
  984.9 24.6 %fusion.5 = (bf16[8,2,128,2048]{2,3,1,0:T(8,128)(2,1)S(1)}, f32[8,2,128]{2,1,0:T(2,128)S(1)}, f32[8,2048,128,2]{2,1,3,0:T(8,128)}) fusion(f32[8,2048,128,2]{2,1,3,0:T(8,128)} %get-tuple-element.104, f32[8,2048,128,2]{2,1,3,0:T(8,128)} %get-tuple-element.100, f32[8,2,128]{2,1,0:T(2,128)S(1)} %get-tuple-element.56, f32[8,2,128]{2,1,0:T(2,128)S(1)} %bitcast.392, ...), kind=kOutput, calls=%fused_computation.9 | convolution fusion | flops 843053056 | bytes 79331328 | tf_op jit(solution)/shard_map/cgrd,lgd->grcl/dot_general | solution.py:78
  1013.8 4.7 copy.99
  1018.7 12.8 fusion.2
  1031.5 4.4 bitcast_convert_fusion.1
  1035.9 4.7 copy.103
  1040.7 10.9 bitcast_convert_fusion
  1051.6 4.7 copy.105
  1056.4 11.1 bitcast_convert_fusion.2
  1067.5 5.0 copy.101
  1072.7 11.9 reduce-scatter.55.cloned.1.call-done
  1085.7 67.9 %reduce-scatter.59.cloned.1.call-done = bf16[128,768]{1,0:T(8,128)(2,1)} async-done(((bf16[2048,768]{1,0:T(8,128)(2,1)}), bf16[128,768]{1,0:T(8,128)(2,1)}) %reduce-scatter.59.cloned.1.call-update) | async-done | bytes 196624
  1157.4 65.1 %reduce-scatter.61.cloned.1.call-done = bf16[128,768]{1,0:T(8,128)(2,1)} async-done(((bf16[2048,768]{1,0:T(8,128)(2,1)}), bf16[128,768]{1,0:T(8,128)(2,1)}) %reduce-scatter.61.cloned.1.call-update) | async-done | bytes 196624
  1223.6 67.8 %reduce-scatter.57.cloned.1.call-done = bf16[128,768]{1,0:T(8,128)(2,1)} async-done(((bf16[2048,768]{1,0:T(8,128)(2,1)}), bf16[128,768]{1,0:T(8,128)(2,1)}) %reduce-scatter.57.cloned.1.call-update) | async-done | bytes 196624
  1296.4 6.7 convolution_multiply_fusion.1
  1303.2 4.8 convolution_multiply_fusion
  1313.9 4.7 convolution_convert_fusion.3
  1318.7 8.2 convolution_convert_fusion
  1328.3 7.6 convolution_convert_fusion.2
  1337.4 7.6 convolution_convert_fusion.1
  1347.6 17.0 reduce-scatter.41.cloned.1.call-done
  1367.1 59.7 %reduce-scatter.37.cloned.1.call-done = bf16[768,1536]{1,0:T(8,128)(2,1)} async-done(((bf16[1536,1536]{1,0:T(8,128)(2,1)}), bf16[768,1536]{1,0:T(8,128)(2,1)}) %reduce-scatter.37.cloned.1.call-update) | async-done | bytes 2359312 | tf_op jit(solution)/shard_map/reduce_scatter | solution.py:101
  1431.2 58.1 %reduce-scatter.43.cloned.1.call-done = bf16[768,1536]{1,0:T(8,128)(2,1)} async-done(((bf16[1536,1536]{1,0:T(8,128)(2,1)}), bf16[768,1536]{1,0:T(8,128)(2,1)}) %reduce-scatter.43.cloned.1.call-update) | async-done | bytes 2359312 | tf_op jit(solution)/shard_map/reduce_scatter | solution.py:101
  1493.6 142.3 %reduce-scatter.53.cloned.1.call-done = bf16[2048,1536]{1,0:T(8,128)(2,1)} async-done(((bf16[4096,1536]{1,0:T(8,128)(2,1)}), bf16[2048,1536]{1,0:T(8,128)(2,1)}) %reduce-scatter.53.cloned.1.call-update) | async-done | bytes 6291472 | tf_op jit(solution)/shard_map/reduce_scatter | solution.py:101
  1635.9 8.7 copy.115
  1644.6 138.1 %reduce-scatter.45.cloned.1.call-done = bf16[768,4096]{1,0:T(8,128)(2,1)} async-done(((bf16[1536,4096]{1,0:T(8,128)(2,1)}), bf16[768,4096]{1,0:T(8,128)(2,1)}) %reduce-scatter.45.cloned.1.call-update) | async-done | bytes 6291472 | tf_op jit(solution)/shard_map/reduce_scatter | solution.py:101
  1783.0 146.5 %reduce-scatter.49.cloned.1.call-done = bf16[768,4096]{1,0:T(8,128)(2,1)} async-done(((bf16[1536,4096]{1,0:T(8,128)(2,1)}), bf16[768,4096]{1,0:T(8,128)(2,1)}) %reduce-scatter.49.cloned.1.call-update) | async-done | bytes 6291472 | tf_op jit(solution)/shard_map/reduce_scatter | solution.py:101
  1929.6 6.5 fusion.29
  1936.2 6.5 fusion.28
  1952.1 41.0 %all-reduce = (f32[1536]{0:T(1024)}, f32[1536]{0:T(1024)}) all-reduce(f32[1536]{0:T(1024)S(1)} %add.219, f32[1536]{0:T(1024)S(1)} %add.220), channel_id=1, replica_groups=mesh['ctx'=16,'fsdp'=2] {'ctx','fsdp'}, use_global_device_ids=true, to_apply=%region_20.21 | all-reduce | flops 3072 | bytes 24576 | tf_op jit(solution)/shard_map/psum | solution.py:292
  1999.5 52.2 %reduce-scatter.67.cloned.1.call-done = bf16[48,768]{1,0:T(8,128)(2,1)} async-done(((bf16[768,768]{1,0:T(8,128)(2,1)}), bf16[48,768]{1,0:T(8,128)(2,1)}) %reduce-scatter.67.cloned.1.call-update) | async-done | bytes 73744
  2053.6 63.9 %reduce-scatter.63.cloned.1.call-done = bf16[96,768]{1,0:T(8,128)(2,1)} async-done(((bf16[1536,768]{1,0:T(8,128)(2,1)}), bf16[96,768]{1,0:T(8,128)(2,1)}) %reduce-scatter.63.cloned.1.call-update) | async-done | bytes 147472
  2119.4 64.2 %reduce-scatter.69.cloned.1.call-done = bf16[96,768]{1,0:T(8,128)(2,1)} async-done(((bf16[1536,768]{1,0:T(8,128)(2,1)}), bf16[96,768]{1,0:T(8,128)(2,1)}) %reduce-scatter.69.cloned.1.call-update) | async-done | bytes 147472
  2185.5 85.8 %reduce-scatter.71.cloned.1.call-done = bf16[96,2048]{1,0:T(8,128)(2,1)} async-done(((bf16[1536,2048]{1,0:T(8,128)(2,1)}), bf16[96,2048]{1,0:T(8,128)(2,1)}) %reduce-scatter.71.cloned.1.call-update) | async-done | bytes 393232
  2273.7 86.6 %reduce-scatter.47.cloned.1.call-done = bf16[768,256]{1,0:T(8,128)(2,1)} async-done(((bf16[768,4096]{1,0:T(8,128)(2,1)}), bf16[768,256]{1,0:T(8,128)(2,1)}) %reduce-scatter.47.cloned.1.call-update) | async-done | bytes 393232 | tf_op jit(solution)/shard_map/reduce_scatter | solution.py:104
  2362.3 86.4 %reduce-scatter.51.cloned.1.call-done = bf16[768,256]{1,0:T(8,128)(2,1)} async-done(((bf16[768,4096]{1,0:T(8,128)(2,1)}), bf16[768,256]{1,0:T(8,128)(2,1)}) %reduce-scatter.51.cloned.1.call-update) | async-done | bytes 393232 | tf_op jit(solution)/shard_map/reduce_scatter | solution.py:104
  (329 shorter events, 116.1 us)
Async XLA Ops:
  7.2 39.6 %all-gather.14.cloned.1.call-start = ((), (), s32[]{:S(2)}) async-start(), calls=%async_computation.18 | async-start | bytes 3538944 | tf_op jit(solution)/shard_map/all_gather | solution.py:149
  7.9 76.5 %all-gather.16.cloned.1.call-start = ((), (), s32[]{:S(2)}) async-start(), calls=%async_computation.19 | async-start | bytes 3538944 | tf_op jit(solution)/shard_map/all_gather | solution.py:148
  8.7 140.0 %all-gather.20.cloned.1.call-start = ((), (), s32[]{:S(2)}) async-start(), calls=%async_computation.21 | async-start | bytes 7077888 | tf_op jit(solution)/shard_map/all_gather | solution.py:147
  9.4 186.7 %all-gather.34.cloned.1.call-start = ((), (), s32[]{:S(2)}) async-start(), calls=%async_computation.37 | async-start | bytes 3342336 | tf_op jit(solution)/shard_map/all_gather | solution.py:170
  9.7 145.6 %copy-start.65 = (f32[128]{0:T(128)}, f32[128]{0:T(128)S(1)}, u32[]{:S(2)}) copy-start(f32[128]{0:T(128)S(1)} %get-tuple-element.111) | copy-start | bytes 1540
  9.7 149.5 %copy-start.67 = (f32[128]{0:T(128)}, f32[128]{0:T(128)S(1)}, u32[]{:S(2)}) copy-start(f32[128]{0:T(128)S(1)} %get-tuple-element.110) | copy-start | bytes 1540
  10.0 74.4 %copy-start.13 = (bf16[128,1536]{1,0:T(8,128)(2,1)}, bf16[128,1536]{1,0:T(8,128)(2,1)S(1)}, u32[]{:S(2)}) copy-start(bf16[128,1536]{1,0:T(8,128)(2,1)S(1)} %get-tuple-element.74) | copy-start | bytes 1179652
  10.0 74.4 %copy-start.15 = (bf16[128,1536]{1,0:T(8,128)(2,1)}, bf16[128,1536]{1,0:T(8,128)(2,1)S(1)}, u32[]{:S(2)}) copy-start(bf16[128,1536]{1,0:T(8,128)(2,1)S(1)} %get-tuple-element.75) | copy-start | bytes 1179652
  49.6 193.2 %all-gather.32.cloned.1.call-start = ((), (), s32[]{:S(2)}) async-start(), calls=%async_computation.36 | async-start | bytes 3342336 | tf_op jit(solution)/shard_map/all_gather | solution.py:170
  52.5 237.3 %all-gather.18.cloned.1.call-start = ((), (), s32[]{:S(2)}) async-start(), calls=%async_computation.20 | async-start | bytes 3342336 | tf_op jit(solution)/shard_map/all_gather | solution.py:169
  53.4 107.4 %copy-start.57 = (f32[128,48]{0,1:T(8,128)}, f32[128,48]{0,1:T(8,128)S(1)}, u32[]{:S(2)}) copy-start(f32[128,48]{0,1:T(8,128)S(1)} %get-tuple-element.98) | copy-start | bytes 73732
  89.8 264.6 %all-gather.22.cloned.1.call-start = ((), (), s32[]{:S(2)}) async-start(), calls=%async_computation.22 | async-start | bytes 7077888 | tf_op jit(solution)/shard_map/all_gather | solution.py:150
  90.6 311.6 %all-gather.30.cloned.1.call-start = ((), (), s32[]{:S(2)}) async-start(), calls=%async_computation.26 | async-start | bytes 3342336 | tf_op jit(solution)/shard_map/all_gather | solution.py:169
  91.3 465.3 %all-gather.24.cloned.1.call-start = ((), (), s32[]{:S(2)}) async-start(), calls=%async_computation.23 | async-start | bytes 18874368 | tf_op jit(solution)/shard_map/all_gather | solution.py:183
  92.1 618.6 %all-gather.28.cloned.1.call-start = ((), (), s32[]{:S(2)}) async-start(), calls=%async_computation.25 | async-start | bytes 18874368 | tf_op jit(solution)/shard_map/all_gather | solution.py:188
  92.6 772.1 %all-gather.26.cloned.1.call-start = ((), (), s32[]{:S(2)}) async-start(), calls=%async_computation.24 | async-start | bytes 18874368 | tf_op jit(solution)/shard_map/all_gather | solution.py:184
  93.4 991.2 %reduce-scatter.55.cloned.1.call-start = ((), (), s32[]{:S(2)}) async-start(), calls=%async_computation.38 | async-start | bytes 3342336
  161.9 240.3 %copy-start.31 = (f32[128,16,48]{0,2,1:T(8,128)}, f32[128,16,48]{0,2,1:T(8,128)S(1)}, u32[]{:S(2)}) copy-start(f32[128,16,48]{0,2,1:T(8,128)S(1)} %get-tuple-element.92) | copy-start | bytes 1179652
  200.8 89.0 %copy-start.34 = (f32[128,16,48]{0,2,1:T(8,128)S(1)}, f32[128,16,48]{0,2,1:T(8,128)}, u32[]{:S(2)}) copy-start(f32[128,16,48]{0,2,1:T(8,128)} %get-tuple-element.70) | copy-start | bytes 1179652
  200.8 89.0 %copy-start.36 = (f32[128,16,48]{0,2,1:T(8,128)S(1)}, f32[128,16,48]{0,2,1:T(8,128)}, u32[]{:S(2)}) copy-start(f32[128,16,48]{0,2,1:T(8,128)} %get-tuple-element.71) | copy-start | bytes 1179652
  320.9 36.8 %copy-start.53 = (bf16[8,96,2,128]{3,1,2,0:T(8,128)(2,1)}, bf16[8,96,2,128]{3,1,2,0:T(8,128)(2,1)S(1)}, u32[]{:S(2)}) copy-start(bf16[8,96,2,128]{3,1,2,0:T(8,128)(2,1)S(1)} %fusion.42) | copy-start | bytes 1179652
  320.9 36.8 %copy-start.61 = (f32[1536]{0:T(1024)S(1)}, f32[1536]{0:T(1024)}, u32[]{:S(2)}) copy-start(f32[1536]{0:T(1024)} %param.17) | copy-start | bytes 18436
  357.6 535.0 %copy-start.7 = (f32[128,1536]{1,0:T(8,128)}, f32[128,1536]{1,0:T(8,128)S(1)}, u32[]{:S(2)}) copy-start(f32[128,1536]{1,0:T(8,128)S(1)} %get-tuple-element.102) | copy-start | bytes 2359300
  357.6 535.0 %copy-start.69 = (f32[128]{0:T(128)}, f32[128]{0:T(128)S(1)}, u32[]{:S(2)}) copy-start(f32[128]{0:T(128)S(1)} %add_rsqrt_fusion.2) | copy-start | bytes 1540
  357.8 506.9 %copy-start.20 = (bf16[128,1536]{1,0:T(8,128)(2,1)}, bf16[128,1536]{1,0:T(8,128)(2,1)S(1)}, u32[]{:S(2)}) copy-start(bf16[128,1536]{1,0:T(8,128)(2,1)S(1)} %multiply_convert_fusion.7) | copy-start | bytes 1179652
  415.1 295.6 %copy-start.17 = (bf16[2,128,1536]{2,1,0:T(8,128)(2,1)S(1)}, bf16[2,128,1536]{2,1,0:T(8,128)(2,1)}, u32[]{:S(2)}) copy-start(bf16[2,128,1536]{2,1,0:T(8,128)(2,1)} %param.21) | copy-start | bytes 2359300
  892.6 27.3 %copy-start.73 = (f32[128]{0:T(128)}, f32[128]{0:T(128)S(1)}, u32[]{:S(2)}) copy-start(f32[128]{0:T(128)S(1)} %broadcast_multiply_fusion.3) | copy-start | bytes 1540
  899.1 20.8 copy-start.38
  919.9 22.9 slice-start
  942.6 37.5 %copy-start.71 = (f32[128]{0:T(128)}, f32[128]{0:T(128)S(1)}, u32[]{:S(2)}) copy-start(f32[128]{0:T(128)S(1)} %add_rsqrt_fusion) | copy-start | bytes 1540
  980.1 29.4 %copy-start.75 = (f32[128]{0:T(128)}, f32[128]{0:T(128)S(1)}, u32[]{:S(2)}) copy-start(f32[128]{0:T(128)S(1)} %broadcast_multiply_fusion.1) | copy-start | bytes 1540
  984.9 24.6 %copy-start.35 = (f32[128,16,48]{0,2,1:T(8,128)S(1)}, f32[128,16,48]{0,2,1:T(8,128)}, u32[]{:S(2)}) copy-start(f32[128,16,48]{0,2,1:T(8,128)} %get-tuple-element.70) | copy-start | bytes 1179652
  984.9 24.6 %copy-start.37 = (f32[128,16,48]{0,2,1:T(8,128)S(1)}, f32[128,16,48]{0,2,1:T(8,128)}, u32[]{:S(2)}) copy-start(f32[128,16,48]{0,2,1:T(8,128)} %get-tuple-element.71) | copy-start | bytes 1179652
  1018.6 135.0 %reduce-scatter.59.cloned.1.call-start = ((), (), s32[]{:S(2)}) async-start(), calls=%async_computation.40 | async-start | bytes 3342336
  1040.7 181.8 %reduce-scatter.61.cloned.1.call-start = ((), (), s32[]{:S(2)}) async-start(), calls=%async_computation.41 | async-start | bytes 3342336
  1056.4 235.1 %reduce-scatter.57.cloned.1.call-start = ((), (), s32[]{:S(2)}) async-start(), calls=%async_computation.39 | async-start | bytes 3342336
  1067.5 87.2 %copy-start.58 = (f32[128,48]{0,1:T(8,128)S(1)}, f32[128,48]{0,1:T(8,128)}, u32[]{:S(2)}) copy-start(f32[128,48]{0,1:T(8,128)} %copy-done.57) | copy-start | bytes 73732
  1067.5 87.2 %copy-start.63 = (f32[128,48]{0,1:T(8,128)S(1)}, f32[128,48]{0,1:T(8,128)}, u32[]{:S(2)}) copy-start(f32[128,48]{0,1:T(8,128)} %get-tuple-element.96) | copy-start | bytes 73732
  1072.6 82.4 %copy-start.14 = (bf16[128,1536]{1,0:T(8,128)(2,1)S(1)}, bf16[128,1536]{1,0:T(8,128)(2,1)}, u32[]{:S(2)}) copy-start(bf16[128,1536]{1,0:T(8,128)(2,1)} %copy-done.13) | copy-start | bytes 1179652
  1072.6 82.4 %copy-start.16 = (bf16[128,1536]{1,0:T(8,128)(2,1)S(1)}, bf16[128,1536]{1,0:T(8,128)(2,1)}, u32[]{:S(2)}) copy-start(bf16[128,1536]{1,0:T(8,128)(2,1)} %copy-done.15) | copy-start | bytes 1179652
  1072.6 272.5 %reduce-scatter.39.cloned.1.call-start = ((), (), s32[]{:S(2)}) async-start(), calls=%async_computation.28 | async-start | bytes 3538944 | tf_op jit(solution)/shard_map/reduce_scatter | solution.py:101
  1154.9 141.4 %copy-start.51 = (bf16[128,8,96]{0,2,1:T(8,128)(2,1)}, bf16[128,8,96]{0,2,1:T(8,128)(2,1)S(1)}, u32[]{:S(2)}) copy-start(bf16[128,8,96]{0,2,1:T(8,128)(2,1)S(1)} %pad_maximum_fusion.14) | copy-start | bytes 589828
  1154.9 141.4 %copy-start.49 = (bf16[128,8,96]{0,2,1:T(8,128)(2,1)}, bf16[128,8,96]{0,2,1:T(8,128)(2,1)S(1)}, u32[]{:S(2)}) copy-start(bf16[128,8,96]{0,2,1:T(8,128)(2,1)S(1)} %pad_maximum_fusion.13) | copy-start | bytes 589828
  1157.3 207.3 %reduce-scatter.41.cloned.1.call-start = ((), (), s32[]{:S(2)}) async-start(), calls=%async_computation.29 | async-start | bytes 3538944 | tf_op jit(solution)/shard_map/reduce_scatter | solution.py:101
  1296.4 130.5 %reduce-scatter.37.cloned.1.call-start = ((), (), s32[]{:S(2)}) async-start(), calls=%async_computation.27 | async-start | bytes 7077888 | tf_op jit(solution)/shard_map/reduce_scatter | solution.py:101
  1312.8 176.4 %reduce-scatter.43.cloned.1.call-start = ((), (), s32[]{:S(2)}) async-start(), calls=%async_computation.30 | async-start | bytes 7077888 | tf_op jit(solution)/shard_map/reduce_scatter | solution.py:101
  1318.6 317.3 %reduce-scatter.53.cloned.1.call-start = ((), (), s32[]{:S(2)}) async-start(), calls=%async_computation.35 | async-start | bytes 18874368 | tf_op jit(solution)/shard_map/reduce_scatter | solution.py:101
  1326.9 455.9 %reduce-scatter.45.cloned.1.call-start = ((), (), s32[]{:S(2)}) async-start(), calls=%async_computation.31 | async-start | bytes 18874368 | tf_op jit(solution)/shard_map/reduce_scatter | solution.py:101
  1335.9 593.6 %reduce-scatter.49.cloned.1.call-start = ((), (), s32[]{:S(2)}) async-start(), calls=%async_computation.33 | async-start | bytes 18874368 | tf_op jit(solution)/shard_map/reduce_scatter | solution.py:101
  1345.1 652.6 %reduce-scatter.65.cloned.1.call-start = ((), (), s32[]{:S(2)}) async-start(), calls=%async_computation.43 | async-start | bytes 1253376
  1347.6 704.2 %reduce-scatter.67.cloned.1.call-start = ((), (), s32[]{:S(2)}) async-start(), calls=%async_computation.44 | async-start | bytes 1253376
  1367.1 750.4 %reduce-scatter.63.cloned.1.call-start = ((), (), s32[]{:S(2)}) async-start(), calls=%async_computation.42 | async-start | bytes 2506752
  1431.1 752.5 %reduce-scatter.69.cloned.1.call-start = ((), (), s32[]{:S(2)}) async-start(), calls=%async_computation.45 | async-start | bytes 2506752
  1493.6 777.8 %reduce-scatter.71.cloned.1.call-start = ((), (), s32[]{:S(2)}) async-start(), calls=%async_computation.46 | async-start | bytes 6684672
  1644.6 715.7 %reduce-scatter.47.cloned.1.call-start = ((), (), s32[]{:S(2)}) async-start(), calls=%async_computation.32 | async-start | bytes 6684672 | tf_op jit(solution)/shard_map/reduce_scatter | solution.py:104
  1782.8 146.8 %copy-start.64 = (f32[1536]{0:T(1024)S(1)}, f32[1536]{0:T(1024)}, u32[]{:S(2)}) copy-start(f32[1536]{0:T(1024)} %get-tuple-element.46) | copy-start | bytes 18436
  1782.8 146.8 %copy-start.25 = (bf16[128,4096]{1,0:T(8,128)(2,1)S(1)}, bf16[128,4096]{1,0:T(8,128)(2,1)}, u32[]{:S(2)}) copy-start(bf16[128,4096]{1,0:T(8,128)(2,1)} %get-tuple-element.62) | copy-start | bytes 3145732
  1782.8 665.9 %reduce-scatter.51.cloned.1.call-start = ((), (), s32[]{:S(2)}) async-start(), calls=%async_computation.34 | async-start | bytes 6684672 | tf_op jit(solution)/shard_map/reduce_scatter | solution.py:104
  1949.1 44.0 %copy-start.19 = (bf16[2,128,1536]{2,1,0:T(8,128)(2,1)S(1)}, bf16[2,128,1536]{2,1,0:T(8,128)(2,1)}, u32[]{:S(2)}) copy-start(bf16[2,128,1536]{2,1,0:T(8,128)(2,1)} %param.21) | copy-start | bytes 2359300
  1949.1 44.0 %copy-start.62 = (f32[1536]{0:T(1024)S(1)}, f32[1536]{0:T(1024)}, u32[]{:S(2)}) copy-start(f32[1536]{0:T(1024)} %param.17) | copy-start | bytes 18436
  1949.1 44.0 %copy-start.72 = (f32[128]{0:T(128)S(1)}, f32[128]{0:T(128)}, u32[]{:S(2)}) copy-start(f32[128]{0:T(128)} %copy-done.71) | copy-start | bytes 1540
  1949.1 44.0 %copy-start.76 = (f32[128]{0:T(128)S(1)}, f32[128]{0:T(128)}, u32[]{:S(2)}) copy-start(f32[128]{0:T(128)} %copy-done.75) | copy-start | bytes 1540
  1950.1 44.8 %copy-start.70 = (f32[128]{0:T(128)S(1)}, f32[128]{0:T(128)}, u32[]{:S(2)}) copy-start(f32[128]{0:T(128)} %copy-done.69) | copy-start | bytes 1540
  1950.1 44.8 %copy-start.74 = (f32[128]{0:T(128)S(1)}, f32[128]{0:T(128)}, u32[]{:S(2)}) copy-start(f32[128]{0:T(128)} %copy-done.73) | copy-start | bytes 1540
  (55 other events, 333.4 us)
Sparse Core Ops, SparseCore 0:
  9.6 37.1 all-gather.13
  48.3 36.0 all-gather.15
  86.0 62.6 all-gather.19
  151.4 44.6 all-gather.33
  198.8 43.9 all-gather.31
  245.4 44.3 all-gather.17
  291.3 63.0 all-gather.21
  357.1 45.0 all-gather.29
  403.7 152.8 all-gather.23
  558.1 152.5 all-gather.27
  712.2 152.4 all-gather.25
  1018.7 65.7 reduce-scatter.54
  1088.4 65.2 reduce-scatter.58
  1157.3 65.2 reduce-scatter.60
  1226.2 65.2 reduce-scatter.56
  1293.5 34.1 reduce-scatter.38
  1329.9 34.7 reduce-scatter.40
  1366.8 59.9 reduce-scatter.36
  1429.2 59.9 reduce-scatter.42
  1491.4 144.4 reduce-scatter.52
  1638.2 144.4 reduce-scatter.44
  1785.0 144.4 reduce-scatter.48
  1933.2 58.0 reduce-scatter.64
  1994.7 56.9 reduce-scatter.66
  2055.5 61.9 reduce-scatter.62
  2121.6 61.9 reduce-scatter.68
  2187.4 83.9 reduce-scatter.70
  2275.8 84.4 reduce-scatter.46
  2364.3 84.3 reduce-scatter.50
where the time goes:
time: 2470 us; the launch traced here: 2460 us
  waiting for transfers between devices  1970 us (80%)
  matrix products  298 us (12%)
  local copies, waits for them, and re-layouts  84.3 us (3%)
  other arithmetic  47.1 us (2%)
  blocking collectives  41 us (2%)
    reduce_scatter x7, waiting for transfers between devices, reduce_grad(): lax.psum_scatter(full_grad.astype(jnp.bfloat16), 'fsdp', scatter_dimensio...  562 us
    unnamed x38, waiting for transfers between devices  484 us
    reduce_scatter x2, waiting for transfers between devices, reduce_grad(): lax.psum_scatter(partial_grad, 'ctx', scatter_dimension=1, tiled=True)  173 us
    all_gather x1, waiting for transfers between devices, shards(): lax.all_gather(w_down, 'fsdp', axis=0, tiled=True)  146 us
    all_gather x1, waiting for transfers between devices, shards(): lax.all_gather(w_up, 'fsdp', axis=0, tiled=True)  144 us
    all_gather x1, waiting for transfers between devices, shards(): lax.all_gather(w_gate, 'fsdp', axis=0, tiled=True)  142 us
    all_gather x2, waiting for transfers between devices, shards(): lax.all_gather(keys, 'ctx', axis=1, tiled=True)  86.4 us
    all_gather x2, waiting for transfers between devices, shards(): lax.all_gather(values, 'ctx', axis=1, tiled=True)  76.3 us
  transfers between devices with their start and end apart: 29, of which 27 were waited for; matrix products, arithmetic and copies ran while one was open for 11% of the time, Pallas kernels for 0%

commit v1 on v0

--- a/solution.py
+++ b/solution.py
@@ -1,12 +1,20 @@
+import functools
+
 import jax
 import jax.numpy as jnp
+import numpy as np
 from jax import lax
+from jax.experimental import pallas as pl
+from jax.experimental.pallas import tpu as pltpu
 from jax.sharding import PartitionSpec as P
 
 HQ = 16
 HK = 8
 HD = 96
 MICRO = 2
+LANES = 128
+HEAD_COLS = 4 * HD
+BF = jnp.bfloat16
 
 
 EPSILON = 1e-05
@@ -307,7 +315,447 @@
     )
 
 
+def nt(a,b):
+    return lax.dot_general(a,b,(((1,),(1,)),((),())),preferred_element_type=jnp.float32)
+def nn(a,b):
+    return jnp.dot(a,b,preferred_element_type=jnp.float32)
+
+def turn(v,cosine,sine):
+    return v*cosine+pltpu.roll(v,LANES//2,1)*sine
+
+def forward_kernel(rows,step_rows,raw_ref,cos_ref,sin_ref,qkv_ref,out_ref,lse_ref,key_ref,val_t_ref):
+    at=pl.program_id(0)
+    here=pl.ds(pl.multiple_of(at*rows,rows),rows)
+    cosine,sine=cos_ref[...],sin_ref[...]
+    raw=raw_ref[...]
+    @pl.when(at==0)
+    def _():
+        val_t_ref[...]=jnp.zeros_like(val_t_ref)
+    scale=HD**-0.5
+    parts=[(turn(raw[:,j*LANES:(j+1)*LANES],cosine,sine)*(scale if j<2 else 1.0)).astype(BF) for j in range(3)]
+    value=raw[:,3*LANES:].astype(BF)
+    for j in range(3):
+        qkv_ref[:,j*LANES:(j+1)*LANES]=parts[j]
+    qkv_ref[:,3*LANES:]=value
+    key_ref[here,:]=parts[2]
+    val_t_ref[:,here]=value.T
+    query=jnp.concatenate(parts[:2],axis=0)
+    length=key_ref.shape[0]
+    per=step_rows//rows
+    for band in range(length//step_rows):
+        @pl.when(at//per==band)
+        def _():
+            extent=(band+1)*step_rows
+            scores=nt(key_ref[0:extent,:],query)
+            tail=scores[band*step_rows:,:]
+            key_pos=lax.broadcasted_iota(jnp.int32,tail.shape,0)
+            query_pos=(at%per)*rows+lax.broadcasted_iota(jnp.int32,tail.shape,1)%rows
+            tail=jnp.where(key_pos<=query_pos,tail,MASK_FILL)
+            pieces=[scores[b*step_rows:(b+1)*step_rows,:] for b in range(band)]+[tail]
+            top=functools.reduce(jnp.maximum,[jnp.max(p,axis=0,keepdims=True) for p in pieces])
+            total=0.0; acc=0.0
+            for b,p in enumerate(pieces):
+                e=jnp.exp(p-top)
+                total=total+jnp.sum(e,axis=0,keepdims=True)
+                acc=acc+nn(val_t_ref[:,b*step_rows:(b+1)*step_rows],e.astype(BF))
+            acc=acc/total
+            out_ref[:,0:LANES]=acc[:,0:rows].T.astype(BF)
+            out_ref[:,LANES:]=acc[:,rows:].T.astype(BF)
+            lse_ref[0]=top+jnp.log(total)
+
+def head_forward(raw,cosine,sine,rows=512,step_rows=512):
+    length=raw.shape[0]
+    steps=length//rows
+    return pl.pallas_call(
+        functools.partial(forward_kernel,rows,step_rows),
+        grid=(steps,),
+        in_specs=[pl.BlockSpec((rows,4*LANES),lambda i:(i,0)),
+                  pl.BlockSpec((rows,LANES),lambda i:(i,0)),
+                  pl.BlockSpec((rows,LANES),lambda i:(i,0))],
+        out_specs=[pl.BlockSpec((rows,4*LANES),lambda i:(i,0)),
+                   pl.BlockSpec((rows,2*LANES),lambda i:(i,0)),
+                   pl.BlockSpec((1,1,2*rows),lambda i:(i,0,0))],
+        out_shape=[jax.ShapeDtypeStruct((length,4*LANES),BF),
+                   jax.ShapeDtypeStruct((length,2*LANES),BF),
+                   jax.ShapeDtypeStruct((steps,1,2*rows),jnp.float32)],
+        scratch_shapes=[pltpu.VMEM((length,LANES),BF),pltpu.VMEM((LANES,length),BF)],
+        compiler_params=pltpu.CompilerParams(vmem_limit_bytes=48*1024*1024),
+    )(raw,cosine,sine)
+
+def backward_kernel(rows,step_rows,qkv_ref,out_ref,grad_ref,lse_ref,cos_ref,sin_ref,pick_ref,res_ref,
+                    key_t_ref,grad_key_ref,grad_val_ref,rows_ref):
+    at=pl.program_id(0)
+    here=pl.ds(pl.multiple_of(at*rows,rows),rows)
+    length=qkv_ref.shape[0]
+    scale=HD**-0.5
+    @pl.when(at==0)
+    def _():
+        grad_key_ref[...]=jnp.zeros_like(grad_key_ref)
+        grad_val_ref[...]=jnp.zeros_like(grad_val_ref)
+        for b in range(length//rows):
+            key_t_ref[:,b*rows:(b+1)*rows]=qkv_ref[b*rows:(b+1)*rows,2*LANES:3*LANES].T
+    query=jnp.concatenate([qkv_ref[here,0:LANES],qkv_ref[here,LANES:2*LANES]],axis=0)
+    grad=jnp.concatenate([grad_ref[:,0:LANES],grad_ref[:,LANES:]],axis=0)
+    out=jnp.concatenate([out_ref[:,0:LANES],out_ref[:,LANES:]],axis=0)
+    inner=jnp.sum((grad.astype(jnp.float32)*out.astype(jnp.float32)).T,axis=0,keepdims=True)
+    lse=lse_ref[0]
+    per=step_rows//rows
+    for band in range(length//step_rows):
+        @pl.when(at//per==band)
+        def _():
+            grad_query=0.0
+            for b in range(band+1):
+                span=slice(b*step_rows,(b+1)*step_rows)
+                scores=nt(qkv_ref[span,2*LANES:3*LANES],query)
+                prob=jnp.exp(scores-lse)
+                if b==band:
+                    key_pos=lax.broadcasted_iota(jnp.int32,scores.shape,0)
+                    query_pos=(at%per)*rows+lax.broadcasted_iota(jnp.int32,scores.shape,1)%rows
+                    prob=jnp.where(key_pos<=query_pos,prob,0.0)
+                grad_prob=nt(qkv_ref[span,3*LANES:],grad)
+                grad_scores=(prob*(grad_prob-inner)).astype(BF)
+                grad_val_ref[span,:]+=nn(prob.astype(BF),grad)
+                grad_key_ref[span,:]+=nn(grad_scores,query)
+                grad_query=grad_query+nn(key_t_ref[:,span],grad_scores)
+            for j in range(2):
+                back=grad_query[:,j*rows:(j+1)*rows].T*scale
+                rows_ref[here,j*LANES:(j+1)*LANES]=turn(back,cos_ref[here,:],-sin_ref[here,:]).astype(BF)
+    @pl.when(at==length//rows-1)
+    def _():
+        for b in range(length//step_rows):
+            span=slice(b*step_rows,(b+1)*step_rows)
+            rows_ref[span,2*LANES:3*LANES]=turn(grad_key_ref[span,:],cos_ref[span,:],-sin_ref[span,:]).astype(BF)
+            rows_ref[span,3*LANES:]=grad_val_ref[span,:].astype(BF)
+            res_ref[span,:]=nn(rows_ref[span,:],pick_ref[...]).astype(BF)
+
+def head_backward(qkv,out,grad,lse,cosine,sine,pick,rows=256,step_rows=256):
+    length=qkv.shape[0]
+    steps=length//rows
+    lse=lse.reshape(-1,2,lse.shape[2]//2).transpose(1,0,2).reshape(2,steps,rows).transpose(1,0,2).reshape(steps,1,2*rows)
+    whole=lambda a:pl.BlockSpec(a.shape,lambda i:(0,)*a.ndim)
+    return pl.pallas_call(
+        functools.partial(backward_kernel,rows,step_rows),
+        grid=(steps,),
+        in_specs=[whole(qkv),
+                  pl.BlockSpec((rows,2*LANES),lambda i:(i,0)),
+                  pl.BlockSpec((rows,2*LANES),lambda i:(i,0)),
+                  pl.BlockSpec((1,1,2*rows),lambda i:(i,0,0)),
+                  whole(cosine),whole(sine),whole(pick)],
+        out_specs=pl.BlockSpec((length,4*HD),lambda i:(0,0)),
+        out_shape=jax.ShapeDtypeStruct((length,4*HD),BF),
+        scratch_shapes=[pltpu.VMEM((LANES,length),BF),pltpu.VMEM((length,LANES),jnp.float32),
+                        pltpu.VMEM((length,LANES),jnp.float32),pltpu.VMEM((length,4*LANES),BF)],
+        compiler_params=pltpu.CompilerParams(vmem_limit_bytes=48*1024*1024),
+    )(qkv,out,grad,lse,cosine,sine,pick)
+
+def pad_columns():
+    half=HD//2
+    lanes=np.arange(4*LANES); block=lanes//LANES; lane=lanes%LANES
+    split=np.where(lane<half,lane,np.where((lane>=LANES//2)&(lane<LANES//2+half),lane-LANES//2+half,-1))
+    plain=np.where(lane<HD,lane,-1)
+    column=np.where(block<3,split,plain)
+    return np.where(column>=0,column+block*HD,-1)
+
+CORES, LINES, PLANES = 2, 2, 4
+CHIPS = LINES * PLANES
+RANKS = CORES * CHIPS
+
+
+def swap_fsdp(value):
+    return lax.ppermute(value, "fsdp", [(0, 1), (1, 0)])
+
+
+def swap_ctx(value, bit):
+    return lax.ppermute(value, "ctx", [(i, i ^ bit) for i in range(RANKS)])
+
+
+def swap_core(value):
+    return swap_ctx(value, 1)
+
+
+def swap_line(value):
+    return swap_ctx(value, CORES)
+
+
+def plane_up(value, sources):
+    step = CORES * LINES
+    return lax.ppermute(value, "ctx", [(z * step + i, z * step + step + i) for z in sources for i in range(step)])
+
+
+def plane_down(value, sources):
+    step = CORES * LINES
+    return lax.ppermute(value, "ctx", [(z * step + i, z * step - step + i) for z in sources for i in range(step)])
+
+
+def at(value, index, axis=0):
+    return lax.dynamic_index_in_dim(value, index, axis, keepdims=False)
+
+
+def in_order(which, mine, other):
+    first = which == 0
+    return jnp.concatenate([jnp.where(first, mine, other), jnp.where(first, other, mine)], axis=0)
+
+
+def after(value, earlier):
+    return lax.optimization_barrier((value, earlier))[0]
+
+
+def plane_scatter(pieces, plane):
+    up = down = None
+    last = PLANES - 1
+    for step in range(last):
+        term_up = at(pieces, jnp.clip(plane + last - step, 0, last))
+        term_down = at(pieces, jnp.clip(plane - last + step, 0, last))
+        if up is not None:
+            term_up = (term_up.astype(jnp.float32) + up.astype(jnp.float32)).astype(BF)
+            term_down = (term_down.astype(jnp.float32) + down.astype(jnp.float32)).astype(BF)
+        up = plane_up(term_up, range(0, step + 1))
+        down = plane_down(term_down, range(last - step, last + 1))
+    own = at(pieces, plane).astype(jnp.float32)
+    return own + up.astype(jnp.float32) + down.astype(jnp.float32)
+
+
+def line_scatter(kept, sent):
+    return (kept.astype(jnp.float32) + swap_line(sent).astype(jnp.float32)).astype(BF)
+
+
+def rope_rows(length):
+    lane = jnp.arange(LANES)
+    half = LANES // 2
+    entry = jnp.where(lane < half, lane, lane - half)
+    used = entry < HD // 2
+    inv_freq = 1.0 / ROPE_BASE ** (entry.astype(jnp.float32) * 2.0 / HD)
+    angles = jnp.arange(length, dtype=jnp.int32).astype(jnp.float32)[:, None] * inv_freq[None, :]
+    sign = jnp.where(lane < half, -1.0, 1.0)
+    return jnp.where(used, jnp.cos(angles), 0.0), jnp.where(used, jnp.sin(angles) * sign, 0.0)
+
+
+def mlp_part(normed, grad_rows, gate_up, down):
+    both = matmul(normed, gate_up)
+    half = both.shape[1] // 2
+    gate, upper = both[:, :half], both[:, half:]
+    sigma = jax.nn.sigmoid(gate)
+    active = gate * sigma
+    inner = (active * upper).astype(BF)
+    grad_inner = times_transposed(grad_rows, down)
+    grad_gate = (grad_inner * upper * sigma * (1.0 + gate * (1.0 - sigma))).astype(BF)
+    grad_upper = (grad_inner * active).astype(BF)
+    grad_both = jnp.concatenate([grad_gate, grad_upper], axis=1)
+    return inner, grad_both, matmul(inner, down), times_transposed(grad_both, gate_up)
+
+
+def head_shards(
+    tokens, attn_gain, w_query, w_key, w_value, w_out, mlp_gain, w_gate, w_up, w_down, cotangent
+):
+    seqs, width, model = tokens.shape
+    length = width * RANKS
+    rows = seqs * width
+    half_model = model // 2
+    hidden = w_gate.shape[1]
+    half_hidden = hidden // 2
+    chunk = hidden // (2 * RANKS)
+    rank = lax.axis_index("ctx")
+    side = lax.axis_index("fsdp")
+    core = rank % CORES
+    line = (rank // CORES) % LINES
+    plane = rank // (CORES * LINES)
+    chip = rank // CORES
+    pick = jnp.asarray((pad_columns()[:, None] == np.arange(HEAD_COLS)[None, :]).astype(np.float32)).astype(BF)
+    cosine, sine = rope_rows(length)
+
+    mine = at(tokens, core)
+    own_block = in_order(core, mine, swap_core(at(tokens, 1 - core)))
+    ups, downs = [], []
+    up = down = own_block
+    for step in range(PLANES - 1):
+        up = plane_up(up, range(step, PLANES - 1))
+        down = plane_down(down, range(1, PLANES - step))
+        ups.append(up)
+        downs.append(down)
+    low = plane < PLANES // 2
+    slots = [
+        own_block,
+        jnp.where(low, downs[0], ups[0]),
+        jnp.where(low, downs[1], ups[1]),
+        jnp.where(plane == 0, downs[2], jnp.where(plane == 1, ups[0], jnp.where(plane == 2, downs[0], ups[2]))),
+    ]
+
+    packed = jnp.concatenate(
+        [w_query.reshape(half_model, HK, -1), w_key.reshape(half_model, HK, -1), w_value.reshape(half_model, HK, -1)],
+        axis=2,
+    )
+    head_rows = at(packed, chip, 1)
+    head_got = swap_fsdp(head_rows)
+    head_weight = in_order(side, head_rows, head_got)
+    head_padded = times_transposed(head_weight, pick).astype(BF)
+
+    def fetch(block, earlier):
+        part = at(block.reshape((CORES, block.shape[0] // CORES) + block.shape[1:]), core)
+        got = swap_fsdp(after(part, earlier))
+        return in_order(core, got, swap_core(got)), got
+
+    out_other, done = fetch(w_out, head_got)
+    out_full = in_order(side, w_out, out_other)
+    out_padded = jnp.pad(out_full.reshape(HQ, HD, model), ((0, 0), (0, LANES - HD), (0, 0))).reshape(HQ * LANES, model)
+
+    def columns_of(block, which):
+        cut = block.reshape(half_model, PLANES, LINES, CORES, 2, chunk)
+        return at(cut, which, 4).transpose(0, 3, 2, 1, 4).reshape(half_model, half_hidden)
+
+    first = core == 0
+    sent = jnp.where(first, columns_of(w_gate, 1 - side), columns_of(w_up, 1 - side))
+    got = swap_fsdp(after(sent, done))
+    other = swap_core(got)
+    gate_up = in_order(
+        side,
+        jnp.concatenate([columns_of(w_gate, side), columns_of(w_up, side)], axis=1),
+        jnp.concatenate([jnp.where(first, got, other), jnp.where(first, other, got)], axis=1),
+    )
+    down_cut = w_down.reshape(PLANES // 2, LINES, CORES, 2, chunk, model)
+    down_other, done = fetch(at(down_cut, 1 - side, 3).reshape(-1, model), got)
+    down_rows = in_order(side, at(down_cut, side, 3).reshape(-1, model), down_other)
+    down_weight = (
+        down_rows.reshape(PLANES, LINES, CORES, chunk, model).transpose(2, 1, 0, 3, 4).reshape(half_hidden, model)
+    )
+    grad_down = cotangent.reshape(rows, model)
+    grad_down_other = swap_fsdp(after(grad_down, done))
+
+    normed_seq = jnp.zeros((CHIPS, 2 * width, model), BF)
+    raw_seq = jnp.zeros((CHIPS, 2 * width, 4 * LANES), jnp.float32)
+    for number, piece in enumerate(slots):
+        place = jnp.where(low, plane + number, plane - number) % PLANES
+        for across in range(LINES):
+            block = swap_line(piece) if across else piece
+            spot = place * LINES + (line if across == 0 else 1 - line)
+            normed = (normalize(block.astype(jnp.float32))[0] * attn_gain).astype(BF)
+            normed_seq = lax.dynamic_update_index_in_dim(normed_seq, normed, spot, 0)
+            raw_seq = lax.dynamic_update_index_in_dim(raw_seq, matmul(normed, head_padded), spot, 0)
+    normed_seq = normed_seq.reshape(length, model)
+    qkv, attended_seq, lse = head_forward(raw_seq.reshape(length, 4 * LANES), cosine, sine)
+
+    def exchange(value):
+        return lax.all_to_all(value.reshape(RANKS, width, -1), "ctx", 0, 0, tiled=True)
+
+    attended = (
+        exchange(attended_seq).reshape(CHIPS, CORES, width, 2 * LANES).transpose(1, 2, 0, 3).reshape(rows, HQ * LANES)
+    )
+    inputs = tokens.reshape(rows, model).astype(jnp.float32)
+    resid = inputs + matmul(attended, out_padded)
+    unit_two, inv_two = normalize(resid)
+    normed_two = (unit_two * mlp_gain).astype(BF)
+
+    normed_other = swap_fsdp(normed_two)
+    inner_own, grad_both_own, mixed_own, back_own = mlp_part(normed_two, grad_down, gate_up, down_weight)
+    inner_other, grad_both_other, mixed_other, back_other = mlp_part(
+        normed_other, grad_down_other, gate_up, down_weight
+    )
+    back_got = swap_fsdp(back_other.astype(BF))
+    mixed_got = swap_fsdp(after(mixed_other.astype(BF), back_got))
+    mixed = (resid + mixed_own + mixed_got.astype(jnp.float32)).astype(BF)
+    grad_normed_two = back_own + back_got.astype(jnp.float32)
+    grad_resid = grad_down.astype(jnp.float32) + norm_back(grad_normed_two, mlp_gain, unit_two, inv_two)
+    mlp_gain_part = jnp.sum(grad_normed_two * unit_two, axis=0)
+    grad_branch = grad_resid.astype(BF)
+    grad_attended = times_transposed(grad_branch, out_padded).astype(BF)
+    grad_att_seq = exchange(grad_attended.reshape(CORES, width, CHIPS, 2 * LANES).transpose(2, 0, 1, 3)).reshape(
+        length, 2 * LANES
+    )
+
+    acts = jnp.concatenate(
+        [
+            jnp.concatenate([inner_own, grad_both_own], axis=1),
+            jnp.concatenate([inner_other, grad_both_other], axis=1),
+        ],
+        axis=0,
+    ).reshape(2 * rows, 3, CORES, half_hidden // CORES)
+    acts_got = swap_core(at(acts, 1 - core, 2))
+    acts_all = jnp.concatenate([at(acts, core, 2), acts_got], axis=0)
+    normed_pair = jnp.concatenate([normed_two, normed_other], axis=0)
+    normed_all = jnp.concatenate([normed_pair, swap_core(normed_pair)], axis=0)
+    cot_pair = jnp.concatenate([grad_down, grad_down_other], axis=0)
+    cot_all = jnp.concatenate([cot_pair, swap_core(cot_pair)], axis=0)
+    part_hidden = half_hidden // CORES
+    grad_down_weight = transposed_times(cot_all, acts_all[:, 0]).astype(BF)
+    grad_gate_up = transposed_times(acts_all[:, 1:].reshape(-1, 2 * part_hidden), normed_all).astype(BF)
+
+    per_chip = model // CHIPS
+    cut = grad_down_weight.reshape(PLANES, LINES, per_chip, part_hidden)
+    reduced = plane_scatter(line_scatter(at(cut, line, 1), at(cut, 1 - line, 1)), plane)
+    cut = grad_gate_up.reshape(2, LINES, PLANES, chunk, model)
+    halves = line_scatter(at(cut, line, 1), at(cut, 1 - line, 1))
+    gate_up_reduced = plane_scatter(halves.transpose(1, 0, 2, 3), plane).astype(BF)
+    cut = gate_up_reduced.reshape(2, chunk, 2, half_model)
+    gate_up_got = swap_fsdp(at(cut, 1 - side, 2))
+    gate_up_keep = at(cut, side, 2)
+    low_side = side == 0
+    gate_up_grad = jnp.concatenate(
+        [jnp.where(low_side, gate_up_keep, gate_up_got), jnp.where(low_side, gate_up_got, gate_up_keep)], axis=1
+    ).astype(jnp.float32)
+    w_gate_grad, w_up_grad = gate_up_grad[0].T, gate_up_grad[1].T
+
+    cut = reduced.astype(BF).reshape(CORES, model // RANKS, LINES, 2, PLANES // 2, chunk)
+    keep, got = at(cut, core), swap_core(at(cut, 1 - core))
+    by_core = jnp.stack([jnp.where(first, keep, got), jnp.where(first, got, keep)], axis=3)
+    keep, got = at(by_core, side, 2), swap_fsdp(at(by_core, 1 - side, 2))
+    by_side = jnp.stack([jnp.where(low_side, keep, got), jnp.where(low_side, got, keep)], axis=4)
+    w_down_grad = by_side.transpose(0, 3, 1, 2, 4, 5).reshape(model // RANKS, -1).T.astype(jnp.float32)
+
+    att_cut = attended.reshape(rows, 2, HK * LANES)
+    att_other, branch_other = swap_fsdp((at(att_cut, 1 - side, 1), grad_branch))
+    att_pair = jnp.concatenate([at(att_cut, side, 1), att_other], axis=0)
+    branch_pair = jnp.concatenate([grad_branch, branch_other], axis=0)
+    cut = transposed_times(branch_pair, att_pair).astype(BF).reshape(CHIPS, CORES, model // RANKS, HK * LANES)
+    got = swap_core(at(cut, 1 - core, 1))
+    pair_sum = (at(cut, core, 1).astype(jnp.float32) + got.astype(jnp.float32)).astype(BF)
+    cut = pair_sum.reshape(PLANES, LINES, model // RANKS, HK * LANES)
+    reduced = plane_scatter(line_scatter(at(cut, line, 1), at(cut, 1 - line, 1)), plane)
+    w_out_grad = reduced.reshape(model // RANKS, HK, LANES)[:, :, :HD].reshape(model // RANKS, half_model).T
+
+    grad_qkv = head_backward(qkv, attended_seq, grad_att_seq, lse, cosine, sine, pick)
+    grad_own = exchange(grad_qkv).reshape(CHIPS, CORES, width, HEAD_COLS).transpose(1, 2, 0, 3).reshape(rows, -1)
+
+    head_grad = transposed_times(grad_qkv, normed_seq)
+    gain_part = jnp.sum(head_grad * head_weight.T.astype(jnp.float32), axis=0) / attn_gain
+    query_cut = head_grad[: 2 * HD].reshape(CORES, HD, model)
+    key_cut = head_grad[2 * HD :].reshape(2, CORES, HD // 2, model)
+
+    def of_core(which):
+        return jnp.concatenate([at(query_cut, which), at(key_cut, which, 1).reshape(HD, model)], axis=0)
+
+    two = of_core(core) + swap_core(of_core(1 - core).astype(BF)).astype(jnp.float32)
+    cut = two.reshape(2 * HD, 2, half_model)
+    four = at(cut, side, 1) + swap_fsdp(at(cut, 1 - side, 1).astype(BF)).astype(jnp.float32)
+    w_query_grad = four[:HD].T
+    w_key_grad = four[HD : HD + HD // 2].T
+    w_value_grad = four[HD + HD // 2 :].T
+
+    gains = jnp.stack([gain_part, mlp_gain_part])
+    gains = gains + swap_fsdp(gains)
+    for bit in (1, 2, 4, 8):
+        gains = gains + swap_ctx(gains, bit)
+
+    packed_other, _ = fetch(packed.reshape(half_model, HK * HEAD_COLS), back_got)
+    packed_full = in_order(side, packed.reshape(half_model, HK * HEAD_COLS), packed_other)
+    grad_normed_one = times_transposed(grad_own, packed_full)
+    unit_one, inv_one = normalize(inputs)
+    tokens_grad = (grad_resid + norm_back(grad_normed_one, attn_gain, unit_one, inv_one)).astype(BF)
+    return (
+        mixed.reshape(seqs, width, model),
+        tokens_grad.reshape(seqs, width, model),
+        gains[0],
+        w_query_grad,
+        w_key_grad,
+        w_value_grad,
+        w_out_grad,
+        gains[1],
+        w_gate_grad,
+        w_up_grad,
+        w_down_grad,
+    )
+
+
 def solution(mesh):
+    by_heads = mesh.shape["ctx"] == RANKS and mesh.shape["fsdp"] == 2
     placed = (
         P("fsdp", "ctx", None),
         P(),
@@ -322,7 +770,7 @@
         P("fsdp", "ctx", None),
     )
     return jax.shard_map(
-        shards,
+        head_shards if by_heads else shards,
         mesh=mesh,
         in_specs=placed,
         out_specs=(

time: 2470 us -> 894 us (0.36)
  waiting for transfers between devices: 1970 us -> 320 us
  matrix products: 298 us -> 94.3 us
  local copies, waits for them, and re-layouts: 84.3 us -> 189 us
  starting transfers between devices: 1.35 us -> 102 us
  other arithmetic: 47.1 us -> 144 us
  blocking collectives: 41 us -> 0 us
  Pallas kernels: 0 us -> 32.5 us
    all_gather x11 -> x0, waiting for transfers between devices: 751 us -> none  [the longest x1 146 us: shards(): lax.all_gather(w_down, 'fsdp', axis=0, tiled=True)]
    reduce_scatter x9 -> x0, waiting for transfers between devices: 735 us -> none  [the longest x7 562 us: reduce_grad(): lax.psum_scatter(full_grad.astype(jnp.bfloat16), 'fsdp', scatter_dimensio...]
    unnamed x38 -> x0, waiting for transfers between devices: 484 us -> none
    ppermute x0 -> x61, waiting for transfers between devices: none -> 306 us  [the longest x22 148 us: swap_ctx(): return lax.ppermute(value, 'ctx', [(i, i ^ bit) for i in range(RANKS)])]
    dot_general x12 -> x0, matrix products: 132 us -> none  [the longest x2 45.4 us: attend_backward(): jnp.einsum('cgrd,lgd->grcl', grad_heads, value_heads, preferred_element_t...]
    ppermute x0 -> x61, starting transfers between devices: none -> 82.5 us  [the longest x12 30.7 us: plane_up(): lax.ppermute(value, 'ctx', [(z * step + i, z * step + step + i) for z in...]
    concatenate x8 -> x9, other arithmetic: 3.33 us -> 58 us  [the longest x1 39.3 us: head_shards(): jnp.concatenate([jnp.concatenate([inner_own, grad_both_own], axis=1), jnp...]
    psum x1 -> x0, blocking collectives: 41 us -> none  [shards(): lax.psum((attn_gain_acc, mlp_gain_acc), ('ctx', 'fsdp'))]
  transfers between devices with their start and end apart: 29 -> 64, of which waited for: 27 -> 28; matrix products, arithmetic and copies ran while one was open for 11% -> 45% of each run, Pallas kernels for 0% -> 4%
where the time goes in v1:
time: 894 us; the launch traced here: 885 us
  waiting for transfers between devices  320 us (36%)
  local copies, waits for them, and re-layouts  189 us (21%)
  other arithmetic  144 us (16%)
  starting transfers between devices  102 us (11%)
  matrix products  94.3 us (11%)
  Pallas kernels  32.5 us (4%)
    ppermute x22, waiting for transfers between devices, swap_ctx(): return lax.ppermute(value, 'ctx', [(i, i ^ bit) for i in range(RANKS)])  148 us
    unnamed x183, local copies, waits for them, and re-layouts  66.8 us
    ppermute x15, waiting for transfers between devices, swap_fsdp(): return lax.ppermute(value, 'fsdp', [(0, 1), (1, 0)])  61.5 us
    ppermute x12, waiting for transfers between devices, plane_down(): lax.ppermute(value, 'ctx', [(z * step + i, z * step - step + i) for z in...  51 us
    ppermute x12, waiting for transfers between devices, plane_up(): lax.ppermute(value, 'ctx', [(z * step + i, z * step + step + i) for z in...  45.9 us
    concatenate x1, other arithmetic, head_shards(): jnp.concatenate([jnp.concatenate([inner_own, grad_both_own], axis=1), jnp...  39.3 us
    dot_general x7, matrix products, times_transposed(): lax.dot_general(left, right, (((1,), (1,)), ((), ())), preferred_element_...  36.7 us
    dot_general x13, matrix products, matmul(): return jnp.dot(left, right, preferred_element_type=jnp.float32)  33.5 us
  transfers between devices with their start and end apart: 64, of which 28 were waited for; matrix products, arithmetic and copies ran while one was open for 45% of the time, Pallas kernels for 4%

profile of v1, /device:TPU:12, one launch (start us, length us, event | category | flops | bytes accessed | tf_op | source)
XLA Modules:
  0.0 884.7 jit_solution(4111461223641104526)
XLA Ops:
  17.1 10.1 %reshape_reshape.10 = bf16[2,384,3072]{1,0,2:T(2,128)(2,1)} reshape(bf16[768,8,384]{0,2,1:T(8,128)(2,1)} %copy-done.3) | data formatting | bytes 9437184 | tf_op jit(solution)/shard_map/reshape;reshape | solution.py:593
  27.2 8.7 copy.60
  35.9 8.6 copy.63
  44.5 7.1 dynamic-slice_bitcast_fusion.2
  51.6 4.1 copy.67
  66.1 6.7 copy.74
  72.8 6.9 constant_dynamic-slice_fusion.10
  79.8 10.7 %copy.103 = bf16[1,384,3072]{2,1,0:T(8,128)(2,1)} copy(bf16[1,384,3072]{1,0,2:T(2,128)(2,1)} %constant_dynamic-slice_fusion.10) | data formatting | bytes 4718592
  90.5 3.8 fusion.81
  109.6 7.3 collective-permute-done.3
  119.2 3.6 collective-permute-start.7
  124.2 13.4 %collective-permute-done.6 = bf16[256,1536]{1,0:T(8,128)(2,1)S(1)} collective-permute-done((bf16[256,1536]{1,0:T(8,128)(2,1)S(1)}, bf16[256,1536]{1,0:T(8,128)(2,1)S(1)}, u32[]{:S(2)}, u32[]{:S(2)}) %collective-permute-start.6) | collective-permute-done | bytes 786464 | tf_op jit(solution)/shard_map/ppermute | solution.py:487
  144.2 11.2 %collective-permute-done.9 = bf16[256,1536]{1,0:T(8,128)(2,1)S(1)} collective-permute-done((bf16[256,1536]{1,0:T(8,128)(2,1)S(1)}, bf16[256,1536]{1,0:T(8,128)(2,1)S(1)}, u32[]{:S(2)}, u32[]{:S(2)}) %collective-permute-start.9) | collective-permute-done | bytes 786464 | tf_op jit(solution)/shard_map/ppermute | solution.py:487
  158.6 4.6 collective-permute-done.8
  169.8 10.2 %collective-permute-done.5 = bf16[256,1536]{1,0:T(8,128)(2,1)S(1)} collective-permute-done((bf16[256,1536]{1,0:T(8,128)(2,1)S(1)}, bf16[256,1536]{1,0:T(8,128)(2,1)S(1)}, u32[]{:S(2)}, u32[]{:S(2)}) %collective-permute-start.5) | collective-permute-done | bytes 786464 | tf_op jit(solution)/shard_map/ppermute | solution.py:469
  180.2 16.2 %collective-permute-done.11 = bf16[256,1536]{1,0:T(8,128)(2,1)S(1)} collective-permute-done((bf16[256,1536]{1,0:T(8,128)(2,1)S(1)}, bf16[256,1536]{1,0:T(8,128)(2,1)S(1)}, u32[]{:S(2)}, u32[]{:S(2)}) %collective-permute-start.11) | collective-permute-done | bytes 786464 | tf_op jit(solution)/shard_map/ppermute | solution.py:469
  201.9 11.8 %shard_map.203 = (bf16[2048,512]{1,0:T(8,128)(2,1)S(1)}, bf16[2048,256]{1,0:T(8,128)(2,1)}, f32[4,1,1024]{2,1,0:T(1,128)S(1)}) custom-call(f32[2048,512]{1,0:T(8,128)} %bitcast.367, f32[2048,128]{1,0:T(8,128)S(1)} %get-tuple-element.107.cos_ref, f32[2048,128]{1,0:T(8,128)S(1)} %get-tuple-element.106.sin_ref), custom_call_target="tpu_custom_call" | custom-call | tf_op jit(solution)/shard_map/pallas_call | solution.py:369
  215.1 7.7 all-to-all-start
  233.6 13.8 %all-to-all-done = bf16[16,128,256]{2,1,0:T(8,128)(2,1)} async-done(((bf16[16,128,256]{2,1,0:T(8,128)(2,1)}), bf16[16,128,256]{2,1,0:T(8,128)(2,1)}, u32[]{:S(2)}, u32[]{:S(2)}) %all-to-all-start) | async-done | bytes 1048608 | tf_op jit(solution)/shard_map/all_to_all | solution.py:637
  250.2 4.7 multiply_reduce_fusion.4
  258.6 9.9 %collective-permute-done.16 = bf16[512,1536]{1,0:T(8,128)(2,1)} collective-permute-done((bf16[512,1536]{1,0:T(8,128)(2,1)}, bf16[512,1536]{1,0:T(8,128)(2,1)}, u32[]{:S(2)}, u32[]{:S(2)}) %collective-permute-start.16) | collective-permute-done | bytes 1572896 | tf_op jit(solution)/shard_map/ppermute | solution.py:465
  279.1 6.3 collective-permute-done.18
  288.1 14.2 %collective-permute-done.19 = bf16[256,1536]{1,0:T(8,128)(2,1)} collective-permute-done((bf16[256,1536]{1,0:T(8,128)(2,1)}, bf16[256,1536]{1,0:T(8,128)(2,1)}, u32[]{:S(2)}, u32[]{:S(2)}) %collective-permute-start.19) | collective-permute-done | bytes 786464 | tf_op jit(solution)/shard_map/ppermute | solution.py:465
  320.6 4.6 broadcast_select_fusion.1
  325.3 9.7 %fusion.124 = f32[256,4096]{1,0:T(8,128)} fusion(bf16[256,1536]{1,0:T(8,128)(2,1)} %multiply_convert_fusion.7, bf16[768,4096]{0,1:T(8,128)(2,1)} %get-tuple-element.40, bf16[768,4096]{0,1:T(8,128)(2,1)S(1)} %get-tuple-element.39), kind=kOutput, calls=%fused_computation.316 | convolution fusion | flops 3246391296 | bytes 17563648 | tf_op jit(solution)/shard_map/dot_general | solution.py:26
  335.0 6.1 multiply_convert_fusion.1
  341.1 7.5 fusion.123
  348.6 6.1 multiply_convert_fusion.3
  354.7 8.6 convolution_convert_fusion.6
  364.8 39.3 %maximum_maximum_fusion = bf16[512,6144]{1,0:T(8,128)(2,1)} fusion(bf16[256,2048]{1,0:T(8,128)(2,1)S(1)} %copy-done.59, bf16[256,2048]{1,0:T(8,128)(2,1)S(1)} %copy-done.58, bf16[256,2048]{1,0:T(8,128)(2,1)S(1)} %get-tuple-element.63, bf16[256,2048]{1,0:T(8,128)(2,1)S(1)} %copy-done.56, bf16[256,2048]{1,0:T(8,128)(2,1)S(1)} %copy-done.54, ...), kind=kLoop, calls=%fused_computation.9 | loop fusion | flops 37748736 | bytes 12582912 | tf_op jit(solution)/shard_map/concatenate | solution.py:664
  404.1 14.5 %reshape.471 = bf16[512,3,2,1024]{3,2,1,0:T(2,128)(2,1)} reshape(bf16[512,6144]{1,0:T(8,128)(2,1)} %maximum_maximum_fusion) | data formatting | bytes 12582912 | tf_op jit(solution)/shard_map/reshape | solution.py:670
  418.7 16.3 %constant_dynamic-slice_fusion.4 = (bf16[512,3,1,1024]{3,2,1,0:T(2,128)(2,1)}, bf16[512,3,1,1024]{3,2,1,0:T(2,128)(2,1)}) fusion(bf16[512,3,2,1024]{3,2,1,0:T(2,128)(2,1)} %reshape.471, s32[]{:T(128)S(6)} %select_n.411, s32[]{:T(128)S(6)} %select_n.410), kind=kLoop, calls=%fused_computation.277 | loop fusion | bytes 12582920 | tf_op jit(solution)/shard_map/jit(dynamic_index_in_dim)/dynamic_slice | solution.py:491
  435.0 8.0 multiply_reduce_fusion
  451.4 6.0 all-to-all-start.1
  457.4 4.9 convolution_convert_fusion.5
  462.3 5.9 copy.130
  468.2 5.9 copy.129
  483.5 11.0 %collective-permute-done.21 = bf16[256,1536]{1,0:T(8,128)(2,1)S(1)} collective-permute-done((bf16[256,1536]{1,0:T(8,128)(2,1)S(1)}, bf16[256,1536]{1,0:T(8,128)(2,1)S(1)}, u32[]{:S(2)}, u32[]{:S(2)}) %collective-permute-start.21) | collective-permute-done | bytes 786464 | tf_op jit(solution)/shard_map/ppermute | solution.py:465
  495.6 20.7 %shard_map.204 = bf16[2048,384]{1,0:T(8,128)(2,1)} custom-call(bf16[2048,512]{1,0:T(8,128)(2,1)} %copy-done, bf16[2048,256]{1,0:T(8,128)(2,1)} %get-tuple-element.20.out_ref, bf16[2048,256]{1,0:T(8,128)(2,1)S(1)} %bitcast.359, f32[8,1,512]{2,1,0:T(1,128)S(1)} %reshape.455.lse_ref, f32[2048,128]{1,0:T(8,128)S(1)} %get-tuple-element.107.cos_ref, ...), custom_call_target="tpu_custom_call" | custom-call | tf_op jit(solution)/shard_map/pallas_call | solution.py:436
  516.3 5.5 fusion.21
  524.4 20.1 %collective-permute-done.24 = f32[2,1536]{1,0:T(2,128)S(1)} collective-permute-done((f32[2,1536]{1,0:T(2,128)S(1)}, f32[2,1536]{1,0:T(2,128)S(1)}, u32[]{:S(2)}, u32[]{:S(2)}) %collective-permute-start.24) | collective-permute-done | bytes 12320 | tf_op jit(solution)/shard_map/ppermute | solution.py:465
  551.0 6.3 all-to-all-start.2
  561.5 30.8 %collective-permute-done.28 = f32[2,1536]{1,0:T(2,128)S(1)} collective-permute-done((f32[2,1536]{1,0:T(2,128)S(1)}, f32[2,1536]{1,0:T(2,128)S(1)}, u32[]{:S(2)}, u32[]{:S(2)}) %collective-permute-start.28) | collective-permute-done | bytes 12320 | tf_op jit(solution)/shard_map/ppermute | solution.py:469
  596.9 6.2 copy.79
  603.1 9.6 %convolution_convert_fusion = bf16[2048,1536]{1,0:T(8,128)(2,1)S(1)} fusion(bf16[1024,2048]{0,1:T(8,128)(2,1)} %bitcast.401, bf16[512,1536]{1,0:T(8,128)(2,1)} %collective-permute-done.42, bf16[256,1536]{1,0:T(8,128)(2,1)} %collective-permute-done.18, bf16[256,1536]{1,0:T(8,128)(2,1)} %multiply_convert_fusion.7), kind=kOutput, calls=%fused_computation.5 | convolution fusion | flops 6455033856 | bytes 13631488 | tf_op jit(solution)/shard_map/dot_general | solution.py:36
  623.1 5.6 convolution_convert_fusion.2
  635.4 69.6 %collective-permute-done.34 = bf16[4,96,1024]{2,1,0:T(8,128)(2,1)} collective-permute-done((bf16[4,96,1024]{2,1,0:T(8,128)(2,1)}, bf16[4,96,1024]{2,1,0:T(8,128)(2,1)}, u32[]{:S(2)}, u32[]{:S(2)}) %collective-permute-start.34) | collective-permute-done | bytes 786464 | tf_op jit(solution)/shard_map/ppermute | solution.py:469
  710.4 4.5 collective-permute-done.35
  718.5 5.5 collective-permute-done.36
  725.6 12.1 %collective-permute-done.52 = bf16[4,192,1024]{2,1,0:T(8,128)(2,1)} collective-permute-done((bf16[4,192,1024]{2,1,0:T(8,128)(2,1)}, bf16[4,192,1024]{2,1,0:T(8,128)(2,1)}, u32[]{:S(2)}, u32[]{:S(2)}) %collective-permute-start.52) | collective-permute-done | bytes 1572896 | tf_op jit(solution)/shard_map/ppermute | solution.py:469
  744.9 3.9 collective-permute-start.40
  748.8 6.0 collective-permute-done.53
  761.1 7.8 collective-permute-done.54
  772.4 4.6 collective-permute-start.55
  776.9 3.8 fusion.4
  787.6 12.8 %collective-permute-done.44 = bf16[2,128,1536]{2,1,0:T(8,128)(2,1)S(1)} collective-permute-done((bf16[2,128,1536]{2,1,0:T(8,128)(2,1)S(1)}, bf16[2,128,1536]{2,1,0:T(8,128)(2,1)S(1)}, u32[]{:S(2)}, u32[]{:S(2)}) %collective-permute-start.44) | collective-permute-done | bytes 786464 | tf_op jit(solution)/shard_map/ppermute | solution.py:482
  803.4 5.4 broadcast_select_fusion.3
  811.6 7.6 collective-permute-done.45
  823.2 3.9 multiply_reduce_fusion.1
  830.2 4.6 collective-permute-start.46
  834.7 9.5 %collective-permute-done.48 = bf16[2,128,1536]{2,1,0:T(8,128)(2,1)S(1)} collective-permute-done((bf16[2,128,1536]{2,1,0:T(8,128)(2,1)S(1)}, bf16[2,128,1536]{2,1,0:T(8,128)(2,1)S(1)}, u32[]{:S(2)}, u32[]{:S(2)}) %collective-permute-start.48) | collective-permute-done | bytes 786464 | tf_op jit(solution)/shard_map/ppermute | solution.py:487
  847.5 5.1 collective-permute-done.58
  859.4 4.4 collective-permute-done.49
  875.2 3.7 add_convert_fusion
  (422 shorter events, 246.6 us)
Async XLA Ops:
  13.6 91.9 %collective-permute-start.1 = (bf16[768,384]{0,1:T(8,128)(2,1)}, bf16[768,384]{0,1:T(8,128)(2,1)}, u32[]{:S(2)}, u32[]{:S(2)}) collective-permute-start(bf16[768,384]{0,1:T(8,128)(2,1)} %dynamic-slice_bitcast_fusion.11), channel_id=1, source_target_pairs={{0,1},{1,0},{2,3},{3,2},{4,5},{5,4},{6,7},{7,6},{8,9},{9,8},{10,11... | collective-permute-start | bytes 1769480 | tf_op jit(solution)/shard_map/ppermute | solution.py:465
  15.8 78.5 %collective-permute-start = (bf16[128,1536]{1,0:T(8,128)(2,1)}, bf16[128,1536]{1,0:T(8,128)(2,1)S(1)}, u32[]{:S(2)}, u32[]{:S(2)}) collective-permute-start(bf16[128,1536]{1,0:T(8,128)(2,1)} %dynamic-slice_bitcast_fusion.14), channel_id=1, source_target_pairs={{0,2},{2,0},{4,6},{6,4},{8,10},{10,8},{12,14},{14,12},{16,18},{18,... | collective-permute-start | bytes 1179656 | tf_op jit(solution)/shard_map/ppermute | solution.py:469
  94.7 28.1 %collective-permute-start.2 = (bf16[256,1536]{1,0:T(8,128)(2,1)S(1)}, bf16[256,1536]{1,0:T(8,128)(2,1)S(1)}, u32[]{:S(2)}, u32[]{:S(2)}) collective-permute-start(bf16[256,1536]{1,0:T(8,128)(2,1)S(1)} %pad_maximum_fusion.13), channel_id=1, source_target_pairs={{0,4},{2,6},{4,0},{6,2},{8,12},{10,14},{12,8},{14,10},{16,20},{18,... | collective-permute-start | bytes 2359304 | tf_op jit(solution)/shard_map/ppermute | solution.py:469
  95.3 21.6 %collective-permute-start.3 = (bf16[256,1536]{1,0:T(8,128)(2,1)S(1)}, bf16[256,1536]{1,0:T(8,128)(2,1)S(1)}, u32[]{:S(2)}, u32[]{:S(2)}) collective-permute-start(bf16[256,1536]{1,0:T(8,128)(2,1)S(1)} %pad_maximum_fusion.13), channel_id=1, source_target_pairs={{8,0},{10,2},{12,4},{14,6},{16,8},{18,10},{20,12},{22,14},{24,16},... | collective-permute-start | bytes 2359304 | tf_op jit(solution)/shard_map/ppermute | solution.py:487
  97.6 21.6 %collective-permute-start.4 = (bf16[256,1536]{1,0:T(8,128)(2,1)S(1)}, bf16[256,1536]{1,0:T(8,128)(2,1)S(1)}, u32[]{:S(2)}, u32[]{:S(2)}) collective-permute-start(bf16[256,1536]{1,0:T(8,128)(2,1)S(1)} %pad_maximum_fusion.13), channel_id=1, source_target_pairs={{0,8},{2,10},{4,12},{6,14},{8,16},{10,18},{12,20},{14,22},{16,24},... | collective-permute-start | bytes 2359304 | tf_op jit(solution)/shard_map/ppermute | solution.py:482
  105.5 36.1 %collective-permute-start.12 = (bf16[384,1536]{1,0:T(8,128)(2,1)S(1)}, bf16[384,1536]{1,0:T(8,128)(2,1)S(1)}, u32[]{:S(2)}, u32[]{:S(2)}) collective-permute-start(bf16[384,1536]{1,0:T(8,128)(2,1)S(1)} %copy-done.49), channel_id=1, source_target_pairs={{0,1},{1,0},{2,3},{3,2},{4,5},{5,4},{6,7},{7,6},{8,9},{9,8},{10,11... | collective-permute-start | bytes 3538952 | tf_op jit(solution)/shard_map/ppermute | solution.py:465
  116.8 20.7 %collective-permute-start.6 = (bf16[256,1536]{1,0:T(8,128)(2,1)S(1)}, bf16[256,1536]{1,0:T(8,128)(2,1)S(1)}, u32[]{:S(2)}, u32[]{:S(2)}) collective-permute-start(bf16[256,1536]{1,0:T(8,128)(2,1)S(1)} %collective-permute-done.3), channel_id=1, source_target_pairs={{8,0},{10,2},{12,4},{14,6},{16,8},{18,10},{20,12},{22,14},{9,1},{1... | collective-permute-start | bytes 2359304 | tf_op jit(solution)/shard_map/ppermute | solution.py:487
  119.2 20.8 %collective-permute-start.7 = (bf16[256,1536]{1,0:T(8,128)(2,1)S(1)}, bf16[256,1536]{1,0:T(8,128)(2,1)S(1)}, u32[]{:S(2)}, u32[]{:S(2)}) collective-permute-start(bf16[256,1536]{1,0:T(8,128)(2,1)S(1)} %collective-permute-done.4), channel_id=1, source_target_pairs={{8,16},{10,18},{12,20},{14,22},{16,24},{18,26},{20,28},{22,30},{9,... | collective-permute-start | bytes 2359304 | tf_op jit(solution)/shard_map/ppermute | solution.py:482
  137.6 17.8 %collective-permute-start.9 = (bf16[256,1536]{1,0:T(8,128)(2,1)S(1)}, bf16[256,1536]{1,0:T(8,128)(2,1)S(1)}, u32[]{:S(2)}, u32[]{:S(2)}) collective-permute-start(bf16[256,1536]{1,0:T(8,128)(2,1)S(1)} %collective-permute-done.6), channel_id=1, source_target_pairs={{8,0},{10,2},{12,4},{14,6},{9,1},{11,3},{13,5},{15,7}} | collective-permute-start | bytes 2359304 | tf_op jit(solution)/shard_map/ppermute | solution.py:487
  140.0 15.4 %collective-permute-start.10 = (bf16[256,1536]{1,0:T(8,128)(2,1)S(1)}, bf16[256,1536]{1,0:T(8,128)(2,1)S(1)}, u32[]{:S(2)}, u32[]{:S(2)}) collective-permute-start(bf16[256,1536]{1,0:T(8,128)(2,1)S(1)} %collective-permute-done.7), channel_id=1, source_target_pairs={{16,24},{18,26},{20,28},{22,30},{17,25},{19,27},{21,29},{23,31}} | collective-permute-start | bytes 2359304 | tf_op jit(solution)/shard_map/ppermute | solution.py:482
  141.6 89.4 %collective-permute-start.14 = (bf16[768,2048]{0,1:T(8,128)(2,1)}, bf16[768,2048]{0,1:T(8,128)(2,1)}, u32[]{:S(2)}, u32[]{:S(2)}) collective-permute-start(bf16[768,2048]{0,1:T(8,128)(2,1)} %bitcast.36), channel_id=1, source_target_pairs={{0,1},{1,0},{2,3},{3,2},{4,5},{5,4},{6,7},{7,6},{8,9},{9,8},{10,11... | collective-permute-start | bytes 9437192 | tf_op jit(solution)/shard_map/ppermute | solution.py:465
  142.4 22.8 %collective-permute-start.13 = (bf16[384,1536]{1,0:T(8,128)(2,1)S(1)}, bf16[384,1536]{1,0:T(8,128)(2,1)S(1)}, u32[]{:S(2)}, u32[]{:S(2)}) collective-permute-start(bf16[384,1536]{1,0:T(8,128)(2,1)S(1)} %collective-permute-done.12), channel_id=1, source_target_pairs={{0,2},{2,0},{4,6},{6,4},{8,10},{10,8},{12,14},{14,12},{16,18},{18,... | collective-permute-start | bytes 3538952 | tf_op jit(solution)/shard_map/ppermute | solution.py:469
  142.7 20.4 %collective-permute-start.8 = (bf16[256,1536]{1,0:T(8,128)(2,1)S(1)}, bf16[256,1536]{1,0:T(8,128)(2,1)S(1)}, u32[]{:S(2)}, u32[]{:S(2)}) collective-permute-start(bf16[256,1536]{1,0:T(8,128)(2,1)S(1)} %get-tuple-element.36), channel_id=1, source_target_pairs={{0,4},{2,6},{4,0},{6,2},{8,12},{10,14},{12,8},{14,10},{16,20},{18,... | collective-permute-start | bytes 2359304 | tf_op jit(solution)/shard_map/ppermute | solution.py:469
  156.5 23.5 %collective-permute-start.5 = (bf16[256,1536]{1,0:T(8,128)(2,1)S(1)}, bf16[256,1536]{1,0:T(8,128)(2,1)S(1)}, u32[]{:S(2)}, u32[]{:S(2)}) collective-permute-start(bf16[256,1536]{1,0:T(8,128)(2,1)S(1)} %get-tuple-element.81), channel_id=1, source_target_pairs={{0,4},{2,6},{4,0},{6,2},{8,12},{10,14},{12,8},{14,10},{16,20},{18,... | collective-permute-start | bytes 2359304 | tf_op jit(solution)/shard_map/ppermute | solution.py:469
  158.1 38.4 %collective-permute-start.11 = (bf16[256,1536]{1,0:T(8,128)(2,1)S(1)}, bf16[256,1536]{1,0:T(8,128)(2,1)S(1)}, u32[]{:S(2)}, u32[]{:S(2)}) collective-permute-start(bf16[256,1536]{1,0:T(8,128)(2,1)S(1)} %get-tuple-element.34), channel_id=1, source_target_pairs={{0,4},{2,6},{4,0},{6,2},{8,12},{10,14},{12,8},{14,10},{16,20},{18,... | collective-permute-start | bytes 2359304 | tf_op jit(solution)/shard_map/ppermute | solution.py:469
  215.1 32.4 %all-to-all-start = ((bf16[16,128,256]{2,1,0:T(8,128)(2,1)}), bf16[16,128,256]{2,1,0:T(8,128)(2,1)}, u32[]{:S(2)}, u32[]{:S(2)}) async-start(bf16[16,128,256]{2,1,0:T(8,128)(2,1)} %bitcast.16), calls=%async_computation | async-start | bytes 2097152 | tf_op jit(solution)/shard_map/all_to_all | solution.py:637
  231.0 37.6 %collective-permute-start.16 = (bf16[512,1536]{1,0:T(8,128)(2,1)}, bf16[512,1536]{1,0:T(8,128)(2,1)}, u32[]{:S(2)}, u32[]{:S(2)}) collective-permute-start(bf16[512,1536]{1,0:T(8,128)(2,1)} %dynamic-slice_bitcast_fusion.5), channel_id=1, source_target_pairs={{0,1},{1,0},{2,3},{3,2},{4,5},{5,4},{6,7},{7,6},{8,9},{9,8},{10,11... | collective-permute-start | bytes 4718600 | tf_op jit(solution)/shard_map/ppermute | solution.py:465
  257.1 28.3 %collective-permute-start.18 = (bf16[256,1536]{1,0:T(8,128)(2,1)}, bf16[256,1536]{1,0:T(8,128)(2,1)}, u32[]{:S(2)}, u32[]{:S(2)}) collective-permute-start(bf16[256,1536]{1,0:T(8,128)(2,1)} %multiply_convert_fusion.7), channel_id=1, source_target_pairs={{0,1},{1,0},{2,3},{3,2},{4,5},{5,4},{6,7},{7,6},{8,9},{9,8},{10,11... | collective-permute-start | bytes 2359304 | tf_op jit(solution)/shard_map/ppermute | solution.py:465
  268.5 36.3 %collective-permute-start.17 = (bf16[512,1536]{1,0:T(8,128)(2,1)}, bf16[512,1536]{1,0:T(8,128)(2,1)}, u32[]{:S(2)}, u32[]{:S(2)}) collective-permute-start(bf16[512,1536]{1,0:T(8,128)(2,1)} %collective-permute-done.16), channel_id=1, source_target_pairs={{0,2},{2,0},{4,6},{6,4},{8,10},{10,8},{12,14},{14,12},{16,18},{18,... | collective-permute-start | bytes 4718600 | tf_op jit(solution)/shard_map/ppermute | solution.py:469
  269.8 46.1 %collective-permute-start.15 = (bf16[768,2048]{0,1:T(8,128)(2,1)}, bf16[768,2048]{0,1:T(8,128)(2,1)}, u32[]{:S(2)}, u32[]{:S(2)}) collective-permute-start(bf16[768,2048]{0,1:T(8,128)(2,1)} %collective-permute-done.14), channel_id=1, source_target_pairs={{0,2},{2,0},{4,6},{6,4},{8,10},{10,8},{12,14},{14,12},{16,18},{18,... | collective-permute-start | bytes 9437192 | tf_op jit(solution)/shard_map/ppermute | solution.py:469
  270.4 31.8 %collective-permute-start.19 = (bf16[256,1536]{1,0:T(8,128)(2,1)}, bf16[256,1536]{1,0:T(8,128)(2,1)}, u32[]{:S(2)}, u32[]{:S(2)}) collective-permute-start(bf16[256,1536]{1,0:T(8,128)(2,1)} %bitcast.44), channel_id=1, source_target_pairs={{0,1},{1,0},{2,3},{3,2},{4,5},{5,4},{6,7},{7,6},{8,9},{9,8},{10,11... | collective-permute-start | bytes 2359304 | tf_op jit(solution)/shard_map/ppermute | solution.py:465
  277.6 200.4 %collective-permute-start.32 = (bf16[256,1024]{1,0:T(8,128)(2,1)}, bf16[256,1024]{1,0:T(8,128)(2,1)}, u32[]{:S(2)}, u32[]{:S(2)}) collective-permute-start(bf16[256,1024]{1,0:T(8,128)(2,1)} %bitcast.352), channel_id=1, source_target_pairs={{0,1},{1,0},{2,3},{3,2},{4,5},{5,4},{6,7},{7,6},{8,9},{9,8},{10,11... | collective-permute-start | bytes 1572872 | tf_op jit(solution)/shard_map/ppermute | solution.py:465
  288.1 315.0 %collective-permute-start.42 = (bf16[512,1536]{1,0:T(8,128)(2,1)}, bf16[512,1536]{1,0:T(8,128)(2,1)}, u32[]{:S(2)}, u32[]{:S(2)}) collective-permute-start(bf16[512,1536]{1,0:T(8,128)(2,1)} %pad_maximum_fusion.10), channel_id=1, source_target_pairs={{0,2},{2,0},{4,6},{6,4},{8,10},{10,8},{12,14},{14,12},{16,18},{18,... | collective-permute-start | bytes 4718600 | tf_op jit(solution)/shard_map/ppermute | solution.py:469
  304.9 318.3 %collective-permute-start.51 = (bf16[512,1536]{1,0:T(8,128)(2,1)}, bf16[512,1536]{1,0:T(8,128)(2,1)}, u32[]{:S(2)}, u32[]{:S(2)}) collective-permute-start(bf16[512,1536]{1,0:T(8,128)(2,1)} %pad_maximum_fusion.11), channel_id=1, source_target_pairs={{0,2},{2,0},{4,6},{6,4},{8,10},{10,8},{12,14},{14,12},{16,18},{18,... | collective-permute-start | bytes 4718600 | tf_op jit(solution)/shard_map/ppermute | solution.py:469
  363.3 71.6 %collective-permute-start.20 = (bf16[256,1536]{1,0:T(8,128)(2,1)}, bf16[256,1536]{1,0:T(8,128)(2,1)}, u32[]{:S(2)}, u32[]{:S(2)}) collective-permute-start(bf16[256,1536]{1,0:T(8,128)(2,1)} %convolution_convert_fusion.6), channel_id=1, source_target_pairs={{0,1},{1,0},{2,3},{3,2},{4,5},{5,4},{6,7},{7,6},{8,9},{9,8},{10,11... | collective-permute-start | bytes 2359304 | tf_op jit(solution)/shard_map/ppermute | solution.py:465
  449.1 28.9 %collective-permute-start.31 = (bf16[256,1536]{1,0:T(8,128)(2,1)}, bf16[256,1536]{1,0:T(8,128)(2,1)}, u32[]{:S(2)}, u32[]{:S(2)}) collective-permute-start(bf16[256,1536]{1,0:T(8,128)(2,1)} %fusion.125), channel_id=1, source_target_pairs={{0,1},{1,0},{2,3},{3,2},{4,5},{5,4},{6,7},{7,6},{8,9},{9,8},{10,11... | collective-permute-start | bytes 2359304 | tf_op jit(solution)/shard_map/ppermute | solution.py:465
  451.4 44.2 %all-to-all-start.1 = ((bf16[16,128,256]{2,1,0:T(8,128)(2,1)}), bf16[16,128,256]{2,1,0:T(8,128)(2,1)S(1)}, u32[]{:S(2)}, u32[]{:S(2)}) async-start(bf16[16,128,256]{2,1,0:T(8,128)(2,1)} %bitcast.402), calls=%async_computation.1 | async-start | bytes 2097152 | tf_op jit(solution)/shard_map/all_to_all | solution.py:637
  474.1 20.4 %collective-permute-start.21 = (bf16[256,1536]{1,0:T(8,128)(2,1)S(1)}, bf16[256,1536]{1,0:T(8,128)(2,1)S(1)}, u32[]{:S(2)}, u32[]{:S(2)}) collective-permute-start(bf16[256,1536]{1,0:T(8,128)(2,1)S(1)} %convolution_convert_fusion.5), channel_id=1, source_target_pairs={{0,1},{1,0},{2,3},{3,2},{4,5},{5,4},{6,7},{7,6},{8,9},{9,8},{10,11... | collective-permute-start | bytes 2359304 | tf_op jit(solution)/shard_map/ppermute | solution.py:465
  478.0 114.9 %collective-permute-start.41 = (bf16[512,3,1024]{2,0,1:T(8,128)(2,1)}, bf16[512,3,1024]{2,0,1:T(8,128)(2,1)}, u32[]{:S(2)}, u32[]{:S(2)}) collective-permute-start(bf16[512,3,1024]{2,0,1:T(8,128)(2,1)} %bitcast.350), channel_id=1, source_target_pairs={{0,2},{2,0},{4,6},{6,4},{8,10},{10,8},{12,14},{14,12},{16,18},{18,... | collective-permute-start | bytes 9437192 | tf_op jit(solution)/shard_map/ppermute | solution.py:469
  478.0 152.8 %collective-permute-start.22 = (bf16[384,3072]{1,0:T(8,128)(2,1)}, bf16[384,3072]{1,0:T(8,128)(2,1)}, u32[]{:S(2)}, u32[]{:S(2)}) collective-permute-start(bf16[384,3072]{1,0:T(8,128)(2,1)} %bitcast.58), channel_id=1, source_target_pairs={{0,1},{1,0},{2,3},{3,2},{4,5},{5,4},{6,7},{7,6},{8,9},{9,8},{10,11... | collective-permute-start | bytes 7077896 | tf_op jit(solution)/shard_map/ppermute | solution.py:465
  521.9 22.7 %collective-permute-start.24 = (f32[2,1536]{1,0:T(2,128)S(1)}, f32[2,1536]{1,0:T(2,128)S(1)}, u32[]{:S(2)}, u32[]{:S(2)}) collective-permute-start(f32[2,1536]{1,0:T(2,128)S(1)} %pad_maximum_fusion.16), channel_id=1, source_target_pairs={{0,1},{1,0},{2,3},{3,2},{4,5},{5,4},{6,7},{7,6},{8,9},{9,8},{10,11... | collective-permute-start | bytes 36872 | tf_op jit(solution)/shard_map/ppermute | solution.py:465
  544.5 1.2 collective-permute-start.25
  545.8 3.8 collective-permute-start.26
  549.6 7.7 collective-permute-start.27
  551.0 257.9 %all-to-all-start.2 = ((bf16[16,128,384]{2,1,0:T(8,128)(2,1)}), bf16[16,128,384]{2,1,0:T(8,128)(2,1)}, u32[]{:S(2)}, u32[]{:S(2)}) async-start(bf16[16,128,384]{2,1,0:T(8,128)(2,1)} %bitcast.54), calls=%async_computation.2 | async-start | bytes 3145728 | tf_op jit(solution)/shard_map/all_to_all | solution.py:637
  557.3 35.0 %collective-permute-start.28 = (f32[2,1536]{1,0:T(2,128)S(1)}, f32[2,1536]{1,0:T(2,128)S(1)}, u32[]{:S(2)}, u32[]{:S(2)}) collective-permute-start(f32[2,1536]{1,0:T(2,128)S(1)} %add.472), channel_id=1, source_target_pairs={{0,16},{2,18},{4,20},{6,22},{8,24},{10,26},{12,28},{14,30},{16,0},... | collective-permute-start | bytes 36872 | tf_op jit(solution)/shard_map/ppermute | solution.py:469
  592.3 25.2 %collective-permute-start.33 = (bf16[8,96,1024]{2,1,0:T(8,128)(2,1)}, bf16[8,96,1024]{2,1,0:T(8,128)(2,1)}, u32[]{:S(2)}, u32[]{:S(2)}) collective-permute-start(bf16[8,96,1024]{2,1,0:T(8,128)(2,1)} %dynamic-slice_bitcast_fusion.4), channel_id=1, source_target_pairs={{0,2},{2,0},{4,6},{6,4},{8,10},{10,8},{12,14},{14,12},{16,18},{18,... | collective-permute-start | bytes 4718600 | tf_op jit(solution)/shard_map/ppermute | solution.py:469
  592.9 37.9 %collective-permute-start.29 = (bf16[192,1536]{1,0:T(8,128)(2,1)}, bf16[192,1536]{1,0:T(8,128)(2,1)}, u32[]{:S(2)}, u32[]{:S(2)}) collective-permute-start(bf16[192,1536]{1,0:T(8,128)(2,1)} %pad_maximum_fusion.15), channel_id=1, source_target_pairs={{0,2},{2,0},{4,6},{6,4},{8,10},{10,8},{12,14},{14,12},{16,18},{18,... | collective-permute-start | bytes 1769480 | tf_op jit(solution)/shard_map/ppermute | solution.py:469
  616.9 160.1 %collective-permute-start.43 = (bf16[2,4,128,1536]{3,2,1,0:T(8,128)(2,1)}, bf16[2,4,128,1536]{3,2,1,0:T(8,128)(2,1)}, u32[]{:S(2)}, u32[]{:S(2)}) collective-permute-start(bf16[2,4,128,1536]{3,2,1,0:T(8,128)(2,1)} %dynamic-slice_bitcast_fusion), channel_id=1, source_target_pairs={{0,4},{2,6},{4,0},{6,2},{8,12},{10,14},{12,8},{14,10},{16,20},{18,... | collective-permute-start | bytes 9437192 | tf_op jit(solution)/shard_map/ppermute | solution.py:469
  621.7 83.3 %collective-permute-start.34 = (bf16[4,96,1024]{2,1,0:T(8,128)(2,1)}, bf16[4,96,1024]{2,1,0:T(8,128)(2,1)}, u32[]{:S(2)}, u32[]{:S(2)}) collective-permute-start(bf16[4,96,1024]{2,1,0:T(8,128)(2,1)} %dynamic-slice_bitcast_fusion.9), channel_id=1, source_target_pairs={{0,4},{2,6},{4,0},{6,2},{8,12},{10,14},{12,8},{14,10},{16,20},{18,... | collective-permute-start | bytes 2359304 | tf_op jit(solution)/shard_map/ppermute | solution.py:469
  630.1 107.6 %collective-permute-start.52 = (bf16[4,192,1024]{2,1,0:T(8,128)(2,1)}, bf16[4,192,1024]{2,1,0:T(8,128)(2,1)}, u32[]{:S(2)}, u32[]{:S(2)}) collective-permute-start(bf16[4,192,1024]{2,1,0:T(8,128)(2,1)} %dynamic-slice_bitcast_fusion.3), channel_id=1, source_target_pairs={{0,4},{2,6},{4,0},{6,2},{8,12},{10,14},{12,8},{14,10},{16,20},{18,... | collective-permute-start | bytes 4718600 | tf_op jit(solution)/shard_map/ppermute | solution.py:469
  630.8 152.5 %collective-permute-start.23 = (bf16[384,3072]{1,0:T(8,128)(2,1)}, bf16[384,3072]{1,0:T(8,128)(2,1)}, u32[]{:S(2)}, u32[]{:S(2)}) collective-permute-start(bf16[384,3072]{1,0:T(8,128)(2,1)} %collective-permute-done.22), channel_id=1, source_target_pairs={{0,2},{2,0},{4,6},{6,4},{8,10},{10,8},{12,14},{14,12},{16,18},{18,... | collective-permute-start | bytes 7077896 | tf_op jit(solution)/shard_map/ppermute | solution.py:469
  706.5 8.4 collective-permute-start.35
  708.4 7.2 collective-permute-start.30
  714.9 3.6 collective-permute-start.38
  715.6 8.4 collective-permute-start.36
  724.1 20.7 %collective-permute-start.39 = (bf16[96,1024]{1,0:T(8,128)(2,1)S(1)}, bf16[96,1024]{1,0:T(8,128)(2,1)S(1)}, u32[]{:S(2)}, u32[]{:S(2)}) collective-permute-start(bf16[96,1024]{1,0:T(8,128)(2,1)S(1)} %get-tuple-element.93), channel_id=1, source_target_pairs={{16,8},{18,10},{20,12},{22,14},{24,16},{26,18},{28,20},{30,22},{17... | collective-permute-start | bytes 589832 | tf_op jit(solution)/shard_map/ppermute | solution.py:487
  739.9 14.8 %collective-permute-start.53 = (bf16[192,1024]{1,0:T(8,128)(2,1)S(1)}, bf16[192,1024]{1,0:T(8,128)(2,1)S(1)}, u32[]{:S(2)}, u32[]{:S(2)}) collective-permute-start(bf16[192,1024]{1,0:T(8,128)(2,1)S(1)} %get-tuple-element.76), channel_id=1, source_target_pairs={{0,8},{2,10},{4,12},{6,14},{1,9},{3,11},{5,13},{7,15}} | collective-permute-start | bytes 1179656 | tf_op jit(solution)/shard_map/ppermute | solution.py:482
  742.0 15.4 %collective-permute-start.37 = (bf16[96,1024]{1,0:T(8,128)(2,1)S(1)}, bf16[96,1024]{1,0:T(8,128)(2,1)S(1)}, u32[]{:S(2)}, u32[]{:S(2)}) collective-permute-start(bf16[96,1024]{1,0:T(8,128)(2,1)S(1)} %get-tuple-element.92), channel_id=1, source_target_pairs={{0,8},{2,10},{4,12},{6,14},{8,16},{10,18},{12,20},{14,22},{16,24},... | collective-permute-start | bytes 589832 | tf_op jit(solution)/shard_map/ppermute | solution.py:482
  744.9 15.1 %collective-permute-start.40 = (bf16[96,1024]{1,0:T(8,128)(2,1)S(1)}, bf16[96,1024]{1,0:T(8,128)(2,1)S(1)}, u32[]{:S(2)}, u32[]{:S(2)}) collective-permute-start(bf16[96,1024]{1,0:T(8,128)(2,1)S(1)} %fusion.96), channel_id=1, source_target_pairs={{8,0},{10,2},{12,4},{14,6},{16,8},{18,10},{20,12},{22,14},{24,16},... | collective-permute-start | bytes 589832 | tf_op jit(solution)/shard_map/ppermute | solution.py:487
  754.7 6.3 collective-permute-start.56
  757.4 11.5 %collective-permute-start.54 = (bf16[192,1024]{1,0:T(8,128)(2,1)S(1)}, bf16[192,1024]{1,0:T(8,128)(2,1)}, u32[]{:S(2)}, u32[]{:S(2)}) collective-permute-start(bf16[192,1024]{1,0:T(8,128)(2,1)S(1)} %fusion.89), channel_id=1, source_target_pairs={{0,8},{2,10},{4,12},{6,14},{8,16},{10,18},{12,20},{14,22},{1,9},{3... | collective-permute-start | bytes 1179656 | tf_op jit(solution)/shard_map/ppermute | solution.py:482
  771.1 56.0 %collective-permute-start.57 = (bf16[192,1024]{1,0:T(8,128)(2,1)}, bf16[192,1024]{1,0:T(8,128)(2,1)}, u32[]{:S(2)}, u32[]{:S(2)}) collective-permute-start(bf16[192,1024]{1,0:T(8,128)(2,1)} %get-tuple-element.75), channel_id=1, source_target_pairs={{16,8},{18,10},{20,12},{22,14},{24,16},{26,18},{28,20},{30,22},{17... | collective-permute-start | bytes 1179656 | tf_op jit(solution)/shard_map/ppermute | solution.py:487
  772.4 75.2 %collective-permute-start.55 = (bf16[192,1024]{1,0:T(8,128)(2,1)}, bf16[192,1024]{1,0:T(8,128)(2,1)}, u32[]{:S(2)}, u32[]{:S(2)}) collective-permute-start(bf16[192,1024]{1,0:T(8,128)(2,1)} %get-tuple-element.74), channel_id=1, source_target_pairs={{0,8},{2,10},{4,12},{6,14},{8,16},{10,18},{12,20},{14,22},{16,24},... | collective-permute-start | bytes 1179656 | tf_op jit(solution)/shard_map/ppermute | solution.py:482
  781.7 18.6 %collective-permute-start.44 = (bf16[2,128,1536]{2,1,0:T(8,128)(2,1)S(1)}, bf16[2,128,1536]{2,1,0:T(8,128)(2,1)S(1)}, u32[]{:S(2)}, u32[]{:S(2)}) collective-permute-start(bf16[2,128,1536]{2,1,0:T(8,128)(2,1)S(1)} %get-tuple-element.66), channel_id=1, source_target_pairs={{0,8},{2,10},{4,12},{6,14},{1,9},{3,11},{5,13},{7,15}} | collective-permute-start | bytes 2359304 | tf_op jit(solution)/shard_map/ppermute | solution.py:482
  786.0 25.6 %collective-permute-start.47 = (bf16[2,128,1536]{2,1,0:T(8,128)(2,1)}, bf16[2,128,1536]{2,1,0:T(8,128)(2,1)}, u32[]{:S(2)}, u32[]{:S(2)}) collective-permute-start(bf16[2,128,1536]{2,1,0:T(8,128)(2,1)} %get-tuple-element.67), channel_id=1, source_target_pairs={{24,16},{26,18},{28,20},{30,22},{25,17},{27,19},{29,21},{31,23}} | collective-permute-start | bytes 2359304 | tf_op jit(solution)/shard_map/ppermute | solution.py:487
  801.5 17.8 %collective-permute-start.45 = (bf16[2,128,1536]{2,1,0:T(8,128)(2,1)}, bf16[2,128,1536]{2,1,0:T(8,128)(2,1)}, u32[]{:S(2)}, u32[]{:S(2)}) collective-permute-start(bf16[2,128,1536]{2,1,0:T(8,128)(2,1)} %fusion.66), channel_id=1, source_target_pairs={{0,8},{2,10},{4,12},{6,14},{8,16},{10,18},{12,20},{14,22},{1,9},{3... | collective-permute-start | bytes 2359304 | tf_op jit(solution)/shard_map/ppermute | solution.py:482
  821.9 22.4 %collective-permute-start.48 = (bf16[2,128,1536]{2,1,0:T(8,128)(2,1)S(1)}, bf16[2,128,1536]{2,1,0:T(8,128)(2,1)S(1)}, u32[]{:S(2)}, u32[]{:S(2)}) collective-permute-start(bf16[2,128,1536]{2,1,0:T(8,128)(2,1)S(1)} %get-tuple-element.65), channel_id=1, source_target_pairs={{16,8},{18,10},{20,12},{22,14},{24,16},{26,18},{28,20},{30,22},{17... | collective-permute-start | bytes 2359304 | tf_op jit(solution)/shard_map/ppermute | solution.py:487
  828.2 24.4 %collective-permute-start.58 = (bf16[192,1024]{1,0:T(8,128)(2,1)S(1)}, bf16[192,1024]{1,0:T(8,128)(2,1)S(1)}, u32[]{:S(2)}, u32[]{:S(2)}) collective-permute-start(bf16[192,1024]{1,0:T(8,128)(2,1)S(1)} %fusion.88), channel_id=1, source_target_pairs={{8,0},{10,2},{12,4},{14,6},{16,8},{18,10},{20,12},{22,14},{24,16},... | collective-permute-start | bytes 1179656 | tf_op jit(solution)/shard_map/ppermute | solution.py:487
  830.2 29.2 %collective-permute-start.46 = (bf16[2,128,1536]{2,1,0:T(8,128)(2,1)}, bf16[2,128,1536]{2,1,0:T(8,128)(2,1)}, u32[]{:S(2)}, u32[]{:S(2)}) collective-permute-start(bf16[2,128,1536]{2,1,0:T(8,128)(2,1)} %get-tuple-element.64), channel_id=1, source_target_pairs={{0,8},{2,10},{4,12},{6,14},{8,16},{10,18},{12,20},{14,22},{16,24},... | collective-permute-start | bytes 2359304 | tf_op jit(solution)/shard_map/ppermute | solution.py:482
  845.3 18.4 %collective-permute-start.49 = (bf16[2,128,1536]{2,1,0:T(8,128)(2,1)}, bf16[2,128,1536]{2,1,0:T(8,128)(2,1)}, u32[]{:S(2)}, u32[]{:S(2)}) collective-permute-start(bf16[2,128,1536]{2,1,0:T(8,128)(2,1)} %fusion.65), channel_id=1, source_target_pairs={{8,0},{10,2},{12,4},{14,6},{16,8},{18,10},{20,12},{22,14},{24,16},... | collective-permute-start | bytes 2359304 | tf_op jit(solution)/shard_map/ppermute | solution.py:487
  856.2 1.5 collective-permute-start.59
  857.8 21.1 %collective-permute-start.60 = (bf16[96,2,2,2,128]{4,0,3,2,1:T(8,128)(2,1)S(1)}, bf16[96,2,2,2,128]{4,0,3,2,1:T(8,128)(2,1)}, u32[]{:S(2)}, u32[]{:S(2)}) collective-permute-start(bf16[96,2,2,2,128]{4,0,3,2,1:T(8,128)(2,1)S(1)} %bitcast.425), channel_id=1, source_target_pairs={{0,1},{1,0},{2,3},{3,2},{4,5},{5,4},{6,7},{7,6},{8,9},{9,8},{10,11... | collective-permute-start | bytes 589832 | tf_op jit(solution)/shard_map/ppermute | solution.py:465
  873.6 9.2 %collective-permute-start.50 = (bf16[2,128,768]{1,2,0:T(8,128)(2,1)S(1)}, bf16[2,128,768]{1,2,0:T(8,128)(2,1)S(1)}, u32[]{:S(2)}, u32[]{:S(2)}) collective-permute-start(bf16[2,128,768]{1,2,0:T(8,128)(2,1)S(1)} %bitcast.422), channel_id=1, source_target_pairs={{0,1},{1,0},{2,3},{3,2},{4,5},{5,4},{6,7},{7,6},{8,9},{9,8},{10,11... | collective-permute-start | bytes 1179656 | tf_op jit(solution)/shard_map/ppermute | solution.py:465
  (83 other events, 1130.7 us)

commit v2 on v1

--- a/solution.py
+++ b/solution.py
@@ -15,6 +15,7 @@
 LANES = 128
 HEAD_COLS = 4 * HD
 BF = jnp.bfloat16
+VMEM_LIMIT = 48 * 1024 * 1024
 
 
 EPSILON = 1e-05
@@ -379,7 +380,7 @@
                    jax.ShapeDtypeStruct((length,2*LANES),BF),
                    jax.ShapeDtypeStruct((steps,1,2*rows),jnp.float32)],
         scratch_shapes=[pltpu.VMEM((length,LANES),BF),pltpu.VMEM((LANES,length),BF)],
-        compiler_params=pltpu.CompilerParams(vmem_limit_bytes=48*1024*1024),
+        compiler_params=pltpu.CompilerParams(vmem_limit_bytes=VMEM_LIMIT),
     )(raw,cosine,sine)
 
 def backward_kernel(rows,step_rows,qkv_ref,out_ref,grad_ref,lse_ref,cos_ref,sin_ref,pick_ref,res_ref,
@@ -445,7 +446,7 @@
         out_shape=jax.ShapeDtypeStruct((length,4*HD),BF),
         scratch_shapes=[pltpu.VMEM((LANES,length),BF),pltpu.VMEM((length,LANES),jnp.float32),
                         pltpu.VMEM((length,LANES),jnp.float32),pltpu.VMEM((length,4*LANES),BF)],
-        compiler_params=pltpu.CompilerParams(vmem_limit_bytes=48*1024*1024),
+        compiler_params=pltpu.CompilerParams(vmem_limit_bytes=VMEM_LIMIT),
     )(qkv,out,grad,lse,cosine,sine,pick)
 
 def pad_columns():
@@ -498,25 +499,6 @@
 
 def after(value, earlier):
     return lax.optimization_barrier((value, earlier))[0]
-
-
-def plane_scatter(pieces, plane):
-    up = down = None
-    last = PLANES - 1
-    for step in range(last):
-        term_up = at(pieces, jnp.clip(plane + last - step, 0, last))
-        term_down = at(pieces, jnp.clip(plane - last + step, 0, last))
-        if up is not None:
-            term_up = (term_up.astype(jnp.float32) + up.astype(jnp.float32)).astype(BF)
-            term_down = (term_down.astype(jnp.float32) + down.astype(jnp.float32)).astype(BF)
-        up = plane_up(term_up, range(0, step + 1))
-        down = plane_down(term_down, range(last - step, last + 1))
-    own = at(pieces, plane).astype(jnp.float32)
-    return own + up.astype(jnp.float32) + down.astype(jnp.float32)
-
-
-def line_scatter(kept, sent):
-    return (kept.astype(jnp.float32) + swap_line(sent).astype(jnp.float32)).astype(BF)
 
 
 def rope_rows(length):
@@ -530,18 +512,476 @@
     return jnp.where(used, jnp.cos(angles), 0.0), jnp.where(used, jnp.sin(angles) * sign, 0.0)
 
 
-def mlp_part(normed, grad_rows, gate_up, down):
-    both = matmul(normed, gate_up)
-    half = both.shape[1] // 2
-    gate, upper = both[:, :half], both[:, half:]
+def take_kernel(info, gate_a, gate_b, up_a, up_b, out_ref):
+    @pl.when(info[1] == 0)
+    def _():
+        out_ref[:, :LANES] = gate_a[...]
+        out_ref[:, LANES:] = gate_b[...]
+
+    @pl.when(info[1] != 0)
+    def _():
+        out_ref[:, :LANES] = up_a[...]
+        out_ref[:, LANES:] = up_b[...]
+
+
+def take_columns(info, w_gate, w_up):
+    depth, hidden = w_gate.shape
+    part = depth // LINES
+    steps = hidden // (4 * LANES)
+
+    def spec(core, odd):
+        return pl.BlockSpec(
+            (part, LANES), lambda j, info: (info[2], jnp.where(info[1] == core, 4 * j + 2 * odd + 1 - info[0], 0))
+        )
+
+    return pl.pallas_call(
+        take_kernel,
+        grid_spec=pltpu.PrefetchScalarGridSpec(
+            num_scalar_prefetch=1,
+            grid=(steps,),
+            in_specs=[spec(0, 0), spec(0, 1), spec(1, 0), spec(1, 1)],
+            out_specs=pl.BlockSpec((part, 2 * LANES), lambda j, info: (0, j)),
+        ),
+        out_shape=jax.ShapeDtypeStruct((part, hidden // 2), BF),
+        compiler_params=pltpu.CompilerParams(vmem_limit_bytes=VMEM_LIMIT),
+        cost_estimate=pl.CostEstimate(flops=0, bytes_accessed=2 * depth * hidden, transcendentals=0),
+    )(info, w_gate, w_gate, w_up, w_up)
+
+
+def mlp_kernel(
+    info, normed, grad_rows, gate_a, gate_b, up_a, up_b, got, other, down_a, down_b, down_got, down_other,
+    inner_ref, grad_gate_ref, grad_up_ref, mixed_ref, back_ref,
+    gate_far, up_far, down, mixed_acc, back_acc,
+):
+    step = pl.program_id(0)
+    half_steps = pl.num_programs(0) // 2
+    side, core = info[0], info[1]
+    depth = gate_a.shape[0]
+    near = pl.ds(pl.multiple_of(side * depth, LANES), depth)
+    far = pl.ds(pl.multiple_of((1 - side) * depth, LANES), depth)
+
+    @pl.when(step == 0)
+    def _():
+        mixed_acc[...] = jnp.zeros_like(mixed_acc)
+        back_acc[...] = jnp.zeros_like(back_acc)
+
+    @pl.when(core == 0)
+    def _():
+        gate_far[...] = got[...]
+        up_far[...] = other[...]
+
+    @pl.when(core != 0)
+    def _():
+        gate_far[...] = other[...]
+        up_far[...] = got[...]
+
+    @pl.when(step < half_steps)
+    def _():
+        down[:LANES, :] = down_a[...]
+        down[LANES:, :] = down_b[...]
+
+    far_half = (step - half_steps) * 2 // half_steps
+
+    @pl.when((step >= half_steps) & (far_half == core))
+    def _():
+        down[...] = down_got[...]
+
+    @pl.when((step >= half_steps) & (far_half != core))
+    def _():
+        down[...] = down_other[...]
+
+    gate_near = jnp.concatenate([gate_a[...], gate_b[...]], axis=1)
+    up_near = jnp.concatenate([up_a[...], up_b[...]], axis=1)
+    gate = nn(normed[:, near], gate_near) + nn(normed[:, far], gate_far[...])
+    upper = nn(normed[:, near], up_near) + nn(normed[:, far], up_far[...])
     sigma = jax.nn.sigmoid(gate)
     active = gate * sigma
     inner = (active * upper).astype(BF)
-    grad_inner = times_transposed(grad_rows, down)
+    grad_inner = nt(grad_rows[...], down[...])
     grad_gate = (grad_inner * upper * sigma * (1.0 + gate * (1.0 - sigma))).astype(BF)
-    grad_upper = (grad_inner * active).astype(BF)
-    grad_both = jnp.concatenate([grad_gate, grad_upper], axis=1)
-    return inner, grad_both, matmul(inner, down), times_transposed(grad_both, gate_up)
+    grad_up = (grad_inner * active).astype(BF)
+    for which in range(CORES):
+        span = slice(which * LANES, (which + 1) * LANES)
+        inner_ref[which] = inner[:, span]
+        grad_gate_ref[which] = grad_gate[:, span]
+        grad_up_ref[which] = grad_up[:, span]
+    mixed_acc[...] += nn(inner, down[...])
+    back_acc[:, near] += nt(grad_gate, gate_near) + nt(grad_up, up_near)
+    back_acc[:, far] += nt(grad_gate, gate_far[...]) + nt(grad_up, up_far[...])
+
+    @pl.when(step == 2 * half_steps - 1)
+    def _():
+        mixed_ref[...] = mixed_acc[...].astype(mixed_ref.dtype)
+        back_ref[...] = back_acc[...].astype(back_ref.dtype)
+
+
+def mlp_part(info, normed, grad_rows, weights, kind):
+    w_gate, w_up, got, other, w_down, down_got, down_other = weights
+    rows, model = normed.shape
+    depth, hidden = w_gate.shape
+    half = hidden // 2
+    steps = half // (2 * LANES)
+    part = steps // 2
+
+    def pair_of(j, info):
+        return jnp.where(j < part, info[0] * part + j, (1 - info[0]) * part + j - part)
+
+    def whole(shape):
+        return pl.BlockSpec(shape, lambda j, info: (0, 0))
+
+    def column(odd):
+        return pl.BlockSpec((depth, LANES), lambda j, info: (0, 4 * pair_of(j, info) + 2 * odd + info[0]))
+
+    def row(odd):
+        return pl.BlockSpec((LANES, model), lambda j, info: (4 * jnp.minimum(j, part - 1) + 2 * odd + info[0], 0))
+
+    def far_row(which):
+        def block(j, info):
+            half_at = jnp.where(which == 0, info[1], 1 - info[1])
+            return (jnp.clip(j - part - half_at * (part // 2), 0, part // 2 - 1), 0)
+
+        return pl.BlockSpec((2 * LANES, model), block)
+
+    far = pl.BlockSpec((depth, 2 * LANES), lambda j, info: (0, pair_of(j, info)))
+
+    def place(j, info):
+        pair = pair_of(j, info)
+        return (0, 0, (pair % LINES) * PLANES + pair // LINES)
+
+    act = pl.BlockSpec((CORES, rows, LANES), place)
+    act_shape = jax.ShapeDtypeStruct((CORES, rows, half // CORES), BF)
+    return pl.pallas_call(
+        mlp_kernel,
+        grid_spec=pltpu.PrefetchScalarGridSpec(
+            num_scalar_prefetch=1,
+            grid=(steps,),
+            in_specs=[
+                whole((rows, model)), whole((rows, model)),
+                column(0), column(1), column(0), column(1), far, far,
+                row(0), row(1), far_row(0), far_row(1),
+            ],
+            out_specs=[act, act, act, whole((rows, model)), whole((rows, model))],
+            scratch_shapes=[
+                pltpu.VMEM((depth, 2 * LANES), BF),
+                pltpu.VMEM((depth, 2 * LANES), BF),
+                pltpu.VMEM((2 * LANES, model), BF),
+                pltpu.VMEM((rows, model), jnp.float32),
+                pltpu.VMEM((rows, model), jnp.float32),
+            ],
+        ),
+        out_shape=[act_shape, act_shape, act_shape] + [jax.ShapeDtypeStruct((rows, model), kind)] * 2,
+        compiler_params=pltpu.CompilerParams(vmem_limit_bytes=VMEM_LIMIT),
+        cost_estimate=pl.CostEstimate(
+            flops=12 * rows * model * half, bytes_accessed=6 * model * half, transcendentals=rows * half
+        ),
+    )(info, normed, grad_rows, w_gate, w_gate, w_up, w_up, got, other, w_down, w_down, down_got, down_other)
+
+
+def ctx_copy(source, target, sems, number, rank):
+    return pltpu.make_async_remote_copy(
+        src_ref=source,
+        dst_ref=target,
+        send_sem=sems.at[0, number],
+        recv_sem=sems.at[1, number],
+        device_id={"ctx": rank},
+        device_id_type=pl.DeviceIdType.MESH,
+    )
+
+
+def side_copy(source, target, sems, number, side):
+    return pltpu.make_async_remote_copy(
+        src_ref=source,
+        dst_ref=target,
+        send_sem=sems.at[0, number],
+        recv_sem=sems.at[1, number],
+        device_id={"fsdp": side},
+        device_id_type=pl.DeviceIdType.MESH,
+    )
+
+
+def greet(rank, side):
+    barrier = pltpu.get_barrier_semaphore()
+    for away in range(1, RANKS):
+        pl.semaphore_signal(
+            barrier,
+            inc=1,
+            device_id={"ctx": lax.rem(rank + away, RANKS)},
+            device_id_type=pl.DeviceIdType.MESH,
+        )
+    pl.semaphore_signal(barrier, inc=1, device_id={"fsdp": 1 - side}, device_id_type=pl.DeviceIdType.MESH)
+    pl.semaphore_wait(barrier, RANKS)
+
+
+def wide(value):
+    return value.astype(jnp.float32)
+
+
+def reduce_kernel(
+    rows_in, down_keep, down_got, gate_keep, gate_got, up_keep, up_sent, out_keep, out_sent, head_keep, head_sent, gains_in,
+    rows_out, down_mine, down_theirs, down_side, gate_mine, gate_side, up_mine, up_side, out_mine, head_out, gains_out,
+    up_got, out_got, down_acc, gate_acc, up_acc, out_acc, down_in, gate_in, up_in, out_in,
+    head_got, head_two, head_side, head_last, gain_buf, gain_in, exchange_sems, plane_sems, sems, local_sem,
+):
+    rank = lax.axis_index("ctx")
+    side = lax.axis_index("fsdp")
+    core = lax.rem(rank, CORES)
+    line = lax.rem(lax.div(rank, CORES), LINES)
+    plane = lax.div(rank, CORES * LINES)
+    step_rank = CORES * LINES
+    last = PLANES - 1
+    other_line = rank + CORES * (1 - 2 * line)
+    other_core = rank + 1 - 2 * core
+    greet(rank, side)
+
+    up_line = ctx_copy(up_sent, up_got, sems, 0, other_line)
+    out_line = ctx_copy(out_sent, out_got, sems, 1, other_line)
+    head_line = ctx_copy(head_sent, head_got, sems, 2, other_line)
+
+    weights = (
+        (down_keep, down_got, down_acc, down_in, 0),
+        (gate_keep, gate_got, gate_acc, gate_in, 1),
+        (up_keep, up_got, up_acc, up_in, 2),
+        (out_keep, out_got, out_acc, out_in, 3),
+    )
+
+    def message(weight, direction, step):
+        _, _, acc, landed, number = weight
+        slot = direction * last + step
+        target = rank + step_rank * (1 - 2 * direction)
+        return ctx_copy(acc.at[slot], landed.at[slot], plane_sems, number * 2 * last + slot, target)
+
+    def hop(weight, step):
+        keep, got, acc, landed, _ = weight
+        for direction in range(2):
+            depth = plane if direction == 0 else last - plane
+            piece = plane + (last - step) * (1 - 2 * direction)
+            slot = direction * last + step
+
+            if step:
+                @pl.when((depth >= 1) & (depth <= step))
+                def _():
+                    message(weight, direction, step - 1).wait_recv()
+
+                @pl.when((depth >= 1) & (depth <= step) & (depth < last))
+                def _():
+                    acc[slot] = (wide(keep[piece]) + wide(got[piece]) + wide(landed[slot - 1])).astype(BF)
+
+            @pl.when(depth == 0)
+            def _():
+                acc[slot] = (wide(keep[piece]) + wide(got[piece])).astype(BF)
+
+            @pl.when((depth <= step) & (depth < last))
+            def _():
+                message(weight, direction, step).start()
+
+    def finish(weight, result):
+        keep, got, _, landed, _ = weight
+        for direction in range(2):
+            depth = plane if direction == 0 else last - plane
+
+            @pl.when(depth >= 1)
+            def _():
+                message(weight, direction, last - 1).wait_recv()
+
+        base = wide(keep[plane]) + wide(got[plane])
+        above, below = landed.at[last - 1], landed.at[2 * last - 1]
+
+        @pl.when(plane == 0)
+        def _():
+            result[...] = (base + wide(below[...])).astype(BF)
+
+        @pl.when(plane == last)
+        def _():
+            result[...] = (base + wide(above[...])).astype(BF)
+
+        @pl.when((plane > 0) & (plane < last))
+        def _():
+            result[...] = (base + wide(above[...]) + wide(below[...])).astype(BF)
+
+    def sent(weight):
+        for step in range(last):
+            for direction in range(2):
+                depth = plane if direction == 0 else last - plane
+
+                @pl.when((depth <= step) & (depth < last))
+                def _():
+                    message(weight, direction, step).wait_send()
+
+    down, gate, up, out = weights
+    hop(down, 0)
+    hop(gate, 0)
+    up_line.start()
+    head_line.start()
+    copies = []
+    for away in range(1, RANKS):
+        to = lax.rem(rank + away, RANKS)
+        copy = ctx_copy(rows_in.at[to], rows_out.at[rank], exchange_sems, away, to)
+        copy.start()
+        copies.append(copy)
+    own = pltpu.make_async_copy(rows_in.at[rank], rows_out.at[rank], local_sem)
+    own.start()
+    out_line.start()
+
+    gain_partners = (None, other_core, other_line, rank + step_rank * (1 - 2 * lax.rem(plane, 2)),
+                     rank + 2 * step_rank * (1 - 2 * lax.div(plane, 2)))
+
+    def gain_copy(number):
+        if number == 0:
+            return side_copy(gain_buf.at[0], gain_in.at[0], sems, 3, 1 - side)
+        return ctx_copy(gain_buf.at[number], gain_in.at[number], sems, 3 + number, gain_partners[number])
+
+    def gain_hop(number):
+        if number:
+            gain_copy(number - 1).wait_recv()
+            gain_buf[number] = gain_buf[number - 1] + gain_in[number - 1]
+        else:
+            gain_buf[0] = gains_in[...]
+        if number < 5:
+            gain_copy(number).start()
+
+    gain_hop(0)
+    hop(down, 1)
+    hop(gate, 1)
+    gain_hop(1)
+
+    model = head_keep.shape[1]
+    half = model // 2
+    near = pl.ds(pl.multiple_of(side * half, LANES), half)
+    far = pl.ds(pl.multiple_of((1 - side) * half, LANES), half)
+    head_line.wait_recv()
+    head_two[...] = (head_keep[...] + wide(head_got[...])).astype(BF)
+    head_cross = side_copy(head_two.at[:, far], head_side, sems, 8, 1 - side)
+    head_cross.start()
+    gain_hop(2)
+
+    up_line.wait_recv()
+    out_line.wait_recv()
+    hop(up, 0)
+    hop(out, 0)
+    hop(down, 2)
+    hop(gate, 2)
+    gain_hop(3)
+    head_cross.wait_recv()
+    head_last[...] = (wide(head_two[:, near]) + wide(head_side[...])).astype(BF)
+    turned = rank - CORES * line - core + CORES * core + line
+    head_turn = ctx_copy(head_last, head_out, sems, 9, turned)
+
+    @pl.when(line != core)
+    def _():
+        head_turn.start()
+
+    @pl.when(line == core)
+    def _():
+        head_out[...] = head_last[...]
+
+    hop(up, 1)
+    hop(out, 1)
+    gain_hop(4)
+
+    finish(down, down_mine)
+    per_core = down_mine.shape[0] // CORES
+    theirs = pl.ds(pl.multiple_of((1 - core) * per_core, 16), per_core)
+    mine = pl.ds(pl.multiple_of(core * per_core, 16), per_core)
+    down_core = ctx_copy(down_mine.at[theirs], down_theirs, sems, 10, other_core)
+    down_core.start()
+    finish(gate, gate_mine)
+    gate_cross = side_copy(gate_mine.at[:, far], gate_side, sems, 11, 1 - side)
+    gate_cross.start()
+
+    hop(up, 2)
+    hop(out, 2)
+    gain_hop(5)
+    gains_out[...] = gain_buf[5]
+
+    down_core.wait_recv()
+    crosses = []
+    span = down_mine.shape[1] // 4
+    for which in range(2):
+        block = down_mine.at[mine] if which == 0 else down_theirs
+        for at_line in range(LINES):
+            lanes = pl.ds(pl.multiple_of(at_line * 2 * span + (1 - side) * span, LANES), span)
+            cross = side_copy(block.at[:, lanes], down_side.at[which, at_line], sems, 13 + which * LINES + at_line, 1 - side)
+            cross.start()
+            crosses.append(cross)
+
+    finish(up, up_mine)
+    up_cross = side_copy(up_mine.at[:, far], up_side, sems, 12, 1 - side)
+    up_cross.start()
+    finish(out, out_mine)
+
+    @pl.when(line != core)
+    def _():
+        head_turn.wait()
+
+    for copy in copies:
+        copy.wait()
+    own.wait()
+    for cross in crosses + [gate_cross, up_cross]:
+        cross.wait()
+    for copy in (up_line, out_line, head_line, head_cross, down_core):
+        copy.wait_send()
+    for number in range(5):
+        gain_copy(number).wait_send()
+    for weight in weights:
+        sent(weight)
+
+
+def reduce_all(rows_in, down, gate, up, out, head, gains):
+    (down_keep, down_got), (gate_keep, gate_got), (up_keep, up_sent), (out_keep, out_sent) = down, gate, up, out
+    head_keep, head_sent = head
+    hops = 2 * (PLANES - 1)
+    vmem = pl.BlockSpec(memory_space=pltpu.VMEM)
+    hbm = pl.BlockSpec(memory_space=pl.ANY)
+
+    def piece(keep):
+        return keep.shape[1:]
+
+    def half_lanes(keep):
+        return (keep.shape[1], keep.shape[2] // 2)
+
+    def shape(dims, kind=BF):
+        return jax.ShapeDtypeStruct(dims, kind)
+
+    down_rows, down_cols = piece(down_keep)
+    keeps = (down_keep, gate_keep, up_keep, out_keep)
+    return pl.pallas_call(
+        reduce_kernel,
+        in_specs=[hbm] + [vmem] * 5 + [hbm, vmem, hbm, vmem, hbm, vmem],
+        out_specs=[hbm] + [vmem] * 10,
+        out_shape=[
+            shape(rows_in.shape),
+            shape((down_rows, down_cols)),
+            shape((down_rows // CORES, down_cols)),
+            shape((2, LINES, down_rows // CORES, down_cols // 4)),
+            shape(piece(gate_keep)),
+            shape(half_lanes(gate_keep)),
+            shape(piece(up_keep)),
+            shape(half_lanes(up_keep)),
+            shape(piece(out_keep)),
+            shape((head_keep.shape[0], head_keep.shape[1] // 2)),
+            shape(gains.shape, jnp.float32),
+        ],
+        scratch_shapes=[pltpu.VMEM(up_keep.shape, BF), pltpu.VMEM(out_keep.shape, BF)]
+        + [pltpu.VMEM((hops,) + piece(keep), BF) for keep in keeps]
+        + [pltpu.VMEM((hops,) + piece(keep), BF) for keep in keeps]
+        + [
+            pltpu.VMEM(head_keep.shape, BF),
+            pltpu.VMEM(head_keep.shape, BF),
+            pltpu.VMEM((head_keep.shape[0], head_keep.shape[1] // 2), BF),
+            pltpu.VMEM((head_keep.shape[0], head_keep.shape[1] // 2), BF),
+            pltpu.VMEM((6,) + gains.shape, jnp.float32),
+            pltpu.VMEM((5,) + gains.shape, jnp.float32),
+            pltpu.SemaphoreType.DMA((2, RANKS)),
+            pltpu.SemaphoreType.DMA((2, 4 * hops)),
+            pltpu.SemaphoreType.DMA((2, 17)),
+            pltpu.SemaphoreType.DMA,
+        ],
+        compiler_params=pltpu.CompilerParams(
+            collective_id=0, has_side_effects=True, vmem_limit_bytes=VMEM_LIMIT
+        ),
+    )(
+        rows_in, down_keep, down_got, gate_keep, gate_got, up_keep, up_sent, out_keep, out_sent, head_keep, head_sent, gains
+    )
 
 
 def head_shards(
@@ -553,152 +993,131 @@
     half_model = model // 2
     hidden = w_gate.shape[1]
     half_hidden = hidden // 2
+    part_hidden = half_hidden // CORES
     chunk = hidden // (2 * RANKS)
     rank = lax.axis_index("ctx")
     side = lax.axis_index("fsdp")
     core = rank % CORES
     line = (rank // CORES) % LINES
     plane = rank // (CORES * LINES)
-    chip = rank // CORES
+    head = plane * CORES + core
+    low_side = side == 0
+    info = jnp.stack([side, core, line]).astype(jnp.int32)
     pick = jnp.asarray((pad_columns()[:, None] == np.arange(HEAD_COLS)[None, :]).astype(np.float32)).astype(BF)
-    cosine, sine = rope_rows(length)
-
-    mine = at(tokens, core)
-    own_block = in_order(core, mine, swap_core(at(tokens, 1 - core)))
-    ups, downs = [], []
-    up = down = own_block
-    for step in range(PLANES - 1):
-        up = plane_up(up, range(step, PLANES - 1))
-        down = plane_down(down, range(1, PLANES - step))
-        ups.append(up)
-        downs.append(down)
+
+    near = at(tokens, line)
+    across = swap_line(at(tokens, 1 - line))
     low = plane < PLANES // 2
-    slots = [
-        own_block,
-        jnp.where(low, downs[0], ups[0]),
-        jnp.where(low, downs[1], ups[1]),
-        jnp.where(plane == 0, downs[2], jnp.where(plane == 1, ups[0], jnp.where(plane == 2, downs[0], ups[2]))),
-    ]
-
-    packed = jnp.concatenate(
-        [w_query.reshape(half_model, HK, -1), w_key.reshape(half_model, HK, -1), w_value.reshape(half_model, HK, -1)],
-        axis=2,
-    )
-    head_rows = at(packed, chip, 1)
+    streams = []
+    for start in (near, across):
+        ups, downs = [], []
+        up = down = start
+        for step in range(PLANES - 1):
+            up = plane_up(up, range(step, PLANES - 1))
+            down = plane_down(down, range(1, PLANES - step))
+            ups.append(up)
+            downs.append(down)
+        streams.append([
+            start,
+            jnp.where(low, downs[0], ups[0]),
+            jnp.where(low, downs[1], ups[1]),
+            jnp.where(plane == 0, downs[2], jnp.where(plane == 1, ups[0], jnp.where(plane == 2, downs[0], ups[2]))),
+        ])
+
+    def head_slice(weight, size):
+        return lax.dynamic_slice_in_dim(weight, head * size, size, 1)
+
+    head_rows = jnp.concatenate(
+        [head_slice(w_query, 2 * HD), head_slice(w_key, HD), head_slice(w_value, HD)], axis=1
+    )
     head_got = swap_fsdp(head_rows)
     head_weight = in_order(side, head_rows, head_got)
     head_padded = times_transposed(head_weight, pick).astype(BF)
-
-    def fetch(block, earlier):
-        part = at(block.reshape((CORES, block.shape[0] // CORES) + block.shape[1:]), core)
-        got = swap_fsdp(after(part, earlier))
-        return in_order(core, got, swap_core(got)), got
-
-    out_other, done = fetch(w_out, head_got)
-    out_full = in_order(side, w_out, out_other)
-    out_padded = jnp.pad(out_full.reshape(HQ, HD, model), ((0, 0), (0, LANES - HD), (0, 0))).reshape(HQ * LANES, model)
-
-    def columns_of(block, which):
-        cut = block.reshape(half_model, PLANES, LINES, CORES, 2, chunk)
-        return at(cut, which, 4).transpose(0, 3, 2, 1, 4).reshape(half_model, half_hidden)
-
-    first = core == 0
-    sent = jnp.where(first, columns_of(w_gate, 1 - side), columns_of(w_up, 1 - side))
-    got = swap_fsdp(after(sent, done))
-    other = swap_core(got)
-    gate_up = in_order(
-        side,
-        jnp.concatenate([columns_of(w_gate, side), columns_of(w_up, side)], axis=1),
-        jnp.concatenate([jnp.where(first, got, other), jnp.where(first, other, got)], axis=1),
-    )
-    down_cut = w_down.reshape(PLANES // 2, LINES, CORES, 2, chunk, model)
-    down_other, done = fetch(at(down_cut, 1 - side, 3).reshape(-1, model), got)
-    down_rows = in_order(side, at(down_cut, side, 3).reshape(-1, model), down_other)
-    down_weight = (
-        down_rows.reshape(PLANES, LINES, CORES, chunk, model).transpose(2, 1, 0, 3, 4).reshape(half_hidden, model)
-    )
+    cosine, sine = rope_rows(length)
+
+    def fetch(part, earlier):
+        crossed = swap_fsdp(after(part, earlier))
+        got = in_order(line, crossed, swap_line(crossed))
+        return got, swap_core(got), crossed
+
+    def quarter(block):
+        return at(block.reshape((CORES * LINES, block.shape[0] // 4) + block.shape[1:]), 2 * core + line)
+
+    out_got, out_other, crossed = fetch(quarter(w_out), head_got)
+    gate_got, gate_other, crossed = fetch(take_columns(info, w_gate, w_up), crossed)
+    cut = w_down.reshape(CORES * LINES, -1, 2, chunk, model)
+    down_got, down_other, crossed = fetch(at(at(cut, 2 * core + line), 1 - side, 1).reshape(-1, model), crossed)
+    weights = (w_gate, w_up, gate_got, gate_other, w_down, down_got, down_other)
     grad_down = cotangent.reshape(rows, model)
-    grad_down_other = swap_fsdp(after(grad_down, done))
-
-    normed_seq = jnp.zeros((CHIPS, 2 * width, model), BF)
-    raw_seq = jnp.zeros((CHIPS, 2 * width, 4 * LANES), jnp.float32)
-    for number, piece in enumerate(slots):
+
+    normed_seq = jnp.zeros((PLANES, CHIPS // PLANES * 2 * width, model), BF)
+    raw_seq = jnp.zeros((PLANES, CHIPS // PLANES * 2 * width, 4 * LANES), jnp.float32)
+    for number in range(PLANES):
         place = jnp.where(low, plane + number, plane - number) % PLANES
-        for across in range(LINES):
-            block = swap_line(piece) if across else piece
-            spot = place * LINES + (line if across == 0 else 1 - line)
-            normed = (normalize(block.astype(jnp.float32))[0] * attn_gain).astype(BF)
-            normed_seq = lax.dynamic_update_index_in_dim(normed_seq, normed, spot, 0)
-            raw_seq = lax.dynamic_update_index_in_dim(raw_seq, matmul(normed, head_padded), spot, 0)
+        both = jnp.stack([streams[0][number], streams[1][number]])
+        theirs = swap_core(both)
+        block = jnp.stack(
+            [
+                jnp.where(core == 0, both, theirs),
+                jnp.where(core == 0, theirs, both),
+            ],
+            axis=1,
+        )
+        block = jnp.where(line == 0, block, block[::-1]).reshape(-1, model)
+        normed = (normalize(block.astype(jnp.float32))[0] * attn_gain).astype(BF)
+        normed_seq = lax.dynamic_update_index_in_dim(normed_seq, normed, place, 0)
+        raw_seq = lax.dynamic_update_index_in_dim(raw_seq, matmul(normed, head_padded), place, 0)
     normed_seq = normed_seq.reshape(length, model)
     qkv, attended_seq, lse = head_forward(raw_seq.reshape(length, 4 * LANES), cosine, sine)
 
     def exchange(value):
         return lax.all_to_all(value.reshape(RANKS, width, -1), "ctx", 0, 0, tiled=True)
 
-    attended = (
-        exchange(attended_seq).reshape(CHIPS, CORES, width, 2 * LANES).transpose(1, 2, 0, 3).reshape(rows, HQ * LANES)
-    )
+    def by_token(value):
+        cut = value.reshape(PLANES, LINES, CORES, width, value.shape[-1])
+        return cut.transpose(1, 3, 0, 2, 4).reshape(rows, HK * value.shape[-1])
+
+    attended = by_token(exchange(attended_seq))
+    out_far = in_order(core, out_got, out_other)
+    out_full = in_order(side, w_out, out_far)
+    out_padded = jnp.pad(out_full.reshape(HQ, HD, model), ((0, 0), (0, LANES - HD), (0, 0))).reshape(HQ * LANES, model)
     inputs = tokens.reshape(rows, model).astype(jnp.float32)
     resid = inputs + matmul(attended, out_padded)
     unit_two, inv_two = normalize(resid)
     normed_two = (unit_two * mlp_gain).astype(BF)
 
-    normed_other = swap_fsdp(normed_two)
-    inner_own, grad_both_own, mixed_own, back_own = mlp_part(normed_two, grad_down, gate_up, down_weight)
-    inner_other, grad_both_other, mixed_other, back_other = mlp_part(
-        normed_other, grad_down_other, gate_up, down_weight
-    )
-    back_got = swap_fsdp(back_other.astype(BF))
-    mixed_got = swap_fsdp(after(mixed_other.astype(BF), back_got))
+    normed_other, grad_down_other = swap_fsdp((normed_two, after(grad_down, crossed)))
+    inner_own, gate_own, up_own, mixed_own, back_own = mlp_part(info, normed_two, grad_down, weights, jnp.float32)
+    normed_other, grad_down_other = after((normed_other, grad_down_other), mixed_own)
+    inner_far, gate_far, up_far, mixed_far, back_far = mlp_part(info, normed_other, grad_down_other, weights, BF)
+    back_got = swap_fsdp(back_far)
+    mixed_got = swap_fsdp(after(mixed_far, back_got))
+
+    normed_pair = jnp.concatenate([normed_two, normed_other], axis=0)
+    normed_sib = swap_core(normed_pair)
+    cot_pair = jnp.concatenate([grad_down, grad_down_other], axis=0)
+    cot_sib = swap_core(cot_pair)
+
+    def pair_acts(own, far):
+        pair = jnp.concatenate([own, far], axis=1)
+        return at(pair, core), swap_core(at(pair, 1 - core))
+
+    inner_pair, inner_sib = pair_acts(inner_own, inner_far)
+    grad_down_weight = (transposed_times(cot_pair, inner_pair) + transposed_times(cot_sib, inner_sib)).astype(BF)
+    gate_pair, gate_sib = pair_acts(gate_own, gate_far)
+    grad_gate_weight = (transposed_times(gate_pair, normed_pair) + transposed_times(gate_sib, normed_sib)).astype(BF)
+    up_pair, up_sib = pair_acts(up_own, up_far)
+    grad_up_weight = (transposed_times(up_pair, normed_pair) + transposed_times(up_sib, normed_sib)).astype(BF)
+
     mixed = (resid + mixed_own + mixed_got.astype(jnp.float32)).astype(BF)
+    back_got = after(back_got, (grad_down_weight, grad_gate_weight, grad_up_weight))
     grad_normed_two = back_own + back_got.astype(jnp.float32)
     grad_resid = grad_down.astype(jnp.float32) + norm_back(grad_normed_two, mlp_gain, unit_two, inv_two)
     mlp_gain_part = jnp.sum(grad_normed_two * unit_two, axis=0)
     grad_branch = grad_resid.astype(BF)
     grad_attended = times_transposed(grad_branch, out_padded).astype(BF)
-    grad_att_seq = exchange(grad_attended.reshape(CORES, width, CHIPS, 2 * LANES).transpose(2, 0, 1, 3)).reshape(
-        length, 2 * LANES
-    )
-
-    acts = jnp.concatenate(
-        [
-            jnp.concatenate([inner_own, grad_both_own], axis=1),
-            jnp.concatenate([inner_other, grad_both_other], axis=1),
-        ],
-        axis=0,
-    ).reshape(2 * rows, 3, CORES, half_hidden // CORES)
-    acts_got = swap_core(at(acts, 1 - core, 2))
-    acts_all = jnp.concatenate([at(acts, core, 2), acts_got], axis=0)
-    normed_pair = jnp.concatenate([normed_two, normed_other], axis=0)
-    normed_all = jnp.concatenate([normed_pair, swap_core(normed_pair)], axis=0)
-    cot_pair = jnp.concatenate([grad_down, grad_down_other], axis=0)
-    cot_all = jnp.concatenate([cot_pair, swap_core(cot_pair)], axis=0)
-    part_hidden = half_hidden // CORES
-    grad_down_weight = transposed_times(cot_all, acts_all[:, 0]).astype(BF)
-    grad_gate_up = transposed_times(acts_all[:, 1:].reshape(-1, 2 * part_hidden), normed_all).astype(BF)
-
-    per_chip = model // CHIPS
-    cut = grad_down_weight.reshape(PLANES, LINES, per_chip, part_hidden)
-    reduced = plane_scatter(line_scatter(at(cut, line, 1), at(cut, 1 - line, 1)), plane)
-    cut = grad_gate_up.reshape(2, LINES, PLANES, chunk, model)
-    halves = line_scatter(at(cut, line, 1), at(cut, 1 - line, 1))
-    gate_up_reduced = plane_scatter(halves.transpose(1, 0, 2, 3), plane).astype(BF)
-    cut = gate_up_reduced.reshape(2, chunk, 2, half_model)
-    gate_up_got = swap_fsdp(at(cut, 1 - side, 2))
-    gate_up_keep = at(cut, side, 2)
-    low_side = side == 0
-    gate_up_grad = jnp.concatenate(
-        [jnp.where(low_side, gate_up_keep, gate_up_got), jnp.where(low_side, gate_up_got, gate_up_keep)], axis=1
-    ).astype(jnp.float32)
-    w_gate_grad, w_up_grad = gate_up_grad[0].T, gate_up_grad[1].T
-
-    cut = reduced.astype(BF).reshape(CORES, model // RANKS, LINES, 2, PLANES // 2, chunk)
-    keep, got = at(cut, core), swap_core(at(cut, 1 - core))
-    by_core = jnp.stack([jnp.where(first, keep, got), jnp.where(first, got, keep)], axis=3)
-    keep, got = at(by_core, side, 2), swap_fsdp(at(by_core, 1 - side, 2))
-    by_side = jnp.stack([jnp.where(low_side, keep, got), jnp.where(low_side, got, keep)], axis=4)
-    w_down_grad = by_side.transpose(0, 3, 1, 2, 4, 5).reshape(model // RANKS, -1).T.astype(jnp.float32)
+    cut = grad_attended.reshape(LINES, width, PLANES, CORES, 2 * LANES)
+    grad_att_seq = exchange(cut.transpose(2, 0, 3, 1, 4)).reshape(length, 2 * LANES)
 
     att_cut = attended.reshape(rows, 2, HK * LANES)
     att_other, branch_other = swap_fsdp((at(att_cut, 1 - side, 1), grad_branch))
@@ -706,36 +1125,69 @@
     branch_pair = jnp.concatenate([grad_branch, branch_other], axis=0)
     cut = transposed_times(branch_pair, att_pair).astype(BF).reshape(CHIPS, CORES, model // RANKS, HK * LANES)
     got = swap_core(at(cut, 1 - core, 1))
-    pair_sum = (at(cut, core, 1).astype(jnp.float32) + got.astype(jnp.float32)).astype(BF)
-    cut = pair_sum.reshape(PLANES, LINES, model // RANKS, HK * LANES)
-    reduced = plane_scatter(line_scatter(at(cut, line, 1), at(cut, 1 - line, 1)), plane)
-    w_out_grad = reduced.reshape(model // RANKS, HK, LANES)[:, :, :HD].reshape(model // RANKS, half_model).T
+    out_pair = (at(cut, core, 1).astype(jnp.float32) + got.astype(jnp.float32)).astype(BF)
+
+    per_chip = model // CHIPS
+    down_cut = grad_down_weight.reshape(PLANES, LINES, per_chip, part_hidden)
+    gate_cut = grad_gate_weight.reshape(LINES, PLANES, chunk, model)
+    up_cut = grad_up_weight.reshape(LINES, PLANES, chunk, model)
+    out_cut = out_pair.reshape(PLANES, LINES, model // RANKS, HK * LANES)
+    down_got = swap_line(at(down_cut, 1 - line, 1))
+    gate_got = swap_line(at(gate_cut, 1 - line))
 
     grad_qkv = head_backward(qkv, attended_seq, grad_att_seq, lse, cosine, sine, pick)
-    grad_own = exchange(grad_qkv).reshape(CHIPS, CORES, width, HEAD_COLS).transpose(1, 2, 0, 3).reshape(rows, -1)
-
     head_grad = transposed_times(grad_qkv, normed_seq)
     gain_part = jnp.sum(head_grad * head_weight.T.astype(jnp.float32), axis=0) / attn_gain
-    query_cut = head_grad[: 2 * HD].reshape(CORES, HD, model)
-    key_cut = head_grad[2 * HD :].reshape(2, CORES, HD // 2, model)
-
-    def of_core(which):
+    query_cut = head_grad[: 2 * HD].reshape(2, HD, model)
+    key_cut = head_grad[2 * HD :].reshape(2, 2, HD // 2, model)
+
+    def half_columns(which):
         return jnp.concatenate([at(query_cut, which), at(key_cut, which, 1).reshape(HD, model)], axis=0)
 
-    two = of_core(core) + swap_core(of_core(1 - core).astype(BF)).astype(jnp.float32)
-    cut = two.reshape(2 * HD, 2, half_model)
-    four = at(cut, side, 1) + swap_fsdp(at(cut, 1 - side, 1).astype(BF)).astype(jnp.float32)
-    w_query_grad = four[:HD].T
-    w_key_grad = four[HD : HD + HD // 2].T
-    w_value_grad = four[HD + HD // 2 :].T
-
-    gains = jnp.stack([gain_part, mlp_gain_part])
-    gains = gains + swap_fsdp(gains)
-    for bit in (1, 2, 4, 8):
-        gains = gains + swap_ctx(gains, bit)
-
-    packed_other, _ = fetch(packed.reshape(half_model, HK * HEAD_COLS), back_got)
-    packed_full = in_order(side, packed.reshape(half_model, HK * HEAD_COLS), packed_other)
+    gains = jnp.concatenate([jnp.stack([gain_part, mlp_gain_part]), jnp.zeros((6, model), jnp.float32)], axis=0)
+    (
+        grad_rows, down_mine, down_theirs, down_side, gate_mine, gate_side, up_mine, up_side, out_mine, head_mine, gains
+    ) = reduce_all(
+        grad_qkv.reshape(RANKS, width, HEAD_COLS),
+        (at(down_cut, line, 1), after(down_got, grad_qkv)),
+        (at(gate_cut, line), after(gate_got, grad_qkv)),
+        (at(up_cut, line), at(up_cut, 1 - line)),
+        (at(out_cut, line, 1), at(out_cut, 1 - line, 1)),
+        (half_columns(line), half_columns(1 - line).astype(BF)),
+        gains,
+    )
+    grad_own = by_token(grad_rows)
+
+    def by_columns(mine, theirs):
+        cut = mine.reshape(chunk, 2, half_model)
+        return in_order(side, at(cut, side, 1), theirs).astype(jnp.float32).T
+
+    w_gate_grad = by_columns(gate_mine, gate_side)
+    w_up_grad = by_columns(up_mine, up_side)
+    shape = (model // RANKS, LINES, 2, PLANES // 2, chunk)
+    parts = [at(down_mine.reshape((CORES,) + shape), core), down_theirs.reshape(shape)]
+    kept = [at(part, side, 2) for part in parts]
+    sided = [down_side[i].reshape(LINES, model // RANKS, PLANES // 2, chunk).transpose(1, 0, 2, 3) for i in range(2)]
+    by_side = [
+        jnp.stack([jnp.where(low_side, k, g), jnp.where(low_side, g, k)], axis=3) for k, g in zip(kept, sided)
+    ]
+    first = core == 0
+    by_core = jnp.stack(
+        [jnp.where(first, by_side[0], by_side[1]), jnp.where(first, by_side[1], by_side[0])], axis=3
+    )
+    w_down_grad = by_core.transpose(0, 2, 1, 3, 4, 5).reshape(model // RANKS, -1).T.astype(jnp.float32)
+    w_out_grad = (
+        out_mine.reshape(model // RANKS, HK, LANES)[:, :, :HD].reshape(model // RANKS, half_model).T.astype(jnp.float32)
+    )
+    head_mine = head_mine.astype(jnp.float32)
+    w_query_grad = head_mine[:HD].T
+    w_key_grad = head_mine[HD : HD + HD // 2].T
+    w_value_grad = head_mine[HD + HD // 2 :].T
+
+    late = after((w_query, w_key, w_value), attended_seq)
+    packed = jnp.concatenate([part.reshape(half_model, HK, -1) for part in late], axis=2).reshape(half_model, -1)
+    packed_got, packed_other, _ = fetch(quarter(packed), mixed_got)
+    packed_full = in_order(side, packed, in_order(core, packed_got, packed_other))
     grad_normed_one = times_transposed(grad_own, packed_full)
     unit_one, inv_one = normalize(inputs)
     tokens_grad = (grad_resid + norm_back(grad_normed_one, attn_gain, unit_one, inv_one)).astype(BF)

time: 894 us -> 667 us (0.75)
  waiting for transfers between devices: 320 us -> 121 us
  Pallas kernels: 32.5 us -> 228 us
  other arithmetic: 144 us -> 66.3 us
  local copies, waits for them, and re-layouts: 189 us -> 119 us
  matrix products: 94.3 us -> 50.3 us
  starting transfers between devices: 102 us -> 70.5 us
    pallas_call x0 -> x4, Pallas kernels: none -> 197 us  [the longest x1 150 us: reduce_all(): pl.pallas_call(reduce_kernel, in_specs=[hbm] + [vmem] * 5 + [hbm, vmem, h...]
    ppermute x22 -> x21, waiting for transfers between devices: 148 us -> 44.6 us  [swap_ctx(): return lax.ppermute(value, 'ctx', [(i, i ^ bit) for i in range(RANKS)])]
    unnamed x183 -> x107, local copies, waits for them, and re-layouts: 66.8 us -> 12 us
    ppermute x12 -> x6, waiting for transfers between devices: 45.9 us -> 0.76 us  [plane_up(): lax.ppermute(value, 'ctx', [(z * step + i, z * step + step + i) for z in...]
    concatenate x4 -> x5, other arithmetic: 47.7 us -> 3.42 us  [the longest x1 2.37 us: head_shards(): jnp.concatenate([part.reshape(half_model, HK, -1) for part in late], axis=2)]
    ppermute x12 -> x6, waiting for transfers between devices: 51 us -> 14.3 us  [plane_down(): lax.ppermute(value, 'ctx', [(z * step + i, z * step - step + i) for z in...]
    dot_general x7 -> x3, matrix products: 36.7 us -> 9.84 us  [times_transposed(): lax.dot_general(left, right, (((1,), (1,)), ((), ())), preferred_element_...]
    dot_general x13 -> x5, matrix products: 33.5 us -> 9.04 us  [matmul(): return jnp.dot(left, right, preferred_element_type=jnp.float32)]
  transfers between devices with their start and end apart: 64 -> 46, of which waited for: 28 -> 13; matrix products, arithmetic and copies ran while one was open for 45% -> 31% of each run, Pallas kernels for 4% -> 32%
where the time goes in v2:
time: 667 us; the launch traced here: 656 us
  Pallas kernels  228 us (34%)
  waiting for transfers between devices  121 us (18%)
  local copies, waits for them, and re-layouts  119 us (18%)
  starting transfers between devices  70.5 us (11%)
  other arithmetic  66.3 us (10%)
  matrix products  50.3 us (8%)
    pallas_call x1, Pallas kernels, reduce_all(): pl.pallas_call(reduce_kernel, in_specs=[hbm] + [vmem] * 5 + [hbm, vmem, h...  150 us
    ppermute x11, waiting for transfers between devices, swap_fsdp(): return lax.ppermute(value, 'fsdp', [(0, 1), (1, 0)])  61 us
    ppermute x21, waiting for transfers between devices, swap_ctx(): return lax.ppermute(value, 'ctx', [(i, i ^ bit) for i in range(RANKS)])  44.6 us
    pallas_call x2, Pallas kernels, mlp_part(): pl.pallas_call(mlp_kernel, grid_spec=pltpu.PrefetchScalarGridSpec(num_sca...  40.2 us
    dot_general x8, matrix products, transposed_times(): lax.dot_general(left, right, (((0,), (0,)), ((), ())), preferred_element_...  31.4 us
    pallas_call x1, Pallas kernels, head_backward(): pl.pallas_call(functools.partial(backward_kernel, rows, step_rows), grid=...  19.4 us
    ppermute x6, starting transfers between devices, plane_up(): lax.ppermute(value, 'ctx', [(z * step + i, z * step + step + i) for z in...  17.6 us
    ppermute x6, starting transfers between devices, plane_down(): lax.ppermute(value, 'ctx', [(z * step + i, z * step - step + i) for z in...  15.9 us
  transfers between devices with their start and end apart: 46, of which 13 were waited for; matrix products, arithmetic and copies ran while one was open for 31% of the time, Pallas kernels for 32%

profile of v2, /device:TPU:12, one launch (start us, length us, event | category | flops | bytes accessed | tf_op | source)
XLA Modules:
  0.0 656.1 jit_solution(7645282025087529795)
XLA Ops:
  2.6 2.3 collective-permute-start.3
  5.0 3.5 collective-permute-start.4
  18.5 3.8 fusion.34
  23.1 6.3 shard_map.204
  31.4 3.2 collective-permute-start.5
  34.6 3.1 collective-permute-start.6
  37.7 2.8 collective-permute-start.8
  40.5 3.1 collective-permute-start.9
  46.0 8.0 %collective-permute-done.8 = bf16[128,1536]{1,0:T(8,128)(2,1)S(1)} collective-permute-done((bf16[128,1536]{1,0:T(8,128)(2,1)}, bf16[128,1536]{1,0:T(8,128)(2,1)S(1)}, u32[]{:S(2)}, u32[]{:S(2)}) %collective-permute-start.8) | collective-permute-done | bytes 393248 | tf_op jit(solution)/shard_map/ppermute | solution.py:488
  59.3 6.1 collective-permute-start.11
  67.3 6.1 collective-permute-done.10
  75.4 4.4 collective-permute-start.15
  79.9 3.1 broadcast_in_dim.75
  89.5 11.3 %collective-permute-done.19 = bf16[192,1536]{1,0:T(8,128)(2,1)S(1)} collective-permute-done((bf16[192,1536]{1,0:T(8,128)(2,1)S(1)}, bf16[192,1536]{1,0:T(8,128)(2,1)S(1)}, u32[]{:S(2)}, u32[]{:S(2)}) %collective-permute-start.19) | collective-permute-done | bytes 589856 | tf_op jit(solution)/shard_map/ppermute | solution.py:470
  116.3 11.4 %shard_map.203 = (bf16[2048,512]{1,0:T(8,128)(2,1)S(1)}, bf16[2048,256]{1,0:T(8,128)(2,1)}, f32[4,1,1024]{2,1,0:T(1,128)S(1)}) custom-call(f32[2048,512]{1,0:T(8,128)} %bitcast.290, f32[2048,128]{1,0:T(8,128)S(1)} %get-tuple-element.219.cos_ref, f32[2048,128]{1,0:T(8,128)S(1)} %get-tuple-element.218.sin_ref), custom_call_target="tpu_custom_call" | custom-call | tf_op jit(solution)/shard_map/pallas_call | solution.py:370
  128.9 8.2 %all-to-all-start = ((bf16[16,128,256]{2,1,0:T(8,128)(2,1)}), bf16[16,128,256]{2,1,0:T(8,128)(2,1)}, u32[]{:S(2)}, u32[]{:S(2)}) async-start(bf16[16,128,256]{2,1,0:T(8,128)(2,1)} %bitcast.32), calls=%async_computation | async-start | bytes 2097152 | tf_op jit(solution)/shard_map/all_to_all | solution.py:1074
  137.1 4.3 copy.209
  141.4 2.4 copy.210
  143.8 2.4 copy.211
  146.2 3.5 fusion.22
  150.3 2.4 pad_maximum_fusion.1
  152.8 7.0 %copy.212 = bf16[768,8,384]{2,1,0:T(8,128)(2,1)} copy(bf16[768,8,384]{0,2,1:T(8,128)(2,1)} %pad_maximum_fusion.1) | data formatting | bytes 9437184 | tf_op jit(solution)/shard_map/concatenate | solution.py:1188
  159.9 8.3 %reshape_reshape.7 = bf16[4,192,3072]{2,1,0:T(8,128)(2,1)} reshape(bf16[768,8,384]{2,1,0:T(8,128)(2,1)} %copy.212) | data formatting | bytes 9437184 | tf_op jit(solution)/shard_map/reshape;reshape | solution.py:1044
  168.2 6.6 %copy.213 = bf16[768,3072]{1,0:T(8,128)(2,1)} copy(bf16[768,3072]{0,1:T(8,128)(2,1)} %bitcast.282) | data formatting | bytes 9437184 | tf_op jit(solution)/shard_map/reshape | solution.py:1188
  174.8 3.4 fusion.23
  179.7 2.4 dynamic-slice_bitcast_fusion.7
  183.8 13.8 %collective-permute-done.24 = bf16[256,1536]{1,0:T(8,128)(2,1)S(1)} collective-permute-done((bf16[256,1536]{1,0:T(8,128)(2,1)S(1)}, bf16[256,1536]{1,0:T(8,128)(2,1)S(1)}, u32[]{:S(2)}, u32[]{:S(2)}) %collective-permute-start.24) | collective-permute-done | bytes 786464 | tf_op jit(solution)/shard_map/ppermute | solution.py:466
  201.1 2.1 pad_maximum_fusion.3.got
  204.6 11.5 %collective-permute-done.25 = bf16[256,1536]{1,0:T(8,128)(2,1)S(1)} collective-permute-done((bf16[256,1536]{1,0:T(8,128)(2,1)S(1)}, bf16[256,1536]{1,0:T(8,128)(2,1)S(1)}, u32[]{:S(2)}, u32[]{:S(2)}) %collective-permute-start.25) | collective-permute-done | bytes 786464 | tf_op jit(solution)/shard_map/ppermute | solution.py:470
  217.7 3.2 pad.4
  222.4 3.3 copy.194
  225.7 2.6 reshape.656
  228.4 5.1 multiply_reduce_fusion.8
  234.3 20.5 %shard_map.205 = (bf16[2,256,1024]{2,1,0:T(8,128)(2,1)S(1)}, bf16[2,256,1024]{2,1,0:T(8,128)(2,1)S(1)}, bf16[2,256,1024]{2,1,0:T(8,128)(2,1)S(1)}, f32[256,1536]{1,0:T(8,128)}, f32[256,1536]{1,0:T(8,128)}) custom-call(s32[3]{0:T(128)S(1)} %pad_add_fusion.info, bf16[256,1536]{1,0:T(8,128)(2,1)S(1)} %multiply_convert_fusion.4.normed, ...), custom_call_target="tpu_custom_call" | custom-call | flops 9663676416 | bytes 18874368 | tf_op jit(solution)/shard_map/pallas_call | solution.py:653
  254.8 2.9 collective-permute-done.27.normed
  257.8 19.7 %shard_map.206 = (bf16[2,256,1024]{2,1,0:T(8,128)(2,1)S(1)}, bf16[2,256,1024]{2,1,0:T(8,128)(2,1)S(1)}, bf16[2,256,1024]{2,1,0:T(8,128)(2,1)}, bf16[256,1536]{1,0:T(8,128)(2,1)S(1)}, bf16[256,1536]{1,0:T(8,128)(2,1)S(1)}) custom-call(s32[3]{0:T(128)S(1)} %pad_add_fusion.info, bf16[256,1536]{1,0:T(8,128)(2,1)S(1)} %collective-permute-done.27.normed, ...), custom_call_target="tpu_custom_call" | custom-call | flops 9663676416 | bytes 18874368 | tf_op jit(solution)/shard_map/pallas_call | solution.py:653
  282.3 4.5 fusion.38
  288.8 3.0 fusion.42
  291.8 5.1 collective-permute-done.29
  298.5 6.4 add_convert_fusion
  304.8 3.6 add_convert_fusion.1
  308.5 3.7 add_convert_fusion.2
  312.8 4.0 collective-permute-done.30
  316.8 2.8 fusion.64
  320.5 2.9 convolution_convert_fusion.2
  326.4 6.0 all-to-all-start.1
  332.4 3.4 fusion.24
  335.8 3.7 copy.199
  339.5 2.5 reshape_reshape.6
  342.0 2.3 constant_dynamic-slice_fusion.6
  352.0 3.9 dynamic-slice_bitcast_fusion.3
  362.4 15.7 %collective-permute-done.38 = bf16[256,1536]{1,0:T(8,128)(2,1)S(1)} collective-permute-done((bf16[256,1536]{1,0:T(8,128)(2,1)}, bf16[256,1536]{1,0:T(8,128)(2,1)S(1)}, u32[]{:S(2)}, u32[]{:S(2)}) %collective-permute-start.38) | collective-permute-done | bytes 786464 | tf_op jit(solution)/shard_map/ppermute | solution.py:466
  378.2 2.9 convolution_convert_fusion
  383.3 19.5 %collective-permute-done.41 = bf16[192,3072]{1,0:T(8,128)(2,1)} collective-permute-done((bf16[192,3072]{1,0:T(8,128)(2,1)}, bf16[192,3072]{1,0:T(8,128)(2,1)}, u32[]{:S(2)}, u32[]{:S(2)}) %collective-permute-start.41) | collective-permute-done | bytes 1179680 | tf_op jit(solution)/shard_map/ppermute | solution.py:466
  403.3 19.4 %shard_map.207 = bf16[2048,384]{1,0:T(8,128)(2,1)S(1)} custom-call(bf16[2048,512]{1,0:T(8,128)(2,1)} %copy-done.2, bf16[2048,256]{1,0:T(8,128)(2,1)} %get-tuple-element.49.out_ref, bf16[2048,256]{1,0:T(8,128)(2,1)S(1)} %bitcast.279, f32[8,1,512]{2,1,0:T(1,128)S(1)} %reshape.669.lse_ref, f32[2048,128]{1,0:T(8,128)S(1)} %get-tuple-element.219.cos_ref, ...), custom_call_target="tpu_custom_call" | custom-call | tf_op jit(solution)/shard_map/pallas_call | solution.py:437
  422.8 5.6 fusion.16
  429.6 21.8 %collective-permute-done.42 = bf16[192,3072]{1,0:T(8,128)(2,1)} collective-permute-done((bf16[192,3072]{1,0:T(8,128)(2,1)}, bf16[192,3072]{1,0:T(8,128)(2,1)}, u32[]{:S(2)}, u32[]{:S(2)}) %collective-permute-start.42) | collective-permute-done | bytes 1179680 | tf_op jit(solution)/shard_map/ppermute | solution.py:470
  458.7 150.3 %shard_map.208 = (bf16[16,128,384]{2,1,0:T(8,128)(2,1)}, bf16[192,1024]{1,0:T(8,128)(2,1)S(1)}, bf16[96,1024]{1,0:T(8,128)(2,1)S(1)}, bf16[2,2,96,256]{3,2,1,0:T...) custom-call(bf16[16,128,384]{2,1,0:T(8,128)(2,1)} %bitcast.274, ...), custom_call_target="tpu_custom_call" | custom-call | tf_op jit(solution)/shard_map/pallas_call | solution.py:947
  620.3 2.6 reshape.704
  626.5 4.2 copy.264
  630.7 5.0 reshape.682
  641.6 3.0 broadcast_select_fusion.3
  644.6 4.1 broadcast_select_fusion.1
  648.7 6.0 multiply_reduce_fusion.4
  (305 shorter events, 122.1 us)
Async XLA Ops:
  2.6 32.0 %collective-permute-start.3 = (bf16[128,1536]{1,0:T(8,128)(2,1)S(1)}, bf16[128,1536]{1,0:T(8,128)(2,1)}, u32[]{:S(2)}, u32[]{:S(2)}) collective-permute-start(bf16[128,1536]{1,0:T(8,128)(2,1)S(1)} %bitcast.308), channel_id=1, source_target_pairs={{8,0},{10,2},{12,4},{14,6},{16,8},{18,10},{20,12},{22,14},{24,16},... | collective-permute-start | bytes 1179656 | tf_op jit(solution)/shard_map/ppermute | solution.py:488
  5.0 32.8 %collective-permute-start.4 = (bf16[128,1536]{1,0:T(8,128)(2,1)S(1)}, bf16[128,1536]{1,0:T(8,128)(2,1)}, u32[]{:S(2)}, u32[]{:S(2)}) collective-permute-start(bf16[128,1536]{1,0:T(8,128)(2,1)S(1)} %bitcast.309), channel_id=1, source_target_pairs={{0,8},{2,10},{4,12},{6,14},{8,16},{10,18},{12,20},{14,22},{16,24},... | collective-permute-start | bytes 1179656 | tf_op jit(solution)/shard_map/ppermute | solution.py:483
  8.4 21.8 %collective-permute-start = (bf16[128,1536]{1,0:T(8,128)(2,1)}, bf16[128,1536]{1,0:T(8,128)(2,1)}, u32[]{:S(2)}, u32[]{:S(2)}) collective-permute-start(bf16[128,1536]{1,0:T(8,128)(2,1)} %get-tuple-element.203), channel_id=1, source_target_pairs={{0,4},{2,6},{4,0},{6,2},{8,12},{10,14},{12,8},{14,10},{16,20},{18,... | collective-permute-start | bytes 1179656 | tf_op jit(solution)/shard_map/ppermute | solution.py:470
  10.4 6.0 copy-start.23
  12.1 6.4 copy-start.31
  13.0 27.5 %collective-permute-start.2 = (bf16[768,384]{0,1:T(8,128)(2,1)}, bf16[768,384]{0,1:T(8,128)(2,1)}, u32[]{:S(2)}, u32[]{:S(2)}) collective-permute-start(bf16[768,384]{0,1:T(8,128)(2,1)} %pad_maximum_fusion.21), channel_id=1, source_target_pairs={{0,1},{1,0},{2,3},{3,2},{4,5},{5,4},{6,7},{7,6},{8,9},{9,8},{10,11... | collective-permute-start | bytes 1769480 | tf_op jit(solution)/shard_map/ppermute | solution.py:466
  23.1 6.3 copy-start.12
  29.4 14.2 %copy-start.24 = (bf16[768,192]{0,1:T(8,128)(2,1)S(1)}, bf16[768,192]{0,1:T(8,128)(2,1)}, u32[]{:S(2)}) copy-start(bf16[768,192]{0,1:T(8,128)(2,1)} %copy-done.23) | copy-start | bytes 884740
  29.4 14.2 %copy-start.32 = (bf16[768,96]{0,1:T(8,128)(2,1)S(1)}, bf16[768,96]{0,1:T(8,128)(2,1)}, u32[]{:S(2)}) copy-start(bf16[768,96]{0,1:T(8,128)(2,1)} %copy-done.31) | copy-start | bytes 442372
  31.3 13.6 %copy-start.3 = (bf16[512,384]{1,0:T(8,128)(2,1)S(1)}, bf16[512,384]{1,0:T(8,128)(2,1)}, u32[]{:S(2)}) copy-start(bf16[512,384]{1,0:T(8,128)(2,1)} %constant.299.pick_ref) | copy-start | bytes 1179652
  31.3 28.0 %collective-permute-start.1 = (bf16[2,128,1536]{2,1,0:T(8,128)(2,1)S(1)}, bf16[2,128,1536]{2,1,0:T(8,128)(2,1)S(1)}, u32[]{:S(2)}, u32[]{:S(2)}) collective-permute-start(bf16[2,128,1536]{2,1,0:T(8,128)(2,1)S(1)} %pad_maximum_fusion.16), channel_id=1, source_target_pairs={{0,2},{2,0},{4,6},{6,4},{8,10},{10,8},{12,14},{14,12},{16,18},{18,... | collective-permute-start | bytes 2359304 | tf_op jit(solution)/shard_map/ppermute | solution.py:470
  31.4 25.3 %collective-permute-start.5 = (bf16[128,1536]{1,0:T(8,128)(2,1)}, bf16[128,1536]{1,0:T(8,128)(2,1)S(1)}, u32[]{:S(2)}, u32[]{:S(2)}) collective-permute-start(bf16[128,1536]{1,0:T(8,128)(2,1)} %collective-permute-done), channel_id=1, source_target_pairs={{8,0},{10,2},{12,4},{14,6},{16,8},{18,10},{20,12},{22,14},{24,16},... | collective-permute-start | bytes 1179656 | tf_op jit(solution)/shard_map/ppermute | solution.py:488
  34.6 22.8 %collective-permute-start.6 = (bf16[128,1536]{1,0:T(8,128)(2,1)}, bf16[128,1536]{1,0:T(8,128)(2,1)S(1)}, u32[]{:S(2)}, u32[]{:S(2)}) collective-permute-start(bf16[128,1536]{1,0:T(8,128)(2,1)} %collective-permute-done), channel_id=1, source_target_pairs={{0,8},{2,10},{4,12},{6,14},{8,16},{10,18},{12,20},{14,22},{16,24},... | collective-permute-start | bytes 1179656 | tf_op jit(solution)/shard_map/ppermute | solution.py:483
  37.7 16.3 %collective-permute-start.8 = (bf16[128,1536]{1,0:T(8,128)(2,1)}, bf16[128,1536]{1,0:T(8,128)(2,1)S(1)}, u32[]{:S(2)}, u32[]{:S(2)}) collective-permute-start(bf16[128,1536]{1,0:T(8,128)(2,1)} %collective-permute-done.3), channel_id=1, source_target_pairs={{8,0},{10,2},{12,4},{14,6},{16,8},{18,10},{20,12},{22,14},{9,1},{1... | collective-permute-start | bytes 1179656 | tf_op jit(solution)/shard_map/ppermute | solution.py:488
  40.5 14.8 %collective-permute-start.9 = (bf16[128,1536]{1,0:T(8,128)(2,1)}, bf16[128,1536]{1,0:T(8,128)(2,1)S(1)}, u32[]{:S(2)}, u32[]{:S(2)}) collective-permute-start(bf16[128,1536]{1,0:T(8,128)(2,1)} %collective-permute-done.4), channel_id=1, source_target_pairs={{8,16},{10,18},{12,20},{14,22},{16,24},{18,26},{20,28},{22,30},{9,... | collective-permute-start | bytes 1179656 | tf_op jit(solution)/shard_map/ppermute | solution.py:483
  45.0 9.0 %copy-start.37 = (bf16[192,1536]{1,0:T(8,128)(2,1)S(1)}, bf16[192,1536]{1,0:T(8,128)(2,1)}, u32[]{:S(2)}) copy-start(bf16[192,1536]{1,0:T(8,128)(2,1)} %dynamic-slice_bitcast_fusion.14) | copy-start | bytes 1769476
  54.0 20.0 %collective-permute-start.18 = (bf16[192,1536]{1,0:T(8,128)(2,1)S(1)}, bf16[192,1536]{1,0:T(8,128)(2,1)S(1)}, u32[]{:S(2)}, u32[]{:S(2)}) collective-permute-start(bf16[192,1536]{1,0:T(8,128)(2,1)S(1)} %copy-done.37), channel_id=1, source_target_pairs={{0,1},{1,0},{2,3},{3,2},{4,5},{5,4},{6,7},{7,6},{8,9},{9,8},{10,11... | collective-permute-start | bytes 1769480 | tf_op jit(solution)/shard_map/ppermute | solution.py:466
  55.3 29.1 %collective-permute-start.13 = (bf16[128,1536]{1,0:T(8,128)(2,1)S(1)}, bf16[128,1536]{1,0:T(8,128)(2,1)S(1)}, u32[]{:S(2)}, u32[]{:S(2)}) collective-permute-start(bf16[128,1536]{1,0:T(8,128)(2,1)S(1)} %collective-permute-done.8), channel_id=1, source_target_pairs={{8,0},{10,2},{12,4},{14,6},{9,1},{11,3},{13,5},{15,7}} | collective-permute-start | bytes 1179656 | tf_op jit(solution)/shard_map/ppermute | solution.py:488
  56.7 28.9 %collective-permute-start.14 = (bf16[128,1536]{1,0:T(8,128)(2,1)S(1)}, bf16[128,1536]{1,0:T(8,128)(2,1)S(1)}, u32[]{:S(2)}, u32[]{:S(2)}) collective-permute-start(bf16[128,1536]{1,0:T(8,128)(2,1)S(1)} %collective-permute-done.9), channel_id=1, source_target_pairs={{16,24},{18,26},{20,28},{22,30},{17,25},{19,27},{21,29},{23,31}} | collective-permute-start | bytes 1179656 | tf_op jit(solution)/shard_map/ppermute | solution.py:483
  57.4 16.0 %collective-permute-start.10 = (bf16[128,1536]{1,0:T(8,128)(2,1)S(1)}, bf16[128,1536]{1,0:T(8,128)(2,1)S(1)}, u32[]{:S(2)}, u32[]{:S(2)}) collective-permute-start(bf16[128,1536]{1,0:T(8,128)(2,1)S(1)} %collective-permute-done.5), channel_id=1, source_target_pairs={{8,0},{10,2},{12,4},{14,6},{16,8},{18,10},{20,12},{22,14},{9,1},{1... | collective-permute-start | bytes 1179656 | tf_op jit(solution)/shard_map/ppermute | solution.py:488
  59.3 14.1 %collective-permute-start.11 = (bf16[128,1536]{1,0:T(8,128)(2,1)S(1)}, bf16[128,1536]{1,0:T(8,128)(2,1)S(1)}, u32[]{:S(2)}, u32[]{:S(2)}) collective-permute-start(bf16[128,1536]{1,0:T(8,128)(2,1)S(1)} %collective-permute-done.6), channel_id=1, source_target_pairs={{8,16},{10,18},{12,20},{14,22},{16,24},{18,26},{20,28},{22,30},{9,... | collective-permute-start | bytes 1179656 | tf_op jit(solution)/shard_map/ppermute | solution.py:483
  73.5 28.5 %collective-permute-start.12 = (bf16[2,128,1536]{2,1,0:T(8,128)(2,1)S(1)}, bf16[2,128,1536]{2,1,0:T(8,128)(2,1)S(1)}, u32[]{:S(2)}, u32[]{:S(2)}) collective-permute-start(bf16[2,128,1536]{2,1,0:T(8,128)(2,1)S(1)} %pad_maximum_fusion.18), channel_id=1, source_target_pairs={{0,2},{2,0},{4,6},{6,4},{8,10},{10,8},{12,14},{14,12},{16,18},{18,... | collective-permute-start | bytes 2359304 | tf_op jit(solution)/shard_map/ppermute | solution.py:470
  74.0 75.7 %collective-permute-start.21 = (bf16[384,2048]{1,0:T(8,128)(2,1)}, bf16[384,2048]{1,0:T(8,128)(2,1)}, u32[]{:S(2)}, u32[]{:S(2)}) collective-permute-start(bf16[384,2048]{1,0:T(8,128)(2,1)} %shard_map.204), channel_id=1, source_target_pairs={{0,1},{1,0},{2,3},{3,2},{4,5},{5,4},{6,7},{7,6},{8,9},{9,8},{10,11... | collective-permute-start | bytes 4718600 | tf_op jit(solution)/shard_map/ppermute | solution.py:466
  75.4 13.1 %collective-permute-start.15 = (bf16[128,1536]{1,0:T(8,128)(2,1)S(1)}, bf16[128,1536]{1,0:T(8,128)(2,1)S(1)}, u32[]{:S(2)}, u32[]{:S(2)}) collective-permute-start(bf16[128,1536]{1,0:T(8,128)(2,1)S(1)} %collective-permute-done.10), channel_id=1, source_target_pairs={{8,0},{10,2},{12,4},{14,6},{9,1},{11,3},{13,5},{15,7}} | collective-permute-start | bytes 1179656 | tf_op jit(solution)/shard_map/ppermute | solution.py:488
  84.4 4.1 collective-permute-start.16
  85.6 15.2 %collective-permute-start.19 = (bf16[192,1536]{1,0:T(8,128)(2,1)S(1)}, bf16[192,1536]{1,0:T(8,128)(2,1)S(1)}, u32[]{:S(2)}, u32[]{:S(2)}) collective-permute-start(bf16[192,1536]{1,0:T(8,128)(2,1)S(1)} %collective-permute-done.18), channel_id=1, source_target_pairs={{0,4},{2,6},{4,0},{6,2},{8,12},{10,14},{12,8},{14,10},{16,20},{18,... | collective-permute-start | bytes 1769480 | tf_op jit(solution)/shard_map/ppermute | solution.py:470
  88.8 14.7 %collective-permute-start.7 = (bf16[2,128,1536]{2,1,0:T(8,128)(2,1)S(1)}, bf16[2,128,1536]{2,1,0:T(8,128)(2,1)S(1)}, u32[]{:S(2)}, u32[]{:S(2)}) collective-permute-start(bf16[2,128,1536]{2,1,0:T(8,128)(2,1)S(1)} %pad_maximum_fusion.17), channel_id=1, source_target_pairs={{0,2},{2,0},{4,6},{6,4},{8,10},{10,8},{12,14},{14,12},{16,18},{18,... | collective-permute-start | bytes 2359304 | tf_op jit(solution)/shard_map/ppermute | solution.py:470
  88.9 14.5 %collective-permute-start.17 = (bf16[2,128,1536]{2,1,0:T(8,128)(2,1)S(1)}, bf16[2,128,1536]{2,1,0:T(8,128)(2,1)S(1)}, u32[]{:S(2)}, u32[]{:S(2)}) collective-permute-start(bf16[2,128,1536]{2,1,0:T(8,128)(2,1)S(1)} %pad_maximum_fusion.19), channel_id=1, source_target_pairs={{0,2},{2,0},{4,6},{6,4},{8,10},{10,8},{12,14},{14,12},{16,18},{18,... | collective-permute-start | bytes 2359304 | tf_op jit(solution)/shard_map/ppermute | solution.py:470
  102.0 80.1 %collective-permute-start.20 = (bf16[384,1536]{1,0:T(8,128)(2,1)}, bf16[384,1536]{1,0:T(8,128)(2,1)}, u32[]{:S(2)}, u32[]{:S(2)}) collective-permute-start(bf16[384,1536]{1,0:T(8,128)(2,1)} %pad_maximum_fusion.14), channel_id=1, source_target_pairs={{0,2},{2,0},{4,6},{6,4},{8,10},{10,8},{12,14},{14,12},{16,18},{18,... | collective-permute-start | bytes 3538952 | tf_op jit(solution)/shard_map/ppermute | solution.py:470
  128.9 93.5 %all-to-all-start = ((bf16[16,128,256]{2,1,0:T(8,128)(2,1)}), bf16[16,128,256]{2,1,0:T(8,128)(2,1)}, u32[]{:S(2)}, u32[]{:S(2)}) async-start(bf16[16,128,256]{2,1,0:T(8,128)(2,1)} %bitcast.32), calls=%async_computation | async-start | bytes 2097152 | tf_op jit(solution)/shard_map/all_to_all | solution.py:1074
  149.8 49.3 %collective-permute-start.22 = (bf16[384,2048]{1,0:T(8,128)(2,1)}, bf16[384,2048]{1,0:T(8,128)(2,1)}, u32[]{:S(2)}, u32[]{:S(2)}) collective-permute-start(bf16[384,2048]{1,0:T(8,128)(2,1)} %collective-permute-done.21), channel_id=1, source_target_pairs={{0,4},{2,6},{4,0},{6,2},{8,12},{10,14},{12,8},{14,10},{16,20},{18,... | collective-permute-start | bytes 4718600 | tf_op jit(solution)/shard_map/ppermute | solution.py:470
  178.3 19.3 %collective-permute-start.24 = (bf16[256,1536]{1,0:T(8,128)(2,1)S(1)}, bf16[256,1536]{1,0:T(8,128)(2,1)S(1)}, u32[]{:S(2)}, u32[]{:S(2)}) collective-permute-start(bf16[256,1536]{1,0:T(8,128)(2,1)S(1)} %bitcast.321), channel_id=1, source_target_pairs={{0,1},{1,0},{2,3},{3,2},{4,5},{5,4},{6,7},{7,6},{8,9},{9,8},{10,11... | collective-permute-start | bytes 2359304 | tf_op jit(solution)/shard_map/ppermute | solution.py:466
  197.6 18.4 %collective-permute-start.25 = (bf16[256,1536]{1,0:T(8,128)(2,1)S(1)}, bf16[256,1536]{1,0:T(8,128)(2,1)S(1)}, u32[]{:S(2)}, u32[]{:S(2)}) collective-permute-start(bf16[256,1536]{1,0:T(8,128)(2,1)S(1)} %collective-permute-done.24), channel_id=1, source_target_pairs={{0,4},{2,6},{4,0},{6,2},{8,12},{10,14},{12,8},{14,10},{16,20},{18,... | collective-permute-start | bytes 2359304 | tf_op jit(solution)/shard_map/ppermute | solution.py:470
  203.2 31.1 %collective-permute-start.23 = (bf16[768,2048]{1,0:T(8,128)(2,1)}, bf16[768,2048]{1,0:T(8,128)(2,1)}, u32[]{:S(2)}, u32[]{:S(2)}) collective-permute-start(bf16[768,2048]{1,0:T(8,128)(2,1)} %pad_maximum_fusion.3.got), channel_id=1, source_target_pairs={{0,2},{2,0},{4,6},{6,4},{8,10},{10,8},{12,14},{14,12},{16,18},{18,... | collective-permute-start | bytes 9437192 | tf_op jit(solution)/shard_map/ppermute | solution.py:470
  217.4 17.0 %collective-permute-start.26 = (bf16[512,1536]{1,0:T(8,128)(2,1)}, bf16[512,1536]{1,0:T(8,128)(2,1)}, u32[]{:S(2)}, u32[]{:S(2)}) collective-permute-start(bf16[512,1536]{1,0:T(8,128)(2,1)} %pad_maximum_fusion.10.down_got), channel_id=1, source_target_pairs={{0,2},{2,0},{4,6},{6,4},{8,10},{10,8},{12,14},{14,12},{16,18},{18,... | collective-permute-start | bytes 4718600 | tf_op jit(solution)/shard_map/ppermute | solution.py:470
  220.9 33.9 %collective-permute-start.28 = (bf16[256,1536]{1,0:T(8,128)(2,1)S(1)}, bf16[256,1536]{1,0:T(8,128)(2,1)}, u32[]{:S(2)}, u32[]{:S(2)}) collective-permute-start(bf16[256,1536]{1,0:T(8,128)(2,1)S(1)} %bitcast.275), channel_id=1, source_target_pairs={{0,1},{1,0},{2,3},{3,2},{4,5},{5,4},{6,7},{7,6},{8,9},{9,8},{10,11... | collective-permute-start | bytes 2359304 | tf_op jit(solution)/shard_map/ppermute | solution.py:466
  233.7 24.0 %collective-permute-start.27 = (bf16[256,1536]{1,0:T(8,128)(2,1)S(1)}, bf16[256,1536]{1,0:T(8,128)(2,1)S(1)}, u32[]{:S(2)}, u32[]{:S(2)}) collective-permute-start(bf16[256,1536]{1,0:T(8,128)(2,1)S(1)} %multiply_convert_fusion.4.normed), channel_id=1, source_target_pairs={{0,1},{1,0},{2,3},{3,2},{4,5},{5,4},{6,7},{7,6},{8,9},{9,8},{10,11... | collective-permute-start | bytes 2359304 | tf_op jit(solution)/shard_map/ppermute | solution.py:466
  277.6 19.2 %collective-permute-start.29 = (bf16[256,1536]{1,0:T(8,128)(2,1)S(1)}, bf16[256,1536]{1,0:T(8,128)(2,1)S(1)}, u32[]{:S(2)}, u32[]{:S(2)}) collective-permute-start(bf16[256,1536]{1,0:T(8,128)(2,1)S(1)} %get-tuple-element.58), channel_id=1, source_target_pairs={{0,1},{1,0},{2,3},{3,2},{4,5},{5,4},{6,7},{7,6},{8,9},{9,8},{10,11... | collective-permute-start | bytes 2359304 | tf_op jit(solution)/shard_map/ppermute | solution.py:466
  279.5 17.3 %collective-permute-start.35 = (bf16[512,1024]{1,0:T(8,128)(2,1)S(1)}, bf16[512,1024]{1,0:T(8,128)(2,1)S(1)}, u32[]{:S(2)}, u32[]{:S(2)}) collective-permute-start(bf16[512,1024]{1,0:T(8,128)(2,1)S(1)} %dynamic-slice_bitcast_fusion.8), channel_id=1, source_target_pairs={{0,2},{2,0},{4,6},{6,4},{8,10},{10,8},{12,14},{14,12},{16,18},{18,... | collective-permute-start | bytes 3145736 | tf_op jit(solution)/shard_map/ppermute | solution.py:470
  279.6 18.9 %collective-permute-start.34 = (bf16[512,1536]{1,0:T(8,128)(2,1)S(1)}, bf16[512,1536]{1,0:T(8,128)(2,1)S(1)}, u32[]{:S(2)}, u32[]{:S(2)}) collective-permute-start(bf16[512,1536]{1,0:T(8,128)(2,1)S(1)} %pad_maximum_fusion.12), channel_id=1, source_target_pairs={{0,2},{2,0},{4,6},{6,4},{8,10},{10,8},{12,14},{14,12},{16,18},{18,... | collective-permute-start | bytes 4718600 | tf_op jit(solution)/shard_map/ppermute | solution.py:470
  280.3 24.5 %collective-permute-start.33 = (bf16[512,1024]{1,0:T(8,128)(2,1)S(1)}, bf16[512,1024]{1,0:T(8,128)(2,1)S(1)}, u32[]{:S(2)}, u32[]{:S(2)}) collective-permute-start(bf16[512,1024]{1,0:T(8,128)(2,1)S(1)} %dynamic-slice_bitcast_fusion.9), channel_id=1, source_target_pairs={{0,2},{2,0},{4,6},{6,4},{8,10},{10,8},{12,14},{14,12},{16,18},{18,... | collective-permute-start | bytes 3145736 | tf_op jit(solution)/shard_map/ppermute | solution.py:470
  281.7 26.7 %collective-permute-start.31 = (bf16[512,1536]{1,0:T(8,128)(2,1)S(1)}, bf16[512,1536]{1,0:T(8,128)(2,1)S(1)}, u32[]{:S(2)}, u32[]{:S(2)}) collective-permute-start(bf16[512,1536]{1,0:T(8,128)(2,1)S(1)} %pad_maximum_fusion.11), channel_id=1, source_target_pairs={{0,2},{2,0},{4,6},{6,4},{8,10},{10,8},{12,14},{14,12},{16,18},{18,... | collective-permute-start | bytes 4718600 | tf_op jit(solution)/shard_map/ppermute | solution.py:470
  296.8 11.6 %collective-permute-start.32 = (bf16[512,1024]{1,0:T(8,128)(2,1)S(1)}, bf16[512,1024]{1,0:T(8,128)(2,1)S(1)}, u32[]{:S(2)}, u32[]{:S(2)}) collective-permute-start(bf16[512,1024]{1,0:T(8,128)(2,1)S(1)} %dynamic-slice_bitcast_fusion.10), channel_id=1, source_target_pairs={{0,2},{2,0},{4,6},{6,4},{8,10},{10,8},{12,14},{14,12},{16,18},{18,... | collective-permute-start | bytes 3145736 | tf_op jit(solution)/shard_map/ppermute | solution.py:470
  296.8 20.0 %collective-permute-start.30 = (bf16[256,1536]{1,0:T(8,128)(2,1)S(1)}, bf16[256,1536]{1,0:T(8,128)(2,1)S(1)}, u32[]{:S(2)}, u32[]{:S(2)}) collective-permute-start(bf16[256,1536]{1,0:T(8,128)(2,1)S(1)} %get-tuple-element.59), channel_id=1, source_target_pairs={{0,1},{1,0},{2,3},{3,2},{4,5},{5,4},{6,7},{7,6},{8,9},{9,8},{10,11... | collective-permute-start | bytes 2359304 | tf_op jit(solution)/shard_map/ppermute | solution.py:466
  308.5 8.3 %copy-start.29 = (f32[256,1536]{1,0:T(8,128)S(1)}, f32[256,1536]{1,0:T(8,128)}, u32[]{:S(2)}) copy-start(f32[256,1536]{1,0:T(8,128)} %get-tuple-element.53) | copy-start | bytes 4718596
  312.1 8.4 %slice-start.2 = ((s8[6291456]{0:T(1024)(128)(4,1)}), s8[4194304]{0:T(1024)(128)(4,1)S(1)}, s32[]{:S(2)}) async-start(s8[6291456]{0:T(1024)(128)(4,1)} %bitcast.296), calls=%async_computation.4 | async-start | bytes 8388608
  312.8 7.7 %slice-start.3 = ((s8[6291456]{0:T(1024)(128)(4,1)}), s8[2097152]{0:T(1024)(128)(4,1)S(1)}, s32[]{:S(2)}) async-start(s8[6291456]{0:T(1024)(128)(4,1)} %bitcast.296), calls=%async_computation.5 | async-start | bytes 4194304
  326.4 76.9 %all-to-all-start.1 = ((bf16[16,128,256]{2,1,0:T(8,128)(2,1)}), bf16[16,128,256]{2,1,0:T(8,128)(2,1)S(1)}, u32[]{:S(2)}, u32[]{:S(2)}) async-start(bf16[16,128,256]{2,1,0:T(8,128)(2,1)} %bitcast.301), calls=%async_computation.1 | async-start | bytes 2097152 | tf_op jit(solution)/shard_map/all_to_all | solution.py:1074
  346.3 16.1 %collective-permute-start.39 = (bf16[256,1024]{1,0:T(8,128)(2,1)}, bf16[256,1024]{1,0:T(8,128)(2,1)}, u32[]{:S(2)}, u32[]{:S(2)}) collective-permute-start(bf16[256,1024]{1,0:T(8,128)(2,1)} %bitcast.324), channel_id=1, source_target_pairs={{0,1},{1,0},{2,3},{3,2},{4,5},{5,4},{6,7},{7,6},{8,9},{9,8},{10,11... | collective-permute-start | bytes 1572872 | tf_op jit(solution)/shard_map/ppermute | solution.py:466
  350.0 28.2 %collective-permute-start.38 = (bf16[256,1536]{1,0:T(8,128)(2,1)}, bf16[256,1536]{1,0:T(8,128)(2,1)S(1)}, u32[]{:S(2)}, u32[]{:S(2)}) collective-permute-start(bf16[256,1536]{1,0:T(8,128)(2,1)} %copy-done.34), channel_id=1, source_target_pairs={{0,1},{1,0},{2,3},{3,2},{4,5},{5,4},{6,7},{7,6},{8,9},{9,8},{10,11... | collective-permute-start | bytes 2359304 | tf_op jit(solution)/shard_map/ppermute | solution.py:466
  350.4 52.4 %collective-permute-start.41 = (bf16[192,3072]{1,0:T(8,128)(2,1)}, bf16[192,3072]{1,0:T(8,128)(2,1)}, u32[]{:S(2)}, u32[]{:S(2)}) collective-permute-start(bf16[192,3072]{1,0:T(8,128)(2,1)} %dynamic-slice_bitcast_fusion.7), channel_id=1, source_target_pairs={{0,1},{1,0},{2,3},{3,2},{4,5},{5,4},{6,7},{7,6},{8,9},{9,8},{10,11... | collective-permute-start | bytes 3538952 | tf_op jit(solution)/shard_map/ppermute | solution.py:466
  356.5 72.0 %collective-permute-start.37 = (bf16[4,128,1536]{2,1,0:T(8,128)(2,1)}, bf16[4,128,1536]{2,1,0:T(8,128)(2,1)}, u32[]{:S(2)}, u32[]{:S(2)}) collective-permute-start(bf16[4,128,1536]{2,1,0:T(8,128)(2,1)} %get-tuple-element.167), channel_id=1, source_target_pairs={{0,4},{2,6},{4,0},{6,2},{8,12},{10,14},{12,8},{14,10},{16,20},{18,... | collective-permute-start | bytes 4718600 | tf_op jit(solution)/shard_map/ppermute | solution.py:470
  359.1 69.7 %collective-permute-start.36 = (bf16[4,192,1024]{2,1,0:T(8,128)(2,1)}, bf16[4,192,1024]{2,1,0:T(8,128)(2,1)}, u32[]{:S(2)}, u32[]{:S(2)}) collective-permute-start(bf16[4,192,1024]{2,1,0:T(8,128)(2,1)} %get-tuple-element.169), channel_id=1, source_target_pairs={{0,4},{2,6},{4,0},{6,2},{8,12},{10,14},{12,8},{14,10},{16,20},{18,... | collective-permute-start | bytes 4718600 | tf_op jit(solution)/shard_map/ppermute | solution.py:470
  360.5 17.6 %copy-start.35 = (bf16[256,1536]{1,0:T(8,128)(2,1)S(1)}, bf16[256,1536]{1,0:T(8,128)(2,1)}, u32[]{:S(2)}) copy-start(bf16[256,1536]{1,0:T(8,128)(2,1)} %copy-done.34) | copy-start | bytes 2359300
  360.5 17.6 %copy-start.38 = (bf16[256,1,1024]{2,0,1:T(8,128)(2,1)S(1)}, bf16[256,1,1024]{2,0,1:T(8,128)(2,1)}, u32[]{:S(2)}) copy-start(bf16[256,1,1024]{2,0,1:T(8,128)(2,1)} %copy.200) | copy-start | bytes 1572868
  381.1 22.3 %copy-start.4 = (bf16[512,384]{1,0:T(8,128)(2,1)S(1)}, bf16[512,384]{1,0:T(8,128)(2,1)}, u32[]{:S(2)}) copy-start(bf16[512,384]{1,0:T(8,128)(2,1)} %constant.299.pick_ref) | copy-start | bytes 1179652
  383.3 71.8 %collective-permute-start.40 = (bf16[8,96,1024]{2,1,0:T(8,128)(2,1)}, bf16[8,96,1024]{2,1,0:T(8,128)(2,1)}, u32[]{:S(2)}, u32[]{:S(2)}) collective-permute-start(bf16[8,96,1024]{2,1,0:T(8,128)(2,1)} %dynamic-slice_bitcast_fusion), channel_id=1, source_target_pairs={{0,2},{2,0},{4,6},{6,4},{8,10},{10,8},{12,14},{14,12},{16,18},{18,... | collective-permute-start | bytes 4718600 | tf_op jit(solution)/shard_map/ppermute | solution.py:470
  402.8 48.7 %collective-permute-start.42 = (bf16[192,3072]{1,0:T(8,128)(2,1)}, bf16[192,3072]{1,0:T(8,128)(2,1)}, u32[]{:S(2)}, u32[]{:S(2)}) collective-permute-start(bf16[192,3072]{1,0:T(8,128)(2,1)} %collective-permute-done.41), channel_id=1, source_target_pairs={{0,4},{2,6},{4,0},{6,2},{8,12},{10,14},{12,8},{14,10},{16,20},{18,... | collective-permute-start | bytes 3538952 | tf_op jit(solution)/shard_map/ppermute | solution.py:470
  403.3 19.4 %copy-start.26 = (bf16[768,384]{0,1:T(8,128)(2,1)S(1)}, bf16[768,384]{0,1:T(8,128)(2,1)}, u32[]{:S(2)}) copy-start(bf16[768,384]{0,1:T(8,128)(2,1)} %copy-done.25) | copy-start | bytes 1769476
  403.3 19.5 %copy-start.28 = (bf16[768,384]{0,1:T(8,128)(2,1)S(1)}, bf16[768,384]{0,1:T(8,128)(2,1)}, u32[]{:S(2)}) copy-start(bf16[768,384]{0,1:T(8,128)(2,1)} %copy-done.27) | copy-start | bytes 1769476
  422.8 5.6 copy-start
  455.0 186.5 %collective-permute-start.43 = (bf16[384,3072]{1,0:T(8,128)(2,1)}, bf16[384,3072]{1,0:T(8,128)(2,1)}, u32[]{:S(2)}, u32[]{:S(2)}) collective-permute-start(bf16[384,3072]{1,0:T(8,128)(2,1)} %pad_maximum_fusion.5), channel_id=1, source_target_pairs={{0,2},{2,0},{4,6},{6,4},{8,10},{10,8},{12,14},{14,12},{16,18},{18,... | collective-permute-start | bytes 7077896 | tf_op jit(solution)/shard_map/ppermute | solution.py:470
  630.7 13.8 %slice-start = ((s8[4718592]{0:T(1024)(128)(4,1)}), s8[524288]{0:T(1024)(128)(4,1)S(1)}, s32[]{:S(2)}) async-start(s8[4718592]{0:T(1024)(128)(4,1)} %bitcast.288), calls=%async_computation.2 | async-start | bytes 1048576
  648.7 6.0 copy-start.15
  (31 other events, 93.0 us)

commit v3 on v2

--- a/solution.py
+++ b/solution.py
@@ -324,14 +324,18 @@
 def turn(v,cosine,sine):
     return v*cosine+pltpu.roll(v,LANES//2,1)*sine
 
-def forward_kernel(rows,step_rows,raw_ref,cos_ref,sin_ref,qkv_ref,out_ref,lse_ref,key_ref,val_t_ref):
+def forward_kernel(tokens_ref,gain_ref,weight_ref,cos_ref,sin_ref,normed_ref,qkv_ref,out_ref,lse_ref,key_ref,val_t_ref):
     at=pl.program_id(0)
+    rows=tokens_ref.shape[0]
     here=pl.ds(pl.multiple_of(at*rows,rows),rows)
     cosine,sine=cos_ref[...],sin_ref[...]
-    raw=raw_ref[...]
     @pl.when(at==0)
     def _():
         val_t_ref[...]=jnp.zeros_like(val_t_ref)
+    unit,_=normalize(tokens_ref[...].astype(jnp.float32))
+    normed=(unit*gain_ref[...]).astype(BF)
+    normed_ref[...]=normed
+    raw=nn(normed,weight_ref[...])
     scale=HD**-0.5
     parts=[(turn(raw[:,j*LANES:(j+1)*LANES],cosine,sine)*(scale if j<2 else 1.0)).astype(BF) for j in range(3)]
     value=raw[:,3*LANES:].astype(BF)
@@ -342,50 +346,58 @@
     val_t_ref[:,here]=value.T
     query=jnp.concatenate(parts[:2],axis=0)
     length=key_ref.shape[0]
-    per=step_rows//rows
-    for band in range(length//step_rows):
-        @pl.when(at//per==band)
+    for band in range(length//rows):
+        @pl.when(at==band)
         def _():
-            extent=(band+1)*step_rows
-            scores=nt(key_ref[0:extent,:],query)
-            tail=scores[band*step_rows:,:]
+            scores=nt(key_ref[0:(band+1)*rows,:],query)
+            tail=scores[band*rows:,:]
             key_pos=lax.broadcasted_iota(jnp.int32,tail.shape,0)
-            query_pos=(at%per)*rows+lax.broadcasted_iota(jnp.int32,tail.shape,1)%rows
+            query_pos=lax.broadcasted_iota(jnp.int32,tail.shape,1)%rows
             tail=jnp.where(key_pos<=query_pos,tail,MASK_FILL)
-            pieces=[scores[b*step_rows:(b+1)*step_rows,:] for b in range(band)]+[tail]
+            pieces=[scores[b*rows:(b+1)*rows,:] for b in range(band)]+[tail]
             top=functools.reduce(jnp.maximum,[jnp.max(p,axis=0,keepdims=True) for p in pieces])
             total=0.0; acc=0.0
             for b,p in enumerate(pieces):
                 e=jnp.exp(p-top)
                 total=total+jnp.sum(e,axis=0,keepdims=True)
-                acc=acc+nn(val_t_ref[:,b*step_rows:(b+1)*step_rows],e.astype(BF))
+                acc=acc+nn(val_t_ref[:,b*rows:(b+1)*rows],e.astype(BF))
             acc=acc/total
             out_ref[:,0:LANES]=acc[:,0:rows].T.astype(BF)
             out_ref[:,LANES:]=acc[:,rows:].T.astype(BF)
             lse_ref[0]=top+jnp.log(total)
 
-def head_forward(raw,cosine,sine,rows=512,step_rows=512):
-    length=raw.shape[0]
+def head_forward(tokens,gain,weight,cosine,sine,rows=512):
+    length,model=tokens.shape
     steps=length//rows
+    block=lambda cols:pl.BlockSpec((rows,cols),lambda i:(i,0))
     return pl.pallas_call(
-        functools.partial(forward_kernel,rows,step_rows),
+        forward_kernel,
         grid=(steps,),
-        in_specs=[pl.BlockSpec((rows,4*LANES),lambda i:(i,0)),
-                  pl.BlockSpec((rows,LANES),lambda i:(i,0)),
-                  pl.BlockSpec((rows,LANES),lambda i:(i,0))],
-        out_specs=[pl.BlockSpec((rows,4*LANES),lambda i:(i,0)),
-                   pl.BlockSpec((rows,2*LANES),lambda i:(i,0)),
-                   pl.BlockSpec((1,1,2*rows),lambda i:(i,0,0))],
-        out_shape=[jax.ShapeDtypeStruct((length,4*LANES),BF),
+        in_specs=[block(model),pl.BlockSpec((1,model),lambda i:(0,0)),pl.BlockSpec(weight.shape,lambda i:(0,0)),
+                  block(LANES),block(LANES)],
+        out_specs=[block(model),block(4*LANES),block(2*LANES),pl.BlockSpec((1,1,2*rows),lambda i:(i,0,0))],
+        out_shape=[jax.ShapeDtypeStruct((length,model),BF),
+                   jax.ShapeDtypeStruct((length,4*LANES),BF),
                    jax.ShapeDtypeStruct((length,2*LANES),BF),
                    jax.ShapeDtypeStruct((steps,1,2*rows),jnp.float32)],
         scratch_shapes=[pltpu.VMEM((length,LANES),BF),pltpu.VMEM((LANES,length),BF)],
         compiler_params=pltpu.CompilerParams(vmem_limit_bytes=VMEM_LIMIT),
-    )(raw,cosine,sine)
-
-def backward_kernel(rows,step_rows,qkv_ref,out_ref,grad_ref,lse_ref,cos_ref,sin_ref,pick_ref,res_ref,
-                    key_t_ref,grad_key_ref,grad_val_ref,rows_ref):
+    )(tokens,gain,weight,cosine,sine)
+
+def backward_kernel(rows,step_rows,qkv_ref,out_ref,grad_ref,lse_ref,cos_ref,sin_ref,pick_ref,sent_ref,res_ref,got_ref,
+                    key_t_ref,grad_key_ref,grad_val_ref,rows_ref,line_sems):
     at=pl.program_id(0)
+    rank=lax.axis_index("ctx")
+    other_line=rank+CORES*(1-2*lax.rem(lax.div(rank,CORES),LINES))
+    copies=[ctx_copy(sent_ref.at[number],got_ref.at[slot],line_sems,slot,other_line)
+            for slot,number in enumerate((PLANES-1,0))]
+    @pl.when(at==0)
+    def _():
+        barrier=pltpu.get_barrier_semaphore()
+        pl.semaphore_signal(barrier,inc=1,device_id={"ctx":other_line},device_id_type=pl.DeviceIdType.MESH)
+        pl.semaphore_wait(barrier,1)
+        for copy in copies:
+            copy.start()
     here=pl.ds(pl.multiple_of(at*rows,rows),rows)
     length=qkv_ref.shape[0]
     scale=HD**-0.5
@@ -428,8 +440,10 @@
             rows_ref[span,2*LANES:3*LANES]=turn(grad_key_ref[span,:],cos_ref[span,:],-sin_ref[span,:]).astype(BF)
             rows_ref[span,3*LANES:]=grad_val_ref[span,:].astype(BF)
             res_ref[span,:]=nn(rows_ref[span,:],pick_ref[...]).astype(BF)
-
-def head_backward(qkv,out,grad,lse,cosine,sine,pick,rows=256,step_rows=256):
+        for copy in copies:
+            copy.wait()
+
+def head_backward(qkv,out,grad,lse,cosine,sine,pick,sent,rows=256,step_rows=256):
     length=qkv.shape[0]
     steps=length//rows
     lse=lse.reshape(-1,2,lse.shape[2]//2).transpose(1,0,2).reshape(2,steps,rows).transpose(1,0,2).reshape(steps,1,2*rows)
@@ -441,13 +455,14 @@
                   pl.BlockSpec((rows,2*LANES),lambda i:(i,0)),
                   pl.BlockSpec((rows,2*LANES),lambda i:(i,0)),
                   pl.BlockSpec((1,1,2*rows),lambda i:(i,0,0)),
-                  whole(cosine),whole(sine),whole(pick)],
-        out_specs=pl.BlockSpec((length,4*HD),lambda i:(0,0)),
-        out_shape=jax.ShapeDtypeStruct((length,4*HD),BF),
+                  whole(cosine),whole(sine),whole(pick),pl.BlockSpec(memory_space=pl.ANY)],
+        out_specs=[pl.BlockSpec((length,4*HD),lambda i:(0,0)),pl.BlockSpec(memory_space=pl.ANY)],
+        out_shape=[jax.ShapeDtypeStruct((length,4*HD),BF),jax.ShapeDtypeStruct((2,)+sent.shape[1:],BF)],
         scratch_shapes=[pltpu.VMEM((LANES,length),BF),pltpu.VMEM((length,LANES),jnp.float32),
-                        pltpu.VMEM((length,LANES),jnp.float32),pltpu.VMEM((length,4*LANES),BF)],
-        compiler_params=pltpu.CompilerParams(vmem_limit_bytes=VMEM_LIMIT),
-    )(qkv,out,grad,lse,cosine,sine,pick)
+                        pltpu.VMEM((length,LANES),jnp.float32),pltpu.VMEM((length,4*LANES),BF),
+                        pltpu.SemaphoreType.DMA((2,2))],
+        compiler_params=pltpu.CompilerParams(collective_id=3,has_side_effects=True,vmem_limit_bytes=VMEM_LIMIT),
+    )(qkv,out,grad,lse,cosine,sine,pick,sent)
 
 def pad_columns():
     half=HD//2
@@ -512,50 +527,14 @@
     return jnp.where(used, jnp.cos(angles), 0.0), jnp.where(used, jnp.sin(angles) * sign, 0.0)
 
 
-def take_kernel(info, gate_a, gate_b, up_a, up_b, out_ref):
-    @pl.when(info[1] == 0)
-    def _():
-        out_ref[:, :LANES] = gate_a[...]
-        out_ref[:, LANES:] = gate_b[...]
-
-    @pl.when(info[1] != 0)
-    def _():
-        out_ref[:, :LANES] = up_a[...]
-        out_ref[:, LANES:] = up_b[...]
-
-
-def take_columns(info, w_gate, w_up):
-    depth, hidden = w_gate.shape
-    part = depth // LINES
-    steps = hidden // (4 * LANES)
-
-    def spec(core, odd):
-        return pl.BlockSpec(
-            (part, LANES), lambda j, info: (info[2], jnp.where(info[1] == core, 4 * j + 2 * odd + 1 - info[0], 0))
-        )
-
-    return pl.pallas_call(
-        take_kernel,
-        grid_spec=pltpu.PrefetchScalarGridSpec(
-            num_scalar_prefetch=1,
-            grid=(steps,),
-            in_specs=[spec(0, 0), spec(0, 1), spec(1, 0), spec(1, 1)],
-            out_specs=pl.BlockSpec((part, 2 * LANES), lambda j, info: (0, j)),
-        ),
-        out_shape=jax.ShapeDtypeStruct((part, hidden // 2), BF),
-        compiler_params=pltpu.CompilerParams(vmem_limit_bytes=VMEM_LIMIT),
-        cost_estimate=pl.CostEstimate(flops=0, bytes_accessed=2 * depth * hidden, transcendentals=0),
-    )(info, w_gate, w_gate, w_up, w_up)
-
-
 def mlp_kernel(
-    info, normed, grad_rows, gate_a, gate_b, up_a, up_b, got, other, down_a, down_b, down_got, down_other,
+    info, normed, grad_rows, gate_a, gate_b, up_a, up_b, gate_far, up_far, down_a, down_b, down_far,
     inner_ref, grad_gate_ref, grad_up_ref, mixed_ref, back_ref,
-    gate_far, up_far, down, mixed_acc, back_acc,
+    down, mixed_acc, back_acc,
 ):
     step = pl.program_id(0)
     half_steps = pl.num_programs(0) // 2
-    side, core = info[0], info[1]
+    side = info[0]
     depth = gate_a.shape[0]
     near = pl.ds(pl.multiple_of(side * depth, LANES), depth)
     far = pl.ds(pl.multiple_of((1 - side) * depth, LANES), depth)
@@ -565,30 +544,14 @@
         mixed_acc[...] = jnp.zeros_like(mixed_acc)
         back_acc[...] = jnp.zeros_like(back_acc)
 
-    @pl.when(core == 0)
-    def _():
-        gate_far[...] = got[...]
-        up_far[...] = other[...]
-
-    @pl.when(core != 0)
-    def _():
-        gate_far[...] = other[...]
-        up_far[...] = got[...]
-
     @pl.when(step < half_steps)
     def _():
         down[:LANES, :] = down_a[...]
         down[LANES:, :] = down_b[...]
 
-    far_half = (step - half_steps) * 2 // half_steps
-
-    @pl.when((step >= half_steps) & (far_half == core))
+    @pl.when(step >= half_steps)
     def _():
-        down[...] = down_got[...]
-
-    @pl.when((step >= half_steps) & (far_half != core))
-    def _():
-        down[...] = down_other[...]
+        down[...] = down_far[...]
 
     gate_near = jnp.concatenate([gate_a[...], gate_b[...]], axis=1)
     up_near = jnp.concatenate([up_a[...], up_b[...]], axis=1)
@@ -616,7 +579,7 @@
 
 
 def mlp_part(info, normed, grad_rows, weights, kind):
-    w_gate, w_up, got, other, w_down, down_got, down_other = weights
+    w_gate, w_up, far, w_down, down_far = weights
     rows, model = normed.shape
     depth, hidden = w_gate.shape
     half = hidden // 2
@@ -635,14 +598,10 @@
     def row(odd):
         return pl.BlockSpec((LANES, model), lambda j, info: (4 * jnp.minimum(j, part - 1) + 2 * odd + info[0], 0))
 
-    def far_row(which):
-        def block(j, info):
-            half_at = jnp.where(which == 0, info[1], 1 - info[1])
-            return (jnp.clip(j - part - half_at * (part // 2), 0, part // 2 - 1), 0)
-
-        return pl.BlockSpec((2 * LANES, model), block)
-
-    far = pl.BlockSpec((depth, 2 * LANES), lambda j, info: (0, pair_of(j, info)))
+    def far_column(which):
+        return pl.BlockSpec((None, depth, 2 * LANES), lambda j, info: (which, 0, pair_of(j, info)))
+
+    far_row = pl.BlockSpec((2 * LANES, model), lambda j, info: (jnp.maximum(j - part, 0), 0))
 
     def place(j, info):
         pair = pair_of(j, info)
@@ -657,13 +616,11 @@
             grid=(steps,),
             in_specs=[
                 whole((rows, model)), whole((rows, model)),
-                column(0), column(1), column(0), column(1), far, far,
-                row(0), row(1), far_row(0), far_row(1),
+                column(0), column(1), column(0), column(1), far_column(0), far_column(1),
+                row(0), row(1), far_row,
             ],
             out_specs=[act, act, act, whole((rows, model)), whole((rows, model))],
             scratch_shapes=[
-                pltpu.VMEM((depth, 2 * LANES), BF),
-                pltpu.VMEM((depth, 2 * LANES), BF),
                 pltpu.VMEM((2 * LANES, model), BF),
                 pltpu.VMEM((rows, model), jnp.float32),
                 pltpu.VMEM((rows, model), jnp.float32),
@@ -674,53 +631,87 @@
         cost_estimate=pl.CostEstimate(
             flops=12 * rows * model * half, bytes_accessed=6 * model * half, transcendentals=rows * half
         ),
-    )(info, normed, grad_rows, w_gate, w_gate, w_up, w_up, got, other, w_down, w_down, down_got, down_other)
-
-
-def ctx_copy(source, target, sems, number, rank):
-    return pltpu.make_async_remote_copy(
-        src_ref=source,
-        dst_ref=target,
-        send_sem=sems.at[0, number],
-        recv_sem=sems.at[1, number],
-        device_id={"ctx": rank},
-        device_id_type=pl.DeviceIdType.MESH,
-    )
-
-
-def side_copy(source, target, sems, number, side):
-    return pltpu.make_async_remote_copy(
-        src_ref=source,
-        dst_ref=target,
-        send_sem=sems.at[0, number],
-        recv_sem=sems.at[1, number],
-        device_id={"fsdp": side},
-        device_id_type=pl.DeviceIdType.MESH,
-    )
-
-
-def greet(rank, side):
-    barrier = pltpu.get_barrier_semaphore()
-    for away in range(1, RANKS):
-        pl.semaphore_signal(
-            barrier,
-            inc=1,
-            device_id={"ctx": lax.rem(rank + away, RANKS)},
-            device_id_type=pl.DeviceIdType.MESH,
-        )
-    pl.semaphore_signal(barrier, inc=1, device_id={"fsdp": 1 - side}, device_id_type=pl.DeviceIdType.MESH)
-    pl.semaphore_wait(barrier, RANKS)
-
-
-def wide(value):
-    return value.astype(jnp.float32)
-
-
-def reduce_kernel(
-    rows_in, down_keep, down_got, gate_keep, gate_got, up_keep, up_sent, out_keep, out_sent, head_keep, head_sent, gains_in,
-    rows_out, down_mine, down_theirs, down_side, gate_mine, gate_side, up_mine, up_side, out_mine, head_out, gains_out,
-    up_got, out_got, down_acc, gate_acc, up_acc, out_acc, down_in, gate_in, up_in, out_in,
-    head_got, head_two, head_side, head_last, gain_buf, gain_in, exchange_sems, plane_sems, sems, local_sem,
+    )(info, normed, grad_rows, w_gate, w_gate, w_up, w_up, far, far, w_down, w_down, down_far)
+
+
+def head_rows_of(info, number, out_near, out_far):
+    heads = []
+    for is_far in range(2):
+        for at_plane in range(PLANES // 2):
+            for at_core in range(CORES):
+                plane = 2 * (info[0] if is_far == 0 else 1 - info[0]) + at_plane
+                heads.append((plane, at_core, out_far if is_far else out_near, (2 * at_plane + at_core) * 2 * HD))
+    return heads
+
+
+def post_kernel(info, att, tokens, out_near, out_far, gain, resid_ref, normed_ref):
+    width = att.shape[1]
+    total = tokens[...].astype(jnp.float32)
+    for plane, core, weight, first in head_rows_of(info, 0, out_near, out_far):
+        both = [att[plane * CORES * LINES + seq * CORES + core] for seq in range(LINES)]
+        for head in range(2):
+            rows = jnp.concatenate([block[:, head * LANES : head * LANES + HD] for block in both], axis=0)
+            total = total + nn(rows, weight[first + head * HD : first + (head + 1) * HD, :])
+    resid_ref[...] = total
+    normed_ref[...] = (normalize(total)[0] * gain[...]).astype(BF)
+
+
+def local_call(kernel, info, operands, outs):
+    def spec(shape):
+        return pl.BlockSpec(shape, lambda i, info: (0,) * len(shape))
+
+    return pl.pallas_call(
+        kernel,
+        grid_spec=pltpu.PrefetchScalarGridSpec(
+            num_scalar_prefetch=1,
+            grid=(1,),
+            in_specs=[spec(operand.shape) for operand in operands],
+            out_specs=[spec(out.shape) for out in outs],
+        ),
+        out_shape=outs,
+        compiler_params=pltpu.CompilerParams(vmem_limit_bytes=VMEM_LIMIT),
+    )(info, *operands)
+
+
+def pre_kernel(
+    info, back_own, back_got, grad_rows, resid, gain, out_near, out_far, grad_ref, branch_ref, att_ref, gain_ref
+):
+    width = att_ref.shape[1]
+    grad_normed = back_own[...] + back_got[...].astype(jnp.float32)
+    unit, inv = normalize(resid[...])
+    gain_ref[...] = jnp.sum(grad_normed * unit, axis=0, keepdims=True)
+    grad = grad_rows[...].astype(jnp.float32) + norm_back(grad_normed, gain[...], unit, inv)
+    grad_ref[...] = grad
+    branch = grad.astype(BF)
+    branch_ref[...] = branch
+    blank = jnp.zeros((width, LANES - HD), BF)
+    for plane, core, weight, first in head_rows_of(info, 0, out_near, out_far):
+        for head in range(2):
+            back = nt(branch, weight[first + head * HD : first + (head + 1) * HD, :]).astype(BF)
+            for seq in range(LINES):
+                number = plane * CORES * LINES + seq * CORES + core
+                att_ref[number, :, head * LANES : head * LANES + HD] = back[seq * width : (seq + 1) * width]
+                att_ref[number, :, head * LANES + HD : (head + 1) * LANES] = blank
+
+
+def last_kernel(info, rows_in, tokens, gain, grad, query, key, value, query_far, key_far, value_far, out_ref, total):
+    width = rows_in.shape[1]
+    half = query.shape[0]
+    for is_far, weights in enumerate(((query, key, value), (query_far, key_far, value_far))):
+        here = pl.ds(pl.multiple_of((info[0] if is_far == 0 else 1 - info[0]) * half, LANES), half)
+        acc = 0.0
+        for head in range(HK):
+            first = head // CORES * CORES * LINES + head % CORES
+            rows = jnp.concatenate([rows_in[first + seq * CORES] for seq in range(LINES)], axis=0)
+            for weight, start, size in zip(weights, (0, 2 * HD, 3 * HD), (2 * HD, HD, HD)):
+                acc = acc + nt(rows[:, start : start + size], weight[:, head * size : (head + 1) * size])
+        total[:, here] = acc
+    unit, inv = normalize(tokens[...].astype(jnp.float32))
+    out_ref[...] = (grad[...] + norm_back(total[...], gain[...], unit, inv)).astype(BF)
+
+
+def gather_kernel(
+    tokens, head_in, w_gate, w_up, w_out, seq_out, head_out, far, out_far, sems_in, sems_up, sems_down, sems_core, weight_sems, column_sems, group_sems, local_sem
 ):
     rank = lax.axis_index("ctx")
     side = lax.axis_index("fsdp")
@@ -733,29 +724,375 @@
     other_core = rank + 1 - 2 * core
     greet(rank, side)
 
-    up_line = ctx_copy(up_sent, up_got, sems, 0, other_line)
-    out_line = ctx_copy(out_sent, out_got, sems, 1, other_line)
+    def spot(at_plane, at_line):
+        return at_plane * step_rank + at_line * CORES + core
+
+    def move(index, send_sems, to, source=None):
+        return pltpu.make_async_remote_copy(
+            src_ref=seq_out.at[index] if source is None else source,
+            dst_ref=seq_out.at[index],
+            send_sem=send_sems.at[index],
+            recv_sem=sems_in.at[index],
+            device_id={"ctx": to},
+            device_id_type=pl.DeviceIdType.MESH,
+        )
+
+    near, across = spot(plane, line), spot(plane, 1 - line)
+    mine = tokens.at[line]
+    to_line = pltpu.make_async_remote_copy(
+        src_ref=tokens.at[1 - line],
+        dst_ref=seq_out.at[near],
+        send_sem=local_sem.at[1],
+        recv_sem=sems_in.at[near],
+        device_id={"ctx": other_line},
+        device_id_type=pl.DeviceIdType.MESH,
+    )
+    landed_line = pltpu.make_async_remote_copy(
+        src_ref=tokens.at[1 - line],
+        dst_ref=seq_out.at[across],
+        send_sem=local_sem.at[1],
+        recv_sem=sems_in.at[across],
+        device_id={"ctx": other_line},
+        device_id_type=pl.DeviceIdType.MESH,
+    )
+    own = pltpu.make_async_copy(mine, seq_out.at[near], local_sem.at[0])
+
+    def spread(index, up, down, source=None):
+        if up:
+            @pl.when(plane < last)
+            def _():
+                move(index, sems_up, rank + step_rank, source).start()
+
+        if down:
+            @pl.when(plane > 0)
+            def _():
+                move(index, sems_down, rank - step_rank, source).start()
+
+        move(index, sems_core, other_core, source).start()
+
+    to_line.start()
+    spread(near, True, True, mine)
+    own.start()
+
+    head_cross = side_copy(head_in, head_out, weight_sems, 0, 1 - side)
+    depth = w_gate.shape[0] // LINES
+    rows = pl.ds(pl.multiple_of(line * depth, 16), depth)
+    other_rows = pl.ds(pl.multiple_of((1 - line) * depth, 16), depth)
+    groups = 4
+    group_columns = far.shape[2] // groups
+    per_group = group_columns // LANES
+
+    def column(weight, number):
+        there = pl.ds(number * LANES, LANES)
+        here = pl.ds(pl.multiple_of((2 * number + 1 - side) * LANES, LANES), LANES)
+        return side_copy(weight.at[rows, here], far.at[core, rows, there], column_sems, number, 1 - side)
+
+    def send_group(group):
+        for number in range(group * per_group, (group + 1) * per_group):
+            @pl.when(core == 0)
+            def _():
+                column(w_gate, number).start()
+
+            @pl.when(core != 0)
+            def _():
+                column(w_up, number).start()
+
+    def group_copy(group, which_rows, kind, to):
+        block = far.at[core, which_rows, pl.ds(group * group_columns, group_columns)]
+        return ctx_copy(block, block, group_sems, kind * groups + group, to)
+
+    def pass_group(group):
+        for number in range(group * per_group, (group + 1) * per_group):
+            column(w_gate, number).wait_recv()
+        group_copy(group, rows, 0, other_line).start()
+        group_copy(group, rows, 1, other_core).start()
+
+    def pass_line(group):
+        group_copy(group, rows, 0, other_line).wait_recv()
+        group_copy(group, other_rows, 2, other_core).start()
+
+    quarter = 2 * core + line
+    out_rows = w_out.shape[0] // 4
+
+    def out_slice(ref, which):
+        return ref.at[pl.ds(pl.multiple_of(which * out_rows, 16), out_rows)]
+
+    out_mine, out_got = out_slice(out_far, quarter), out_slice(out_far, 2 * core + 1 - line)
+    out_cross = side_copy(out_slice(w_out, quarter), out_mine, weight_sems, 1, 1 - side)
+    out_line = ctx_copy(out_mine, out_mine, weight_sems, 2, other_line)
+    out_core = ctx_copy(out_mine, out_mine, weight_sems, 3, other_core)
+    out_more = ctx_copy(out_got, out_got, weight_sems, 4, other_core)
+    send_group(0)
+    send_group(1)
+
+    def forward(index, up, down):
+        move(index, sems_core, other_core).wait_recv()
+        spread(index, up, down)
+
+    landed_line.wait_recv()
+    spread(across, True, True)
+
+    def pass_on(away, at_line):
+        @pl.when(plane >= away)
+        def _():
+            forward(spot(plane - away, at_line), True, False)
+
+        @pl.when(plane + away <= last)
+        def _():
+            forward(spot(plane + away, at_line), False, True)
+
+    pass_on(1, line)
+    pass_group(0)
+    send_group(2)
+    pass_group(1)
+    send_group(3)
+    pass_on(1, 1 - line)
+    pass_line(0)
+    pass_on(2, line)
+    pass_group(2)
+    out_cross.start()
+    pass_group(3)
+    head_cross.start()
+    pass_line(1)
+    pass_on(2, 1 - line)
+    pass_line(2)
+    pass_on(3, line)
+    out_cross.wait_recv()
+    out_line.start()
+    out_core.start()
+    pass_line(3)
+    pass_on(3, 1 - line)
+    out_line.wait_recv()
+    out_more.start()
+
+    for at_plane in range(PLANES):
+        for at_line in range(LINES):
+            index = at_plane * step_rank + at_line * CORES + 1 - core
+            move(index, sems_core, other_core).wait_recv()
+    head_cross.wait_recv()
+    out_core.wait_recv()
+    out_more.wait_recv()
+    for group in range(groups):
+        group_copy(group, rows, 1, other_core).wait_recv()
+        group_copy(group, other_rows, 2, other_core).wait_recv()
+
+    own.wait()
+    to_line.wait_send()
+    for at_plane in range(PLANES):
+        for at_line in range(LINES):
+            index = at_plane * step_rank + at_line * CORES + core
+            move(index, sems_core, other_core).wait_send()
+
+            @pl.when((plane < last) & (at_plane <= plane))
+            def _():
+                move(index, sems_up, rank + step_rank).wait_send()
+
+            @pl.when((plane > 0) & (at_plane >= plane))
+            def _():
+                move(index, sems_down, rank - step_rank).wait_send()
+
+    for copy in (head_cross, out_cross, out_line, out_core, out_more):
+        copy.wait_send()
+    for number in range(groups * per_group):
+        column(w_gate, number).wait_send()
+    for group in range(groups):
+        group_copy(group, rows, 0, other_line).wait_send()
+        group_copy(group, rows, 1, other_core).wait_send()
+        group_copy(group, other_rows, 2, other_core).wait_send()
+
+
+def gather_all(tokens, head_rows, w_gate, w_up, w_out):
+    width, model = tokens.shape[1:]
+    depth, hidden = w_gate.shape
+    hbm = pl.BlockSpec(memory_space=pl.ANY)
+    dma = pltpu.SemaphoreType.DMA
+    return pl.pallas_call(
+        gather_kernel,
+        in_specs=[hbm] * 5,
+        out_specs=[hbm] * 4,
+        out_shape=[
+            jax.ShapeDtypeStruct((RANKS, width, model), BF),
+            jax.ShapeDtypeStruct(head_rows.shape, BF),
+            jax.ShapeDtypeStruct((2, depth, hidden // 2), BF),
+            jax.ShapeDtypeStruct(w_out.shape, BF),
+        ],
+        scratch_shapes=[dma((RANKS,)), dma((RANKS,)), dma((RANKS,)), dma((RANKS,)), dma((2, 5)), dma((2, RANKS)), dma((2, 12)), dma((2,))],
+        compiler_params=pltpu.CompilerParams(collective_id=1, has_side_effects=True, vmem_limit_bytes=VMEM_LIMIT),
+    )(tokens, head_rows, w_gate, w_up, w_out)
+
+
+def scatter_kernel(rows_in, w_down, rows_out, down_far, exchange_sems, weight_sems, local_sem):
+    rank = lax.axis_index("ctx")
+    side = lax.axis_index("fsdp")
+    core = lax.rem(rank, CORES)
+    line = lax.rem(lax.div(rank, CORES), LINES)
+    other_line = rank + CORES * (1 - 2 * line)
+    other_core = rank + 1 - 2 * core
+    greet(rank, side)
+    chunk = w_down.shape[0] // RANKS
+    quarter = 2 * core + line
+    crosses = []
+    for part in range(2):
+        number = 2 * quarter + part
+        source = w_down.at[pl.ds(pl.multiple_of((2 * number + 1 - side) * chunk, chunk), chunk)]
+        target = down_far.at[pl.ds(pl.multiple_of(number * chunk, chunk), chunk)]
+        crosses.append(side_copy(source, target, weight_sems, part, 1 - side))
+    copies = []
+    for away in range(1, RANKS):
+        to = lax.rem(rank + away, RANKS)
+        copy = ctx_copy(rows_in.at[to], rows_out.at[rank], exchange_sems, away, to)
+        copy.start()
+        copies.append(copy)
+    crosses[0].start()
+    own = pltpu.make_async_copy(rows_in.at[rank], rows_out.at[rank], local_sem)
+    own.start()
+
+    def down_slice(which, part):
+        return down_far.at[pl.ds(pl.multiple_of((2 * which + part) * chunk, chunk), chunk)]
+
+    here = [down_slice(quarter, part) for part in range(2)]
+    there = [down_slice(2 * core + 1 - line, part) for part in range(2)]
+    lines = [ctx_copy(here[i], here[i], weight_sems, 2 + i, other_line) for i in range(2)]
+    cores = [ctx_copy(here[i], here[i], weight_sems, 4 + i, other_core) for i in range(2)]
+    mores = [ctx_copy(there[i], there[i], weight_sems, 6 + i, other_core) for i in range(2)]
+    for number in range(2):
+        crosses[number].wait_recv()
+        if number == 0:
+            crosses[1].start()
+        lines[number].start()
+        cores[number].start()
+    for number in range(2):
+        lines[number].wait_recv()
+        mores[number].start()
+    for copy in cores + mores:
+        copy.wait_recv()
+    for copy in copies:
+        copy.wait()
+    own.wait()
+    for copy in crosses + lines + cores + mores:
+        copy.wait_send()
+
+
+def scatter_rows(rows_in, w_down):
+    hbm = pl.BlockSpec(memory_space=pl.ANY)
+    dma = pltpu.SemaphoreType.DMA
+    return pl.pallas_call(
+        scatter_kernel,
+        in_specs=[hbm] * 2,
+        out_specs=[hbm] * 2,
+        out_shape=[
+            jax.ShapeDtypeStruct(rows_in.shape, BF),
+            jax.ShapeDtypeStruct((w_down.shape[0] // 2, w_down.shape[1]), BF),
+        ],
+        scratch_shapes=[dma((2, RANKS)), dma((2, 8)), dma],
+        compiler_params=pltpu.CompilerParams(collective_id=2, has_side_effects=True, vmem_limit_bytes=VMEM_LIMIT),
+    )(rows_in, w_down)
+
+
+def ctx_copy(source, target, sems, number, rank):
+    return pltpu.make_async_remote_copy(
+        src_ref=source,
+        dst_ref=target,
+        send_sem=sems.at[0, number],
+        recv_sem=sems.at[1, number],
+        device_id={"ctx": rank},
+        device_id_type=pl.DeviceIdType.MESH,
+    )
+
+
+def side_copy(source, target, sems, number, side):
+    return pltpu.make_async_remote_copy(
+        src_ref=source,
+        dst_ref=target,
+        send_sem=sems.at[0, number],
+        recv_sem=sems.at[1, number],
+        device_id={"fsdp": side},
+        device_id_type=pl.DeviceIdType.MESH,
+    )
+
+
+def greet(rank, side):
+    barrier = pltpu.get_barrier_semaphore()
+    for away in range(1, RANKS):
+        pl.semaphore_signal(
+            barrier,
+            inc=1,
+            device_id={"ctx": lax.rem(rank + away, RANKS)},
+            device_id_type=pl.DeviceIdType.MESH,
+        )
+    pl.semaphore_signal(barrier, inc=1, device_id={"fsdp": 1 - side}, device_id_type=pl.DeviceIdType.MESH)
+    pl.semaphore_wait(barrier, RANKS)
+
+
+def wide(value):
+    return value.astype(jnp.float32)
+
+
+def reduce_kernel(
+    rows_in, down_keep, down_got, gate_keep, gate_first, gate_sent, up_keep, up_sent, out_part, out_sent, head_keep, head_sent, gains_in,
+    w_query, w_key, w_value, rows_out, down_mine, down_theirs, down_side, gate_mine, gate_side, up_mine, up_side, out_mine, head_out, gains_out,
+    query_far, key_far, value_far, gate_got, up_got, out_core, out_side, out_sum, out_got, down_acc, gate_acc, up_acc, out_acc, down_in, gate_in, up_in, out_in,
+    head_got, head_two, head_side, head_last, gain_buf, gain_in, exchange_sems, plane_sems, sems, line_sems, fetch_sems, local_sem,
+):
+    rank = lax.axis_index("ctx")
+    side = lax.axis_index("fsdp")
+    core = lax.rem(rank, CORES)
+    line = lax.rem(lax.div(rank, CORES), LINES)
+    plane = lax.div(rank, CORES * LINES)
+    step_rank = CORES * LINES
+    last = PLANES - 1
+    other_line = rank + CORES * (1 - 2 * line)
+    other_core = rank + 1 - 2 * core
+    greet(rank, side)
+
+
+    def gate_line(number):
+        return ctx_copy(gate_sent.at[number], gate_got.at[number], line_sems, number, other_line)
+
+    def up_line(number):
+        return ctx_copy(up_sent.at[number], up_got.at[number], line_sems, PLANES + number, other_line)
+
+    out_cross_core = ctx_copy(out_sent, out_core, sems, 1, other_core)
+    model = head_keep.shape[1]
+    half = model // 2
+    near = pl.ds(pl.multiple_of(side * half, LANES), half)
+    far = pl.ds(pl.multiple_of((1 - side) * half, LANES), half)
+    half_out = out_sum.shape[3]
+    out_near = pl.ds(pl.multiple_of(side * half_out, LANES), half_out)
+    out_away = pl.ds(pl.multiple_of((1 - side) * half_out, LANES), half_out)
+    out_cross = side_copy(out_core.at[:, :, :, out_away], out_side, sems, 17, 1 - side)
+    out_line = ctx_copy(out_sum.at[1 - line], out_got, sems, 18, other_line)
     head_line = ctx_copy(head_sent, head_got, sems, 2, other_line)
 
     weights = (
-        (down_keep, down_got, down_acc, down_in, 0),
-        (gate_keep, gate_got, gate_acc, gate_in, 1),
-        (up_keep, up_got, up_acc, up_in, 2),
-        (out_keep, out_got, out_acc, out_in, 3),
-    )
+        (down_keep, down_got, down_acc, down_in, 0, None),
+        (gate_keep, gate_got, gate_acc, gate_in, 1, gate_line),
+        (up_keep, up_got, up_acc, up_in, 2, up_line),
+        (out_sum.at[line], out_got, out_acc, out_in, 3, None),
+    )
+
+    def arrives(arrival, piece):
+        return (piece >= 0) if arrival is up_line else (piece > 0) & (piece < last)
 
     def message(weight, direction, step):
-        _, _, acc, landed, number = weight
+        _, _, acc, landed, number, _ = weight
         slot = direction * last + step
         target = rank + step_rank * (1 - 2 * direction)
-        return ctx_copy(acc.at[slot], landed.at[slot], plane_sems, number * 2 * last + slot, target)
+        place = jnp.clip(step - direction * (last - plane), 0, last - 1)
+        return ctx_copy(acc.at[place], landed.at[slot], plane_sems, number * 2 * last + slot, target)
 
     def hop(weight, step):
-        keep, got, acc, landed, _ = weight
+        keep, got, acc, landed, _, arrival = weight
         for direction in range(2):
             depth = plane if direction == 0 else last - plane
             piece = plane + (last - step) * (1 - 2 * direction)
             slot = direction * last + step
+            place = step - direction * (last - plane)
+
+            if arrival is not None:
+                @pl.when((depth <= step) & (depth < last) & arrives(arrival, piece))
+                def _():
+                    arrival(piece).wait_recv()
 
             if step:
                 @pl.when((depth >= 1) & (depth <= step))
@@ -764,24 +1101,29 @@
 
                 @pl.when((depth >= 1) & (depth <= step) & (depth < last))
                 def _():
-                    acc[slot] = (wide(keep[piece]) + wide(got[piece]) + wide(landed[slot - 1])).astype(BF)
+                    acc[place] = (wide(keep[piece]) + wide(got[piece]) + wide(landed[slot - 1])).astype(BF)
 
             @pl.when(depth == 0)
             def _():
-                acc[slot] = (wide(keep[piece]) + wide(got[piece])).astype(BF)
+                acc[place] = (wide(keep[piece]) + wide(got[piece])).astype(BF)
 
             @pl.when((depth <= step) & (depth < last))
             def _():
                 message(weight, direction, step).start()
 
     def finish(weight, result):
-        keep, got, _, landed, _ = weight
+        keep, got, _, landed, _, arrival = weight
         for direction in range(2):
             depth = plane if direction == 0 else last - plane
 
             @pl.when(depth >= 1)
             def _():
                 message(weight, direction, last - 1).wait_recv()
+
+        if arrival is not None:
+            @pl.when(arrives(arrival, plane))
+            def _():
+                arrival(plane).wait_recv()
 
         base = wide(keep[plane]) + wide(got[plane])
         above, below = landed.at[last - 1], landed.at[2 * last - 1]
@@ -809,8 +1151,11 @@
 
     down, gate, up, out = weights
     hop(down, 0)
+    for number in (2, 1):
+        gate_line(number).start()
+    gate_got[0] = gate_first[1]
+    gate_got[PLANES - 1] = gate_first[0]
     hop(gate, 0)
-    up_line.start()
     head_line.start()
     copies = []
     for away in range(1, RANKS):
@@ -820,7 +1165,13 @@
         copies.append(copy)
     own = pltpu.make_async_copy(rows_in.at[rank], rows_out.at[rank], local_sem)
     own.start()
-    out_line.start()
+    out_cross_core.start()
+    fetched = []
+    for number, (source, target) in enumerate(((w_query, query_far), (w_key, key_far), (w_value, value_far))):
+        per = source.shape[0] // CORES
+        part = pl.ds(pl.multiple_of(core * per, 16), per)
+        cross = side_copy(source.at[part], target.at[part], fetch_sems, number, 1 - side)
+        fetched.append((cross, ctx_copy(target.at[part], target.at[part], fetch_sems, 3 + number, other_core)))
 
     gain_partners = (None, other_core, other_line, rank + step_rank * (1 - 2 * lax.rem(plane, 2)),
                      rank + 2 * step_rank * (1 - 2 * lax.div(plane, 2)))
@@ -841,25 +1192,39 @@
 
     gain_hop(0)
     hop(down, 1)
+    gain_hop(1)
+    for number in (3, 0, 2, 1):
+        up_line(number).start()
+
+    out_cross_core.wait_recv()
+
+    @pl.loop(0, PLANES)
+    def _(index):
+        for at_line in range(LINES):
+            out_core[at_line, index] = (wide(out_part[at_line, index]) + wide(out_core[at_line, index])).astype(BF)
+
+    out_cross.start()
     hop(gate, 1)
-    gain_hop(1)
-
-    model = head_keep.shape[1]
-    half = model // 2
-    near = pl.ds(pl.multiple_of(side * half, LANES), half)
-    far = pl.ds(pl.multiple_of((1 - side) * half, LANES), half)
+    hop(down, 2)
     head_line.wait_recv()
     head_two[...] = (head_keep[...] + wide(head_got[...])).astype(BF)
     head_cross = side_copy(head_two.at[:, far], head_side, sems, 8, 1 - side)
     head_cross.start()
     gain_hop(2)
-
-    up_line.wait_recv()
-    out_line.wait_recv()
+    hop(gate, 2)
     hop(up, 0)
-    hop(out, 0)
-    hop(down, 2)
-    hop(gate, 2)
+    out_cross.wait_recv()
+    for cross, _ in fetched:
+        cross.start()
+
+    @pl.loop(0, PLANES)
+    def _(index):
+        for at_line in range(LINES):
+            out_sum[at_line, index] = (
+                wide(out_core[at_line, index, :, out_near]) + wide(out_side[at_line, index])
+            ).astype(BF)
+
+    out_line.start()
     gain_hop(3)
     head_cross.wait_recv()
     head_last[...] = (wide(head_two[:, near]) + wide(head_side[...])).astype(BF)
@@ -875,22 +1240,25 @@
         head_out[...] = head_last[...]
 
     hop(up, 1)
-    hop(out, 1)
+    out_line.wait_recv()
+    hop(out, 0)
     gain_hop(4)
-
     finish(down, down_mine)
     per_core = down_mine.shape[0] // CORES
     theirs = pl.ds(pl.multiple_of((1 - core) * per_core, 16), per_core)
     mine = pl.ds(pl.multiple_of(core * per_core, 16), per_core)
     down_core = ctx_copy(down_mine.at[theirs], down_theirs, sems, 10, other_core)
     down_core.start()
+    hop(out, 1)
     finish(gate, gate_mine)
     gate_cross = side_copy(gate_mine.at[:, far], gate_side, sems, 11, 1 - side)
     gate_cross.start()
 
     hop(up, 2)
-    hop(out, 2)
     gain_hop(5)
+    for cross, onward in fetched:
+        cross.wait_recv()
+        onward.start()
     gains_out[...] = gain_buf[5]
 
     down_core.wait_recv()
@@ -904,6 +1272,7 @@
             cross.start()
             crosses.append(cross)
 
+    hop(out, 2)
     finish(up, up_mine)
     up_cross = side_copy(up_mine.at[:, far], up_side, sems, 12, 1 - side)
     up_cross.start()
@@ -918,16 +1287,23 @@
     own.wait()
     for cross in crosses + [gate_cross, up_cross]:
         cross.wait()
-    for copy in (up_line, out_line, head_line, head_cross, down_core):
+    for copy in (out_cross_core, out_cross, out_line, head_line, head_cross, down_core):
         copy.wait_send()
+    for cross, onward in fetched:
+        cross.wait_send()
+        onward.wait()
     for number in range(5):
         gain_copy(number).wait_send()
+    for number in range(PLANES):
+        up_line(number).wait_send()
+    for number in (2, 1):
+        gate_line(number).wait_send()
     for weight in weights:
         sent(weight)
 
 
-def reduce_all(rows_in, down, gate, up, out, head, gains):
-    (down_keep, down_got), (gate_keep, gate_got), (up_keep, up_sent), (out_keep, out_sent) = down, gate, up, out
+def reduce_all(rows_in, down, gate, up, out, head, gains, attn_weights):
+    (down_keep, down_got), (gate_keep, gate_first, gate_sent), (up_keep, up_sent), (out_part, out_sent) = down, gate, up, out
     head_keep, head_sent = head
     hops = 2 * (PLANES - 1)
     vmem = pl.BlockSpec(memory_space=pltpu.VMEM)
@@ -943,11 +1319,12 @@
         return jax.ShapeDtypeStruct(dims, kind)
 
     down_rows, down_cols = piece(down_keep)
-    keeps = (down_keep, gate_keep, up_keep, out_keep)
+    out_half = out_part.shape[1:3] + (out_part.shape[3] // 2,)
+    keeps = (down_keep, gate_keep, up_keep, jax.ShapeDtypeStruct(out_half, BF))
     return pl.pallas_call(
         reduce_kernel,
-        in_specs=[hbm] + [vmem] * 5 + [hbm, vmem, hbm, vmem, hbm, vmem],
-        out_specs=[hbm] + [vmem] * 10,
+        in_specs=[hbm] + [vmem] * 4 + [hbm, vmem] * 4 + [hbm] * 3,
+        out_specs=[hbm] + [vmem] * 10 + [hbm] * 3,
         out_shape=[
             shape(rows_in.shape),
             shape((down_rows, down_cols)),
@@ -957,12 +1334,20 @@
             shape(half_lanes(gate_keep)),
             shape(piece(up_keep)),
             shape(half_lanes(up_keep)),
-            shape(piece(out_keep)),
+            shape(out_half[1:]),
             shape((head_keep.shape[0], head_keep.shape[1] // 2)),
             shape(gains.shape, jnp.float32),
-        ],
-        scratch_shapes=[pltpu.VMEM(up_keep.shape, BF), pltpu.VMEM(out_keep.shape, BF)]
-        + [pltpu.VMEM((hops,) + piece(keep), BF) for keep in keeps]
+        ]
+        + [shape(weight.shape) for weight in attn_weights],
+        scratch_shapes=[
+            pltpu.VMEM(gate_keep.shape, BF),
+            pltpu.VMEM(up_keep.shape, BF),
+            pltpu.VMEM(out_part.shape, BF),
+            pltpu.VMEM(out_part.shape[:1] + out_half, BF),
+            pltpu.VMEM(out_part.shape[:1] + out_half, BF),
+            pltpu.VMEM(out_half, BF),
+        ]
+        + [pltpu.VMEM((PLANES - 1,) + piece(keep), BF) for keep in keeps]
         + [pltpu.VMEM((hops,) + piece(keep), BF) for keep in keeps]
         + [
             pltpu.VMEM(head_keep.shape, BF),
@@ -973,15 +1358,38 @@
             pltpu.VMEM((5,) + gains.shape, jnp.float32),
             pltpu.SemaphoreType.DMA((2, RANKS)),
             pltpu.SemaphoreType.DMA((2, 4 * hops)),
-            pltpu.SemaphoreType.DMA((2, 17)),
+            pltpu.SemaphoreType.DMA((2, 19)),
+            pltpu.SemaphoreType.DMA((2, 2 * PLANES)),
+            pltpu.SemaphoreType.DMA((2, 6)),
             pltpu.SemaphoreType.DMA,
         ],
         compiler_params=pltpu.CompilerParams(
             collective_id=0, has_side_effects=True, vmem_limit_bytes=VMEM_LIMIT
         ),
     )(
-        rows_in, down_keep, down_got, gate_keep, gate_got, up_keep, up_sent, out_keep, out_sent, head_keep, head_sent, gains
-    )
+        rows_in, down_keep, down_got, gate_keep, gate_first, gate_sent, up_keep, up_sent, out_part, out_sent, head_keep, head_sent, gains,
+        *attn_weights,
+    )
+
+
+def local_last(info, operands):
+    rows, model = operands[1].shape
+
+    def spec(shape):
+        return pl.BlockSpec(shape, lambda i, info: (0,) * len(shape))
+
+    return pl.pallas_call(
+        last_kernel,
+        grid_spec=pltpu.PrefetchScalarGridSpec(
+            num_scalar_prefetch=1,
+            grid=(1,),
+            in_specs=[spec(operand.shape) for operand in operands],
+            out_specs=spec((rows, model)),
+            scratch_shapes=[pltpu.VMEM((rows, model), jnp.float32)],
+        ),
+        out_shape=jax.ShapeDtypeStruct((rows, model), BF),
+        compiler_params=pltpu.CompilerParams(vmem_limit_bytes=VMEM_LIMIT),
+    )(info, *operands)
 
 
 def head_shards(
@@ -1005,93 +1413,40 @@
     info = jnp.stack([side, core, line]).astype(jnp.int32)
     pick = jnp.asarray((pad_columns()[:, None] == np.arange(HEAD_COLS)[None, :]).astype(np.float32)).astype(BF)
 
-    near = at(tokens, line)
-    across = swap_line(at(tokens, 1 - line))
-    low = plane < PLANES // 2
-    streams = []
-    for start in (near, across):
-        ups, downs = [], []
-        up = down = start
-        for step in range(PLANES - 1):
-            up = plane_up(up, range(step, PLANES - 1))
-            down = plane_down(down, range(1, PLANES - step))
-            ups.append(up)
-            downs.append(down)
-        streams.append([
-            start,
-            jnp.where(low, downs[0], ups[0]),
-            jnp.where(low, downs[1], ups[1]),
-            jnp.where(plane == 0, downs[2], jnp.where(plane == 1, ups[0], jnp.where(plane == 2, downs[0], ups[2]))),
-        ])
-
     def head_slice(weight, size):
         return lax.dynamic_slice_in_dim(weight, head * size, size, 1)
 
     head_rows = jnp.concatenate(
         [head_slice(w_query, 2 * HD), head_slice(w_key, HD), head_slice(w_value, HD)], axis=1
     )
-    head_got = swap_fsdp(head_rows)
-    head_weight = in_order(side, head_rows, head_got)
+    tokens_seq, head_far, far, out_far = gather_all(tokens, head_rows, w_gate, w_up, w_out)
+    grad_down = cotangent.reshape(rows, model)
+    grad_down_other = swap_fsdp(after(grad_down, tokens_seq))
+    head_weight = in_order(side, head_rows, head_far)
     head_padded = times_transposed(head_weight, pick).astype(BF)
     cosine, sine = rope_rows(length)
-
-    def fetch(part, earlier):
-        crossed = swap_fsdp(after(part, earlier))
-        got = in_order(line, crossed, swap_line(crossed))
-        return got, swap_core(got), crossed
-
-    def quarter(block):
-        return at(block.reshape((CORES * LINES, block.shape[0] // 4) + block.shape[1:]), 2 * core + line)
-
-    out_got, out_other, crossed = fetch(quarter(w_out), head_got)
-    gate_got, gate_other, crossed = fetch(take_columns(info, w_gate, w_up), crossed)
-    cut = w_down.reshape(CORES * LINES, -1, 2, chunk, model)
-    down_got, down_other, crossed = fetch(at(at(cut, 2 * core + line), 1 - side, 1).reshape(-1, model), crossed)
-    weights = (w_gate, w_up, gate_got, gate_other, w_down, down_got, down_other)
-    grad_down = cotangent.reshape(rows, model)
-
-    normed_seq = jnp.zeros((PLANES, CHIPS // PLANES * 2 * width, model), BF)
-    raw_seq = jnp.zeros((PLANES, CHIPS // PLANES * 2 * width, 4 * LANES), jnp.float32)
-    for number in range(PLANES):
-        place = jnp.where(low, plane + number, plane - number) % PLANES
-        both = jnp.stack([streams[0][number], streams[1][number]])
-        theirs = swap_core(both)
-        block = jnp.stack(
-            [
-                jnp.where(core == 0, both, theirs),
-                jnp.where(core == 0, theirs, both),
-            ],
-            axis=1,
-        )
-        block = jnp.where(line == 0, block, block[::-1]).reshape(-1, model)
-        normed = (normalize(block.astype(jnp.float32))[0] * attn_gain).astype(BF)
-        normed_seq = lax.dynamic_update_index_in_dim(normed_seq, normed, place, 0)
-        raw_seq = lax.dynamic_update_index_in_dim(raw_seq, matmul(normed, head_padded), place, 0)
-    normed_seq = normed_seq.reshape(length, model)
-    qkv, attended_seq, lse = head_forward(raw_seq.reshape(length, 4 * LANES), cosine, sine)
+    attn_row, mlp_row = attn_gain[None], mlp_gain[None]
+    normed_seq, qkv, attended_seq, lse = head_forward(
+        tokens_seq.reshape(length, model), attn_row, head_padded, cosine, sine
+    )
+    attended_blocks, down_far = scatter_rows(attended_seq.reshape(RANKS, width, -1), w_down)
+    weights = (w_gate, w_up, far, w_down, down_far)
+    token_rows = tokens.reshape(rows, model)
+    resid, normed_two = local_call(
+        post_kernel,
+        info,
+        (attended_blocks, token_rows, w_out, out_far, mlp_row),
+        [jax.ShapeDtypeStruct((rows, model), jnp.float32), jax.ShapeDtypeStruct((rows, model), BF)],
+    )
 
     def exchange(value):
         return lax.all_to_all(value.reshape(RANKS, width, -1), "ctx", 0, 0, tiled=True)
 
-    def by_token(value):
-        cut = value.reshape(PLANES, LINES, CORES, width, value.shape[-1])
-        return cut.transpose(1, 3, 0, 2, 4).reshape(rows, HK * value.shape[-1])
-
-    attended = by_token(exchange(attended_seq))
-    out_far = in_order(core, out_got, out_other)
-    out_full = in_order(side, w_out, out_far)
-    out_padded = jnp.pad(out_full.reshape(HQ, HD, model), ((0, 0), (0, LANES - HD), (0, 0))).reshape(HQ * LANES, model)
-    inputs = tokens.reshape(rows, model).astype(jnp.float32)
-    resid = inputs + matmul(attended, out_padded)
-    unit_two, inv_two = normalize(resid)
-    normed_two = (unit_two * mlp_gain).astype(BF)
-
-    normed_other, grad_down_other = swap_fsdp((normed_two, after(grad_down, crossed)))
+    normed_other = swap_fsdp(normed_two)
     inner_own, gate_own, up_own, mixed_own, back_own = mlp_part(info, normed_two, grad_down, weights, jnp.float32)
     normed_other, grad_down_other = after((normed_other, grad_down_other), mixed_own)
     inner_far, gate_far, up_far, mixed_far, back_far = mlp_part(info, normed_other, grad_down_other, weights, BF)
     back_got = swap_fsdp(back_far)
-    mixed_got = swap_fsdp(after(mixed_far, back_got))
 
     normed_pair = jnp.concatenate([normed_two, normed_other], axis=0)
     normed_sib = swap_core(normed_pair)
@@ -1109,33 +1464,37 @@
     up_pair, up_sib = pair_acts(up_own, up_far)
     grad_up_weight = (transposed_times(up_pair, normed_pair) + transposed_times(up_sib, normed_sib)).astype(BF)
 
-    mixed = (resid + mixed_own + mixed_got.astype(jnp.float32)).astype(BF)
-    back_got = after(back_got, (grad_down_weight, grad_gate_weight, grad_up_weight))
-    grad_normed_two = back_own + back_got.astype(jnp.float32)
-    grad_resid = grad_down.astype(jnp.float32) + norm_back(grad_normed_two, mlp_gain, unit_two, inv_two)
-    mlp_gain_part = jnp.sum(grad_normed_two * unit_two, axis=0)
-    grad_branch = grad_resid.astype(BF)
-    grad_attended = times_transposed(grad_branch, out_padded).astype(BF)
-    cut = grad_attended.reshape(LINES, width, PLANES, CORES, 2 * LANES)
-    grad_att_seq = exchange(cut.transpose(2, 0, 3, 1, 4)).reshape(length, 2 * LANES)
-
-    att_cut = attended.reshape(rows, 2, HK * LANES)
-    att_other, branch_other = swap_fsdp((at(att_cut, 1 - side, 1), grad_branch))
-    att_pair = jnp.concatenate([at(att_cut, side, 1), att_other], axis=0)
-    branch_pair = jnp.concatenate([grad_branch, branch_other], axis=0)
-    cut = transposed_times(branch_pair, att_pair).astype(BF).reshape(CHIPS, CORES, model // RANKS, HK * LANES)
-    got = swap_core(at(cut, 1 - core, 1))
-    out_pair = (at(cut, core, 1).astype(jnp.float32) + got.astype(jnp.float32)).astype(BF)
-
     per_chip = model // CHIPS
     down_cut = grad_down_weight.reshape(PLANES, LINES, per_chip, part_hidden)
     gate_cut = grad_gate_weight.reshape(LINES, PLANES, chunk, model)
     up_cut = grad_up_weight.reshape(LINES, PLANES, chunk, model)
-    out_cut = out_pair.reshape(PLANES, LINES, model // RANKS, HK * LANES)
-    down_got = swap_line(at(down_cut, 1 - line, 1))
-    gate_got = swap_line(at(gate_cut, 1 - line))
-
-    grad_qkv = head_backward(qkv, attended_seq, grad_att_seq, lse, cosine, sine, pick)
+    down_sent, gate_sent, up_sent = at(down_cut, 1 - line, 1), at(gate_cut, 1 - line), at(up_cut, 1 - line)
+    down_got = swap_line(down_sent)
+    back_got, mixed_far = after((back_got, mixed_far), (down_sent, gate_sent))
+    mixed_got = swap_fsdp(mixed_far)
+    mixed = (resid + mixed_own + mixed_got.astype(jnp.float32)).astype(BF)
+    grad_resid, grad_branch, grad_attended, mlp_gain_part = local_call(
+        pre_kernel,
+        info,
+        (back_own, back_got, grad_down, resid, mlp_row, w_out, out_far),
+        [
+            jax.ShapeDtypeStruct((rows, model), jnp.float32),
+            jax.ShapeDtypeStruct((rows, model), BF),
+            jax.ShapeDtypeStruct(attended_blocks.shape, BF),
+            jax.ShapeDtypeStruct((1, model), jnp.float32),
+        ],
+    )
+    grad_att_seq = exchange(grad_attended).reshape(length, 2 * LANES)
+
+    attended = attended_blocks.reshape(PLANES, LINES, CORES, width, 2 * LANES)
+    attended = attended.transpose(1, 3, 0, 2, 4).reshape(rows, HQ * LANES)
+    out_cut = transposed_times(grad_branch, attended).astype(BF)
+    out_cut = out_cut.reshape(PLANES, LINES, CORES, model // RANKS, HQ * LANES)
+
+    def of_lines(which):
+        return at(out_cut, which, 2).transpose(1, 0, 2, 3)
+
+    grad_qkv, gate_first = head_backward(qkv, attended_seq, grad_att_seq, lse, cosine, sine, pick, gate_sent)
     head_grad = transposed_times(grad_qkv, normed_seq)
     gain_part = jnp.sum(head_grad * head_weight.T.astype(jnp.float32), axis=0) / attn_gain
     query_cut = head_grad[: 2 * HD].reshape(2, HD, model)
@@ -1144,19 +1503,20 @@
     def half_columns(which):
         return jnp.concatenate([at(query_cut, which), at(key_cut, which, 1).reshape(HD, model)], axis=0)
 
-    gains = jnp.concatenate([jnp.stack([gain_part, mlp_gain_part]), jnp.zeros((6, model), jnp.float32)], axis=0)
+    gains = jnp.concatenate([jnp.stack([gain_part, mlp_gain_part[0]]), jnp.zeros((6, model), jnp.float32)], axis=0)
     (
-        grad_rows, down_mine, down_theirs, down_side, gate_mine, gate_side, up_mine, up_side, out_mine, head_mine, gains
+        grad_rows, down_mine, down_theirs, down_side, gate_mine, gate_side, up_mine, up_side, out_mine, head_mine, gains,
+        *attn_far,
     ) = reduce_all(
         grad_qkv.reshape(RANKS, width, HEAD_COLS),
         (at(down_cut, line, 1), after(down_got, grad_qkv)),
-        (at(gate_cut, line), after(gate_got, grad_qkv)),
-        (at(up_cut, line), at(up_cut, 1 - line)),
-        (at(out_cut, line, 1), at(out_cut, 1 - line, 1)),
+        (at(gate_cut, line), gate_first, gate_sent),
+        (at(up_cut, line), up_sent),
+        (of_lines(core), of_lines(1 - core)),
         (half_columns(line), half_columns(1 - line).astype(BF)),
         gains,
-    )
-    grad_own = by_token(grad_rows)
+        (w_query, w_key, w_value),
+    )
 
     def by_columns(mine, theirs):
         cut = mine.reshape(chunk, 2, half_model)
@@ -1184,13 +1544,9 @@
     w_key_grad = head_mine[HD : HD + HD // 2].T
     w_value_grad = head_mine[HD + HD // 2 :].T
 
-    late = after((w_query, w_key, w_value), attended_seq)
-    packed = jnp.concatenate([part.reshape(half_model, HK, -1) for part in late], axis=2).reshape(half_model, -1)
-    packed_got, packed_other, _ = fetch(quarter(packed), mixed_got)
-    packed_full = in_order(side, packed, in_order(core, packed_got, packed_other))
-    grad_normed_one = times_transposed(grad_own, packed_full)
-    unit_one, inv_one = normalize(inputs)
-    tokens_grad = (grad_resid + norm_back(grad_normed_one, attn_gain, unit_one, inv_one)).astype(BF)
+    tokens_grad = local_last(
+        info, (grad_rows, token_rows, attn_row, grad_resid, w_query, w_key, w_value) + tuple(attn_far)
+    )
     return (
         mixed.reshape(seqs, width, model),
         tokens_grad.reshape(seqs, width, model),

time: 667 us -> 488 us (0.73)
  Pallas kernels: 228 us -> 348 us
  waiting for transfers between devices: 121 us -> 6.76 us
  starting transfers between devices: 70.5 us -> 12.4 us
  other arithmetic: 66.3 us -> 14.6 us
  local copies, waits for them, and re-layouts: 119 us -> 70.7 us
  matrix products: 50.3 us -> 24.9 us
    pallas_call x3 -> x7, Pallas kernels: 168 us -> 285 us  [the longest x1 135 us: reduce_all(): pl.pallas_call(reduce_kernel, in_specs=[hbm] + [vmem] * 4 + [hbm, vmem] *...]
    ppermute x11 -> x4, waiting for transfers between devices: 61 us -> 1.11 us  [swap_fsdp(): return lax.ppermute(value, 'fsdp', [(0, 1), (1, 0)])]
    ppermute x21 -> x6, waiting for transfers between devices: 44.6 us -> 0.02 us  [swap_ctx(): return lax.ppermute(value, 'ctx', [(i, i ^ bit) for i in range(RANKS)])]
    ppermute x12 -> x0, starting transfers between devices: 33.5 us -> none  [the longest x6 17.6 us: plane_up(): lax.ppermute(value, 'ctx', [(z * step + i, z * step + step + i) for z in...]
    unnamed x107 -> x93, local copies, waits for them, and re-layouts: 12 us -> 33.7 us
    ppermute x12 -> x0, waiting for transfers between devices: 15 us -> none  [the longest x6 14.3 us: plane_down(): lax.ppermute(value, 'ctx', [(z * step + i, z * step - step + i) for z in...]
    select_n x11 -> x3, other arithmetic: 15.2 us -> 0.47 us  [in_order(): jnp.where(first, mine, other)]
    reshape x5 -> x2, local copies, waits for them, and re-layouts: 20.3 us -> 5.91 us  [the longest x1 3.32 us: head_shards(): attended = attended_blocks.reshape(PLANES, LINES, CORES, width, 2 * LANES)]
  transfers between devices with their start and end apart: 46 -> 11, of which waited for: 13 -> 2; matrix products, arithmetic and copies ran while one was open for 31% -> 11% of each run, Pallas kernels for 32% -> 15%
where the time goes in v3:
time: 488 us; the launch traced here: 479 us
  Pallas kernels  348 us (71%)
  local copies, waits for them, and re-layouts  70.7 us (14%)
  matrix products  24.9 us (5%)
  other arithmetic  14.6 us (3%)
  starting transfers between devices  12.4 us (3%)
  waiting for transfers between devices  6.76 us (1%)
    pallas_call x1, Pallas kernels, reduce_all(): pl.pallas_call(reduce_kernel, in_specs=[hbm] + [vmem] * 4 + [hbm, vmem] *...  135 us
    pallas_call x1, Pallas kernels, gather_all(): pl.pallas_call(gather_kernel, in_specs=[hbm] * 5, out_specs=[hbm] * 4, ou...  69.2 us
    pallas_call x2, Pallas kernels, mlp_part(): pl.pallas_call(mlp_kernel, grid_spec=pltpu.PrefetchScalarGridSpec(num_sca...  39.7 us
    pallas_call x1, Pallas kernels, scatter_rows(): pl.pallas_call(scatter_kernel, in_specs=[hbm] * 2, out_specs=[hbm] * 2, o...  37.9 us
    unnamed x93, local copies, waits for them, and re-layouts  33.7 us
    dot_general x8, matrix products, transposed_times(): lax.dot_general(left, right, (((0,), (0,)), ((), ())), preferred_element_...  23.9 us
    pallas_call x1, Pallas kernels, head_backward(): pl.pallas_call(functools.partial(backward_kernel, rows, step_rows), grid=...  23.3 us
    pallas_call x1, Pallas kernels, head_forward(): pl.pallas_call(forward_kernel, grid=(steps,), in_specs=[block(model), pl....  16.9 us
  transfers between devices with their start and end apart: 11, of which 2 were waited for; matrix products, arithmetic and copies ran while one was open for 11% of the time, Pallas kernels for 15%

profile of v3, /device:TPU:12, one launch (start us, length us, event | category | flops | bytes accessed | tf_op | source)
XLA Modules:
  0.0 478.7 jit_solution(12892253160463436417)
XLA Ops:
  2.2 1.2 constant_dynamic-slice_fusion.9
  3.5 1.3 constant_dynamic-slice_fusion.7
  5.1 69.2 %shard_map.203 = (bf16[16,128,1536]{2,1,0:T(8,128)(2,1)}, bf16[768,384]{1,0:T(8,128)(2,1)S(1)}, bf16[2,768,2048]{2,1,0:T(8,128)(2,1)}, bf16[768,1536]{1,0:T(8,128)(2,1)S(1)}) custom-call(bf16[2,128,1536]{2,1,0:T(8,128)(2,1)S(1)} %copy-done.2, bf16[768,384]{1,0:T(8,128)(2,1)S(1)} %pad_maximum_fusion.4.head_in, bf16[768,4096]{1,0:T(8,128)(2,1)} %gate_b.3, ...), custom_call_target="tpu_custom_call" | custom-call | tf_op jit(solution)/shard_map/pallas_call | solution.py:909
  75.5 1.0 convolution_convert_fusion.1.weight_ref
  76.6 3.8 fusion.3
  80.4 16.9 %shard_map.204 = (bf16[2048,1536]{1,0:T(8,128)(2,1)}, bf16[2048,512]{1,0:T(8,128)(2,1)}, bf16[2048,256]{1,0:T(8,128)(2,1)S(1)}, f32[4,1,1024]{2,1,0:T(1,128)S(1)}) custom-call(bf16[2048,1536]{1,0:T(8,128)(2,1)} %bitcast.155, f32[1,1536]{1,0:T(1,128)S(1)} %broadcast_in_dim.34.gain_ref.gain, bf16[1536,512]{1,0:T(8,128)(2,1)S(1)} %convolution_convert_fusion.1.weight_ref, ...), custom_call_target="tpu_custom_call" | custom-call | tf_op jit(solution)/shard_map/pallas_call | solution.py:373
  97.3 37.9 %shard_map.205 = (bf16[16,128,256]{2,1,0:T(8,128)(2,1)S(1)}, bf16[1024,1536]{1,0:T(8,128)(2,1)S(1)}) custom-call(bf16[16,128,256]{2,1,0:T(8,128)(2,1)S(1)} %bitcast.149, bf16[2048,1536]{1,0:T(8,128)(2,1)} %down_b.3), custom_call_target="tpu_custom_call" | custom-call | tf_op jit(solution)/shard_map/pallas_call | solution.py:979
  135.2 1.6 copy-done
  136.9 7.4 %shard_map.206 = (f32[256,1536]{1,0:T(8,128)S(1)}, bf16[256,1536]{1,0:T(8,128)(2,1)}) custom-call(s32[3]{0:T(128)S(1)} %pad_add_fusion.info, bf16[16,128,256]{2,1,0:T(8,128)(2,1)S(1)} %get-tuple-element.62.att, bf16[256,1536]{1,0:T(8,128)(2,1)S(1)} %bitcast.146, bf16[768,1536]{1,0:T(8,128)(2,1)} %out_near.3, bf16[768,1536]{1,0:T(8,128)(2,1)} %copy-done.1, ...), custom_call_target="tpu_custom_call" | custom-call | tf_op jit(solution)/shard_map/pallas_call | solution.py:663
  144.3 1.2 copy-done.3
  145.5 1.2 collective-permute-start
  147.6 20.2 %shard_map.207 = (bf16[2,256,1024]{2,1,0:T(8,128)(2,1)S(1)}, bf16[2,256,1024]{2,1,0:T(8,128)(2,1)S(1)}, bf16[2,256,1024]{2,1,0:T(8,128)(2,1)S(1)}, f32[256,1536]{1,0:T(8,128)}, f32[256,1536]{1,0:T(8,128)}) custom-call(s32[3]{0:T(128)S(1)} %pad_add_fusion.info, bf16[256,1536]{1,0:T(8,128)(2,1)} %get-tuple-element.65.normed, ...), custom_call_target="tpu_custom_call" | custom-call | flops 9663676416 | bytes 18874368 | tf_op jit(solution)/shard_map/pallas_call | solution.py:612
  167.8 1.0 copy-done.13
  170.8 3.3 copy.80
  174.2 2.6 reshape.262
  176.8 2.4 constant_dynamic-update-slice_fusion.1
  179.4 2.1 constant_dynamic-update-slice_fusion.5
  181.5 1.1 collective-permute-done.1.grad_rows
  182.6 2.7 pad_maximum_fusion
  185.3 19.5 %shard_map.208 = (bf16[2,256,1024]{2,1,0:T(8,128)(2,1)S(1)}, bf16[2,256,1024]{2,1,0:T(8,128)(2,1)S(1)}, bf16[2,256,1024]{2,1,0:T(8,128)(2,1)}, bf16[256,1536]{1,0:T(8,128)(2,1)}, bf16[256,1536]{1,0:T(8,128)(2,1)S(1)}) custom-call(s32[3]{0:T(128)S(1)} %pad_add_fusion.info, bf16[256,1536]{1,0:T(8,128)(2,1)} %collective-permute-done.normed, ...), custom_call_target="tpu_custom_call" | custom-call | flops 9663676416 | bytes 18874368 | tf_op jit(solution)/shard_map/pallas_call | solution.py:612
  204.8 1.4 collective-permute-start.2
  206.2 1.0 constant_dynamic-update-slice_fusion
  207.2 1.3 dynamic-slice_bitcast_fusion.8
  208.8 1.2 constant_dynamic-update-slice_fusion.4
  211.9 1.1 dynamic-slice_bitcast_fusion.6
  213.0 1.5 copy-done.33
  214.5 3.2 fusion.6
  218.1 3.2 add_convert_fusion.2
  221.3 2.0 dynamic-slice_bitcast_fusion.3
  223.3 1.2 copy-done.40
  224.5 1.8 fusion.22
  226.4 1.9 add_convert_fusion.1
  228.3 1.8 dynamic-slice_bitcast_fusion.2
  230.8 8.3 %shard_map.209 = (f32[256,1536]{1,0:T(8,128)S(1)}, bf16[256,1536]{1,0:T(8,128)(2,1)S(1)}, bf16[16,128,256]{2,1,0:T(8,128)(2,1)S(1)}, f32[1,1536]{1,0:T(1,128)S(1)}) custom-call(s32[3]{0:T(128)S(1)} %pad_add_fusion.info, f32[256,1536]{1,0:T(8,128)} %get-tuple-element.80.back_own, bf16[256,1536]{1,0:T(8,128)(2,1)S(1)} %collective-permute-done.2.back_got, ...), custom_call_target="tpu_custom_call" | custom-call | tf_op jit(solution)/shard_map/pallas_call | solution.py:663
  239.2 1.1 copy-done.10
  241.2 1.0 copy-done.18
  242.2 7.0 %all-to-all-start = ((bf16[16,128,256]{2,1,0:T(8,128)(2,1)}), bf16[16,128,256]{2,1,0:T(8,128)(2,1)}, u32[]{:S(2)}, u32[]{:S(2)}) async-start(bf16[16,128,256]{2,1,0:T(8,128)(2,1)} %copy-done.18), calls=%async_computation | async-start | bytes 2097152 | tf_op jit(solution)/shard_map/all_to_all | solution.py:1443
  249.1 3.3 convolution_convert_fusion
  252.4 1.1 constant_dynamic-slice_fusion.5
  253.6 1.9 copy.79
  255.5 2.0 copy.78
  257.5 3.2 fusion.23
  260.7 2.0 add_convert_fusion
  262.8 1.9 dynamic-slice_bitcast_fusion
  264.7 1.1 copy-done.34
  265.8 2.4 add_convert_fusion.3
  268.2 5.6 %all-to-all-done = bf16[16,128,256]{2,1,0:T(8,128)(2,1)} async-done(((bf16[16,128,256]{2,1,0:T(8,128)(2,1)}), bf16[16,128,256]{2,1,0:T(8,128)(2,1)}, u32[]{:S(2)}, u32[]{:S(2)}) %all-to-all-start) | async-done | bytes 1048608 | tf_op jit(solution)/shard_map/all_to_all | solution.py:1443
  273.8 1.2 copy-done.9
  275.0 23.3 %shard_map.210 = (bf16[2048,384]{1,0:T(8,128)(2,1)}, bf16[2,128,1536]{2,1,0:T(8,128)(2,1)S(1)}) custom-call(bf16[2048,512]{1,0:T(8,128)(2,1)} %get-tuple-element.79.qkv_ref, bf16[2048,256]{1,0:T(8,128)(2,1)S(1)} %copy-done.9, bf16[2048,256]{1,0:T(8,128)(2,1)} %bitcast.16.grad_ref, f32[8,1,512]{2,1,0:T(1,128)S(1)} %reshape.258.lse_ref, ...), custom_call_target="tpu_custom_call" | custom-call | tf_op jit(solution)/shard_map/pallas_call | solution.py:451
  299.2 5.2 %fusion.24 = f32[384,1536]{1,0:T(8,128)S(1)} fusion(bf16[2048,384]{1,0:T(8,128)(2,1)} %get-tuple-element.84, bf16[2048,1536]{1,0:T(8,128)(2,1)} %get-tuple-element.90), kind=kOutput, calls=%fused_computation.104 | convolution fusion | flops 2415919104 | bytes 10223616 | tf_op jit(solution)/shard_map/dot_general | solution.py:37
  304.4 2.0 copy.44
  306.8 1.4 copy-done.26
  308.9 1.1 pad_maximum_fusion.2.head_keep
  310.2 134.8 %shard_map.211 = (bf16[16,128,384]{2,1,0:T(8,128)(2,1)}, bf16[192,1024]{1,0:T(8,128)(2,1)S(1)}, bf16[96,1024]{1,0:T(8,128)(2,1)S(1)}, bf16[2,2,96,256]{3,2,1,0:T...) custom-call(bf16[16,128,384]{2,1,0:T(8,128)(2,1)} %bitcast.154, ...), custom_call_target="tpu_custom_call" | custom-call | tf_op jit(solution)/shard_map/pallas_call | solution.py:1324
  448.6 1.9 reshape.274
  451.3 1.4 constant_dynamic-slice_fusion.3
  453.7 2.3 copy.50
  456.8 1.4 constant_dynamic-slice_fusion.2
  458.4 1.1 copy.51
  461.5 1.5 copy.49
  463.0 2.6 reshape.275
  465.6 1.3 copy-done.6
  466.9 1.3 copy-done.12
  468.2 10.4 %shard_map.212 = bf16[256,1536]{1,0:T(8,128)(2,1)} custom-call(s32[3]{0:T(128)S(1)} %pad_add_fusion.info, bf16[16,128,384]{2,1,0:T(8,128)(2,1)} %get-tuple-element.92.rows_in, bf16[256,1536]{1,0:T(8,128)(2,1)S(1)} %bitcast.147, f32[1,1536]{1,0:T(1,128)S(1)} %broadcast_in_dim.34.gain_ref.gain, f32[256,1536]{1,0:T(8,128)} %copy-done.10, ...), custom_call_target="tpu_custom_call" | custom-call | tf_op jit(solution)/shard_map/pallas_call | solution.py:1381
  (138 shorter events, 20.7 us)
Async XLA Ops:
  0.6 4.4 copy-start.2
  74.3 2.3 copy-start.1
  74.3 1.3 copy-start.21
  74.7 5.7 %copy-start.27 = (bf16[768,384]{1,0:T(8,128)(2,1)}, bf16[768,384]{1,0:T(8,128)(2,1)S(1)}, u32[]{:S(2)}) copy-start(bf16[768,384]{1,0:T(8,128)(2,1)S(1)} %get-tuple-element.141) | copy-start | bytes 1769476
  74.7 5.7 %copy-start.29 = (bf16[768,384]{1,0:T(8,128)(2,1)}, bf16[768,384]{1,0:T(8,128)(2,1)S(1)}, u32[]{:S(2)}) copy-start(bf16[768,384]{1,0:T(8,128)(2,1)S(1)} %get-tuple-element.142) | copy-start | bytes 1769476
  97.3 38.0 %copy-start.8 = (bf16[2048,256]{1,0:T(8,128)(2,1)}, bf16[2048,256]{1,0:T(8,128)(2,1)S(1)}, u32[]{:S(2)}) copy-start(bf16[2048,256]{1,0:T(8,128)(2,1)S(1)} %get-tuple-element.61.out_ref) | copy-start | bytes 3145732
  135.2 1.6 copy-start
  136.9 7.4 %copy-start.7 = (bf16[16,128,256]{2,1,0:T(8,128)(2,1)}, bf16[16,128,256]{2,1,0:T(8,128)(2,1)S(1)}, u32[]{:S(2)}) copy-start(bf16[16,128,256]{2,1,0:T(8,128)(2,1)S(1)} %get-tuple-element.62.att) | copy-start | bytes 3145732
  144.3 1.2 copy-start.3
  145.5 36.0 %collective-permute-start = (bf16[256,1536]{1,0:T(8,128)(2,1)}, bf16[256,1536]{1,0:T(8,128)(2,1)}, u32[]{:S(2)}, u32[]{:S(2)}) collective-permute-start(bf16[256,1536]{1,0:T(8,128)(2,1)} %get-tuple-element.65.normed), channel_id=1, source_target_pairs={{0,1},{1,0},{2,3},{3,2},{4,5},{5,4},{6,7},{7,6},{8,9},{9,8},{10,11... | collective-permute-start | bytes 2359304 | tf_op jit(solution)/shard_map/ppermute | solution.py:481
  146.7 35.9 %collective-permute-start.1 = (bf16[256,1536]{1,0:T(8,128)(2,1)}, bf16[256,1536]{1,0:T(8,128)(2,1)}, u32[]{:S(2)}, u32[]{:S(2)}) collective-permute-start(bf16[256,1536]{1,0:T(8,128)(2,1)} %bitcast.6.grad_rows), channel_id=1, source_target_pairs={{0,1},{1,0},{2,3},{3,2},{4,5},{5,4},{6,7},{7,6},{8,9},{9,8},{10,11... | collective-permute-start | bytes 2359304 | tf_op jit(solution)/shard_map/ppermute | solution.py:481
  167.8 1.0 copy-start.13
  168.8 1.0 copy-start.15
  169.8 1.0 copy-start.17
  176.8 2.5 copy-start.16
  176.8 2.5 copy-start.14
  185.3 32.8 %collective-permute-start.3 = (bf16[512,1536]{1,0:T(8,128)(2,1)}, bf16[512,1536]{1,0:T(8,128)(2,1)}, u32[]{:S(2)}, u32[]{:S(2)}) collective-permute-start(bf16[512,1536]{1,0:T(8,128)(2,1)} %pad_maximum_fusion), channel_id=1, source_target_pairs={{0,2},{2,0},{4,6},{6,4},{8,10},{10,8},{12,14},{14,12},{16,18},{18,... | collective-permute-start | bytes 4718600 | tf_op jit(solution)/shard_map/ppermute | solution.py:485
  204.8 25.3 %collective-permute-start.2 = (bf16[256,1536]{1,0:T(8,128)(2,1)S(1)}, bf16[256,1536]{1,0:T(8,128)(2,1)S(1)}, u32[]{:S(2)}, u32[]{:S(2)}) collective-permute-start(bf16[256,1536]{1,0:T(8,128)(2,1)S(1)} %get-tuple-element.72), channel_id=1, source_target_pairs={{0,1},{1,0},{2,3},{3,2},{4,5},{5,4},{6,7},{7,6},{8,9},{9,8},{10,11... | collective-permute-start | bytes 2359304 | tf_op jit(solution)/shard_map/ppermute | solution.py:481
  206.2 2.6 copy-start.36
  208.5 9.2 %collective-permute-start.4 = (bf16[512,1024]{1,0:T(8,128)(2,1)S(1)}, bf16[512,1024]{1,0:T(8,128)(2,1)S(1)}, u32[]{:S(2)}, u32[]{:S(2)}) collective-permute-start(bf16[512,1024]{1,0:T(8,128)(2,1)S(1)} %dynamic-slice_bitcast_fusion.8), channel_id=1, source_target_pairs={{0,2},{2,0},{4,6},{6,4},{8,10},{10,8},{12,14},{14,12},{16,18},{18,... | collective-permute-start | bytes 3145736 | tf_op jit(solution)/shard_map/ppermute | solution.py:485
  210.0 16.4 %copy-start.37 = (bf16[512,1536]{1,0:T(8,128)(2,1)}, bf16[512,1536]{1,0:T(8,128)(2,1)S(1)}, u32[]{:S(2)}) copy-start(bf16[512,1536]{1,0:T(8,128)(2,1)S(1)} %constant_dynamic-update-slice_fusion.4) | copy-start | bytes 4718596
  210.0 13.3 %collective-permute-start.6 = (bf16[512,1536]{1,0:T(8,128)(2,1)S(1)}, bf16[512,1536]{1,0:T(8,128)(2,1)S(1)}, u32[]{:S(2)}, u32[]{:S(2)}) collective-permute-start(bf16[512,1536]{1,0:T(8,128)(2,1)S(1)} %constant_dynamic-update-slice_fusion.4), channel_id=1, source_target_pairs={{0,2},{2,0},{4,6},{6,4},{8,10},{10,8},{12,14},{14,12},{16,18},{18,... | collective-permute-start | bytes 4718600 | tf_op jit(solution)/shard_map/ppermute | solution.py:485
  210.4 1.4 copy-start.35
  210.5 12.8 %collective-permute-start.5 = (bf16[512,1024]{1,0:T(8,128)(2,1)S(1)}, bf16[512,1024]{1,0:T(8,128)(2,1)S(1)}, u32[]{:S(2)}, u32[]{:S(2)}) collective-permute-start(bf16[512,1024]{1,0:T(8,128)(2,1)S(1)} %dynamic-slice_bitcast_fusion.7), channel_id=1, source_target_pairs={{0,2},{2,0},{4,6},{6,4},{8,10},{10,8},{12,14},{14,12},{16,18},{18,... | collective-permute-start | bytes 3145736 | tf_op jit(solution)/shard_map/ppermute | solution.py:485
  211.8 2.7 copy-start.33
  211.9 5.9 %copy-start.31 = (bf16[2,512,1024]{2,1,0:T(8,128)(2,1)}, bf16[2,512,1024]{2,1,0:T(8,128)(2,1)S(1)}, u32[]{:S(2)}) copy-start(bf16[2,512,1024]{2,1,0:T(8,128)(2,1)S(1)} %constant_dynamic-update-slice_fusion.6) | copy-start | bytes 6291460
  217.7 39.7 %collective-permute-start.9 = (bf16[512,1024]{1,0:T(8,128)(2,1)}, bf16[512,1024]{1,0:T(8,128)(2,1)}, u32[]{:S(2)}, u32[]{:S(2)}) collective-permute-start(bf16[512,1024]{1,0:T(8,128)(2,1)} %dynamic-slice_bitcast_fusion.6), channel_id=1, source_target_pairs={{0,2},{2,0},{4,6},{6,4},{8,10},{10,8},{12,14},{14,12},{16,18},{18,... | collective-permute-start | bytes 3145736 | tf_op jit(solution)/shard_map/ppermute | solution.py:485
  223.3 83.5 %collective-permute-start.8 = (bf16[4,192,1024]{2,1,0:T(8,128)(2,1)}, bf16[4,192,1024]{2,1,0:T(8,128)(2,1)}, u32[]{:S(2)}, u32[]{:S(2)}) collective-permute-start(bf16[4,192,1024]{2,1,0:T(8,128)(2,1)} %get-tuple-element.138), channel_id=1, source_target_pairs={{0,4},{2,6},{4,0},{6,2},{8,12},{10,14},{12,8},{14,10},{16,20},{18,... | collective-permute-start | bytes 4718600 | tf_op jit(solution)/shard_map/ppermute | solution.py:485
  223.3 1.2 copy-start.40
  230.1 34.5 %collective-permute-start.7 = (bf16[256,1536]{1,0:T(8,128)(2,1)}, bf16[256,1536]{1,0:T(8,128)(2,1)}, u32[]{:S(2)}, u32[]{:S(2)}) collective-permute-start(bf16[256,1536]{1,0:T(8,128)(2,1)} %get-tuple-element.78), channel_id=1, source_target_pairs={{0,1},{1,0},{2,3},{3,2},{4,5},{5,4},{6,7},{7,6},{8,9},{9,8},{10,11... | collective-permute-start | bytes 2359304 | tf_op jit(solution)/shard_map/ppermute | solution.py:481
  239.2 1.1 copy-start.10
  240.3 0.9 copy-start.11
  241.2 1.0 copy-start.18
  242.2 31.6 %all-to-all-start = ((bf16[16,128,256]{2,1,0:T(8,128)(2,1)}), bf16[16,128,256]{2,1,0:T(8,128)(2,1)}, u32[]{:S(2)}, u32[]{:S(2)}) async-start(bf16[16,128,256]{2,1,0:T(8,128)(2,1)} %copy-done.18), calls=%async_computation | async-start | bytes 2097152 | tf_op jit(solution)/shard_map/all_to_all | solution.py:1443
  255.5 2.0 copy-start.41
  257.5 3.2 copy-start.32
  257.5 3.3 copy-start.38
  262.7 2.0 copy-start.4
  262.7 3.0 copy-start.34
  273.8 1.2 copy-start.9
  298.3 0.9 copy-start.19
  306.6 1.7 copy-start.26
  306.6 1.8 copy-start.28
  306.6 1.9 copy-start.30
  306.8 2.1 copy-start.39
  308.8 1.4 copy-start.20
  445.0 0.7 copy-start.22
  445.0 1.4 copy-start.24
  456.8 2.7 copy-start.25
  458.2 1.3 copy-start.23
  461.0 4.7 copy-start.5
  465.6 1.3 copy-start.6
  466.9 1.3 copy-start.12
